TPU v7x, 32 devices: a whole 2x2x4 slice. The times are simulated.
32 devices in a mesh: groups: 2 (over y), vocab: 8 (over z, x), rows: 2 (over core).
Axes of the slice: x: 2, y: 2, z: 4, core: 2. Of those that a mesh axis runs over, the one named last changes fastest.
Arguments:
- teacher_hidden: bfloat16 [64, 4608], P(('groups', 'vocab', 'rows')), parts along dimension 0, may hold values from -140 to 140
- student_hidden: bfloat16 [64, 3584], P(('groups', 'vocab', 'rows')), parts along dimension 0, may hold values from -140 to 140
- teacher_head: bfloat16 [4608, 1024], P(None, 'vocab'), may hold values from -0.176776695 to 0.176776695
- student_head: bfloat16 [3584, 1024], P(None, 'vocab'), may hold values from -0.20044593 to 0.20044593
- labels: int32 [64], P(('groups', 'vocab', 'rows')), parts along dimension 0, may hold values from 0 to 1023
Outputs:
- token_loss: float32 [64], P(('groups', 'vocab', 'rows')), parts along dimension 0
- hidden_grad: float32 [64, 3584], P(('groups', 'vocab', 'rows')), parts along dimension 0
- head_grad: float32 [7168, 1024], P('groups', 'vocab'), parts along dimension 0
There are 2 independent parts, one for each index of `groups`. A program takes and returns all parts, laid end to end along the dimension named above; an argument that names none is the same for every part. Nothing has to cross between parts.
All inputs are finite; a program needn't handle non-finite values.
Results may differ from a plain program's by a relative error of at most 0.0021.
Values may be sent and summed in bfloat16 or wider, within the bound.
No kernel may reach another device: no remote copies, remote signals or barrier semaphores. Data moves between devices by JAX's collectives and lax.ppermute only.
A program may use at most 64 MiB of HBM per device.

v0:
```python
import jax
import jax.numpy as jnp
from jax import lax
from jax.sharding import PartitionSpec as P


def shard_summary(teacher_logits, student_logits, label_rows, first_column):
    columns = lax.broadcasted_iota(jnp.int32, student_logits.shape, 1)
    target = (label_rows - first_column)[:, None] == columns
    top_teacher = jnp.max(teacher_logits, axis=1)
    scaled = jnp.exp(teacher_logits - top_teacher[:, None])
    mass_teacher = jnp.sum(scaled, axis=1)
    cross_term = jnp.sum(scaled * (teacher_logits - student_logits), axis=1)
    top_student = jnp.max(student_logits, axis=1)
    mass_student = jnp.sum(jnp.exp(student_logits - top_student[:, None]), axis=1)
    picked = jnp.sum(jnp.where(target, student_logits, jnp.zeros_like(student_logits)), axis=1)
    return (top_teacher, mass_teacher, cross_term, top_student, mass_student, picked)


def fold_stacked(stacked):
    top_teacher = jnp.max(stacked[0], axis=0)
    teacher_factor = jnp.exp(stacked[0] - top_teacher[None])
    top_student = jnp.max(stacked[3], axis=0)
    student_factor = jnp.exp(stacked[3] - top_student[None])
    return (
        top_teacher,
        jnp.sum(stacked[1] * teacher_factor, axis=0),
        jnp.sum(stacked[2] * teacher_factor, axis=0),
        top_student,
        jnp.sum(stacked[4] * student_factor, axis=0),
        jnp.sum(stacked[5], axis=0),
    )


def row_loss(summary):
    return (
        summary[2] / summary[1]
        - summary[0]
        - jnp.log(summary[1])
        + 2.0 * (summary[3] + jnp.log(summary[4]))
        - summary[5]
    )


def logit_gradient(teacher_logits, student_logits, label_rows, first_column, summary):
    columns = lax.broadcasted_iota(jnp.int32, student_logits.shape, 1)
    target = (label_rows - first_column)[:, None] == columns
    teacher_prob = jnp.exp(teacher_logits - summary[0][:, None]) / summary[1][:, None]
    student_prob = jnp.exp(student_logits - summary[3][:, None]) / summary[4][:, None]
    return (2.0 * student_prob - teacher_prob - target.astype(jnp.float32)).astype(jnp.bfloat16)


def on_device(teacher_hidden, student_hidden, teacher_head, student_head, labels):
    vocab_width = student_head.shape[1]
    own_rows = labels.shape[0]
    first_column = lax.axis_index("vocab") * vocab_width
    label_rows = lax.all_gather(labels, "vocab", axis=0, tiled=True)

    def both_logits(teacher_rows, student_rows):
        teacher_logits = jnp.dot(teacher_rows, teacher_head, preferred_element_type=jnp.float32)
        student_logits = jnp.dot(student_rows, student_head, preferred_element_type=jnp.float32)
        return (teacher_logits, student_logits)

    pieces = lax.all_gather((teacher_hidden, student_hidden), "vocab", axis=0, tiled=True)
    teacher_logits, student_logits = both_logits(pieces[0], pieces[1])
    labels_here = label_rows
    forward_summary = shard_summary(teacher_logits, student_logits, labels_here, first_column)
    partial_value = forward_summary[:6]
    stacked = (
        lax.all_gather(partial_value[0][None], "vocab", axis=0, tiled=True),
        lax.all_gather(partial_value[1][None], "vocab", axis=0, tiled=True),
        lax.all_gather(partial_value[2][None], "vocab", axis=0, tiled=True),
        lax.all_gather(partial_value[3][None], "vocab", axis=0, tiled=True),
        lax.all_gather(partial_value[4][None], "vocab", axis=0, tiled=True),
        lax.all_gather(partial_value[5][None], "vocab", axis=0, tiled=True),
    )
    summary = fold_stacked(stacked)
    offset = lax.axis_index("vocab") * own_rows
    own_summary = tuple(
        (lax.dynamic_slice_in_dim(member, offset, own_rows, 0) for member in summary)
    )
    token_loss = row_loss(own_summary)
    pieces = lax.all_gather((teacher_hidden, student_hidden), "vocab", axis=0, tiled=True)
    teacher_logits, student_logits = both_logits(pieces[0], pieces[1])
    labels_here = label_rows
    summary_here = tuple((member for member in summary))
    grad_rows = logit_gradient(
        teacher_logits, student_logits, labels_here, first_column, summary_here
    )
    rows_student = pieces[1]
    partial_head = lax.dot_general(
        rows_student, grad_rows, (((0,), (0,)), ((), ())), preferred_element_type=jnp.float32
    )
    head_grad = lax.psum(partial_head, "rows")
    hidden_grad = lax.psum_scatter(
        lax.dot_general(
            grad_rows, student_head, (((1,), (1,)), ((), ())), preferred_element_type=jnp.float32
        ),
        "vocab",
        scatter_dimension=0,
        tiled=True,
    )
    return (token_loss, hidden_grad, head_grad)


def solution(mesh):
    in_specs = (
        P(("groups", "vocab", "rows"), None),
        P(("groups", "vocab", "rows"), None),
        P(None, "vocab"),
        P(None, "vocab"),
        P(("groups", "vocab", "rows")),
    )
    out_specs = (
        P(("groups", "vocab", "rows")),
        P(("groups", "vocab", "rows"), None),
        P("groups", "vocab"),
    )
    return jax.shard_map(
        on_device, mesh=mesh, in_specs=in_specs, out_specs=out_specs, check_vma=False
    )
```

profile of v0, /device:TPU:0, one launch (start us, length us, event | category | flops | bytes accessed | tf_op | source)
XLA Modules:
  0.0 209.7 jit_solution(13679790523009616390)
XLA Ops:
  7.2 0.0 copy-start
  7.2 0.0 copy-start.1
  7.2 0.0 all-reduce.14.cloned.1.call-start
  7.2 1.4 fusion.2
  9.3 0.9 dynamic-update-slice.5
  10.2 13.1 %all-reduce.5 = s32[16]{0:T(128)S(1)} all-reduce(s32[16]{0:T(128)S(1)} %dynamic-update-slice.5), channel_id=1, replica_groups=mesh['groups'=2,'vocab'=8,'rows'=2] {'vocab'}, use_global_device_ids=true, to_apply=%add.5 | all-reduce | flops 16 | bytes 128
  23.2 30.8 %all-gather.7 = bf16[8,2,3584]{2,1,0:T(2,128)(2,1)S(1)} all-gather(bf16[1,2,3584]{2,1,0:T(2,128)(2,1)} %bitcast.14), channel_id=1, replica_groups=mesh['groups'=2,'vocab'=8,'rows'=2] {'vocab'}, dimensions={0}, use_global_device_ids=true | all-gather | bytes 129024 | tf_op jit(solution)/shard_map/all_gather | solution.py:64
  54.1 30.8 %all-gather.6 = bf16[8,2,4608]{2,1,0:T(2,128)(2,1)S(1)} all-gather(bf16[1,2,4608]{2,1,0:T(2,128)(2,1)} %bitcast.13), channel_id=1, replica_groups=mesh['groups'=2,'vocab'=8,'rows'=2] {'vocab'}, dimensions={0}, use_global_device_ids=true | all-gather | bytes 165888 | tf_op jit(solution)/shard_map/all_gather | solution.py:64
  84.8 0.1 reshape.43
  85.6 1.5 fusion.4
  87.1 0.0 copy-done
  87.1 0.4 fusion.3
  87.5 0.2 dynamic-update-slice.3
  87.7 0.2 dynamic-update-slice.1
  87.9 0.2 multiply_reduce_fusion
  88.2 0.2 dynamic-update-slice.2
  88.4 0.2 dynamic-update-slice
  88.6 0.2 dynamic-update-slice.4
  88.8 0.2 dynamic-update-slice.6
  89.0 18.6 %all-reduce.8 = (f32[128]{0:T(128)S(1)}, f32[128]{0:T(128)S(1)}, f32[128]{0:T(128)S(1)}, f32[128]{0:T(128)S(1)}, f32[128]{0:T(128)S(1)}, /*index=5*/f32[128]{0:T(128)S(1)}) all-reduce(f32[128]{0:T(128)S(1)} %dynamic-update-slice.6, f32[128]{0:T(128)S(1)} %dynamic-update-slice.4, ...), channel_id=7, replica_groups=mesh['groups'=2,'vocab'=8,'rows'=2] {'vocab'}, use_global_device_ids=true, to_apply=%add.6 | all-reduce | flops 768 | bytes 6144
  107.6 0.1 reshape.16
  107.7 0.1 reshape.18
  107.8 0.1 reshape.15
  107.9 0.1 reshape.17
  108.0 0.1 reshape.19
  108.1 0.0 copy-done.1
  108.1 1.1 fusion.1
  109.2 0.0 all-reduce.14.cloned.1.call-update
  109.2 0.0 all-reduce.12.cloned.1.call-start
  109.3 1.7 convolution_bitcast_fusion
  111.0 0.0 all-reduce.12.cloned.1.call-update
  111.0 0.1 reshape.20
  111.8 0.6 dynamic-slice_subtract_fusion
  112.4 64.7 %all-reduce.14.cloned.1.call-done = f32[16,3584]{1,0:T(8,128)} async-done(((f32[16,3584]{1,0:T(8,128)}), f32[16,3584]{1,0:T(8,128)}) %all-reduce.14.cloned.1.call-update) | async-done | bytes 229392
  177.1 1.5 constant_dynamic-slice_fusion
  178.6 21.6 %all-reduce.12.cloned.1.call-done = f32[3584,128]{0,1:T(8,128)} async-done(((f32[3584,128]{0,1:T(8,128)}), f32[3584,128]{0,1:T(8,128)}) %all-reduce.12.cloned.1.call-update) | async-done | bytes 1835024 | tf_op jit(solution)/shard_map/psum | solution.py:94
  200.2 2.7 %copy.9 = f32[3584,128]{1,0:T(8,128)} copy(f32[3584,128]{0,1:T(8,128)} %all-reduce.12.cloned.1.call-done) | data formatting | bytes 3670016
  (13 shorter events, 0.1 us)
Async XLA Ops:
  7.2 79.9 %copy-start = (bf16[4608,128]{1,0:T(8,128)(2,1)S(1)}, bf16[4608,128]{1,0:T(8,128)(2,1)}, u32[]{:S(2)}) copy-start(bf16[4608,128]{1,0:T(8,128)(2,1)} %param.7) | copy-start | bytes 3538948
  7.2 100.9 %copy-start.1 = (bf16[3584,128]{1,0:T(8,128)(2,1)S(1)}, bf16[3584,128]{1,0:T(8,128)(2,1)}, u32[]{:S(2)}) copy-start(bf16[3584,128]{1,0:T(8,128)(2,1)} %param.8) | copy-start | bytes 2752516
  7.2 169.9 %all-reduce.14.cloned.1.call-start = ((), (), s32[]{:S(2)}) async-start(), calls=%async_computation.1 | async-start | bytes 458752
  109.2 91.0 %all-reduce.12.cloned.1.call-start = ((), (), s32[]{:S(2)}) async-start(), calls=%async_computation | async-start | bytes 3670016 | tf_op jit(solution)/shard_map/psum | solution.py:94
Sparse Core Ops, SparseCore 0:
  109.3 67.7 all-reduce.13
  180.1 20.0 all-reduce.11
where the time goes:
time: 210 us
  blocking collectives  93.2 us (44%)
  waiting for transfers between devices  86.3 us (41%)
  between operations  16.1 us (8%)
  local copies, waits for them, and re-layouts  8.39 us (4%)
  matrix products  4.75 us (2%)
    unnamed x3, waiting for transfers between devices  64.7 us
    all_gather x2, blocking collectives, on_device(): lax.all_gather((teacher_hidden, student_hidden), 'vocab', axis=0, tiled=T...  61.6 us
    unnamed x2, blocking collectives  31.6 us
    psum x1, waiting for transfers between devices, on_device(): head_grad = lax.psum(partial_head, 'rows')  21.6 us
    unnamed x23, local copies, waits for them, and re-layouts  7.91 us
  transfers between devices with their start and end apart: 2, of which 2 were waited for; matrix products, arithmetic and copies ran while one was open for 2% of the time, Pallas kernels for 0%

commit v1 on v0

v1 whole, which is shorter than its diff:
```python
import jax
import jax.numpy as jnp
from jax import lax
from jax.sharding import PartitionSpec as P

F32 = jnp.float32
BF16 = jnp.bfloat16
CODE = 128


def spread(block, axis, size):
    copies = jnp.broadcast_to(block[None], (size,) + block.shape)
    return lax.all_to_all(copies, axis, split_axis=0, concat_axis=0, tiled=True)


def on_device(teacher_hidden, student_hidden, teacher_head, student_head, labels, *, shards):
    own, teacher_width = teacher_hidden.shape
    student_width = student_hidden.shape[1]
    columns_here = student_head.shape[1]
    first_column = lax.axis_index("vocab") * columns_here
    lanes = lax.broadcasted_iota(jnp.int32, (own, CODE), 1)
    digits = jnp.where(lanes == 0, (labels // 128)[:, None], (labels % 128)[:, None])
    payload = jnp.concatenate([teacher_hidden, student_hidden, digits.astype(BF16)], axis=1)
    rows = spread(payload, "vocab", shards).reshape(shards * own, -1)
    teacher_rows = rows[:, :teacher_width]
    student_rows = rows[:, teacher_width : teacher_width + student_width]
    code = rows[:, teacher_width + student_width :].astype(jnp.int32)
    label_rows = code[:, 0] * 128 + code[:, 1]
    other = [(0, 1), (1, 0)]
    student_other = lax.ppermute(student_rows, "rows", other)

    teacher_logits = jnp.dot(teacher_rows, teacher_head, preferred_element_type=F32)
    student_logits = jnp.dot(student_rows, student_head, preferred_element_type=F32)
    columns = lax.broadcasted_iota(jnp.int32, student_logits.shape, 1)
    target = (label_rows - first_column)[:, None] == columns
    top_t = jnp.max(teacher_logits, axis=1, keepdims=True)
    exp_t = jnp.exp(teacher_logits - top_t)
    top_s = jnp.max(student_logits, axis=1, keepdims=True)
    exp_s = jnp.exp(student_logits - top_s)
    stats = jnp.concatenate(
        [
            top_t,
            jnp.sum(exp_t, axis=1, keepdims=True),
            jnp.sum(exp_t * (teacher_logits - student_logits), axis=1, keepdims=True),
            top_s,
            jnp.sum(exp_s, axis=1, keepdims=True),
            jnp.sum(jnp.where(target, student_logits, 0.0), axis=1, keepdims=True),
        ],
        axis=1,
    )
    every = spread(stats, "vocab", shards)
    all_top_t = jnp.max(every[:, :, 0], axis=0)
    factor_t = jnp.exp(every[:, :, 0] - all_top_t[None])
    all_top_s = jnp.max(every[:, :, 3], axis=0)
    factor_s = jnp.exp(every[:, :, 3] - all_top_s[None])
    mass_t = jnp.sum(every[:, :, 1] * factor_t, axis=0)
    cross = jnp.sum(every[:, :, 2] * factor_t, axis=0)
    mass_s = jnp.sum(every[:, :, 4] * factor_s, axis=0)
    picked = jnp.sum(every[:, :, 5], axis=0)
    loss = cross / mass_t - all_top_t - jnp.log(mass_t) + 2.0 * (all_top_s + jnp.log(mass_s)) - picked
    token_loss = lax.dynamic_slice_in_dim(loss, lax.axis_index("vocab") * own, own, 0)

    teacher_prob = jnp.exp(teacher_logits - all_top_t[:, None]) / mass_t[:, None]
    student_prob = jnp.exp(student_logits - all_top_s[:, None]) / mass_s[:, None]
    grad_rows = (2.0 * student_prob - teacher_prob - target.astype(F32)).astype(BF16)
    grad_other = lax.ppermute(grad_rows, "rows", other)
    partial = lax.dot_general(grad_rows, student_head, (((1,), (1,)), ((), ())), preferred_element_type=F32)
    arrived = lax.all_to_all(partial.reshape(shards, own, student_width), "vocab", split_axis=0, concat_axis=0, tiled=True)
    hidden_grad = jnp.sum(arrived, axis=0)
    head_grad = lax.dot_general(
        jnp.concatenate([student_rows, student_other], axis=0),
        jnp.concatenate([grad_rows, grad_other], axis=0),
        (((0,), (0,)), ((), ())),
        preferred_element_type=F32,
    )
    return (token_loss, hidden_grad, head_grad)


def solution(mesh):
    tokens = ("groups", "vocab", "rows")
    in_specs = (P(tokens, None), P(tokens, None), P(None, "vocab"), P(None, "vocab"), P(tokens))
    out_specs = (P(tokens), P(tokens, None), P("groups", "vocab"))

    def body(*arrays):
        return on_device(*arrays, shards=mesh.shape["vocab"])

    return jax.shard_map(body, mesh=mesh, in_specs=in_specs, out_specs=out_specs, check_vma=False)
```

time: 210 us -> 44.6 us (0.21)
  blocking collectives: 93.2 us -> 10.1 us
  waiting for transfers between devices: 86.3 us -> 14.1 us
  between operations: 16.1 us -> 0.75 us
  starting transfers between devices: 0.08 us -> 11.2 us
  local copies, waits for them, and re-layouts: 8.39 us -> 2.41 us
    unnamed x3 -> x0, waiting for transfers between devices: 64.7 us -> none
    all_gather x2 -> x0, blocking collectives: 61.6 us -> none  [on_device(): lax.all_gather((teacher_hidden, student_hidden), 'vocab', axis=0, tiled=T...]
    unnamed x2 -> x0, blocking collectives: 31.6 us -> none
    psum x1 -> x0, waiting for transfers between devices: 21.6 us -> none  [on_device(): head_grad = lax.psum(partial_head, 'rows')]
    all_to_all x0 -> x2, waiting for transfers between devices: none -> 13.8 us  [the longest x1 9 us: spread(): return lax.all_to_all(copies, axis, split_axis=0, concat_axis=0, tiled=True)]
    all_to_all x0 -> x2, starting transfers between devices: none -> 10.7 us  [the longest x1 7.25 us: spread(): return lax.all_to_all(copies, axis, split_axis=0, concat_axis=0, tiled=True)]
    all_to_all x0 -> x1, blocking collectives: none -> 10.1 us  [spread(): return lax.all_to_all(copies, axis, split_axis=0, concat_axis=0, tiled=True)]
    unnamed x23 -> x4, local copies, waits for them, and re-layouts: 7.91 us -> 0.01 us
  transfers between devices with their start and end apart: 2 -> 4, of which waited for: 2 -> 3; matrix products, arithmetic and copies ran while one was open for 2% -> 5% of each run, Pallas kernels for 0% -> 0%
where the time goes in v1:
time: 44.6 us; the launch traced here: 44.2 us
  waiting for transfers between devices  14.1 us (32%)
  starting transfers between devices  11.2 us (25%)
  blocking collectives  10.1 us (23%)
  other arithmetic  3 us (7%)
  matrix products  2.74 us (6%)
  local copies, waits for them, and re-layouts  2.41 us (5%)
  between operations  0.75 us (2%)
    all_to_all x1, blocking collectives, spread(): return lax.all_to_all(copies, axis, split_axis=0, concat_axis=0, tiled=True)  10.1 us
    all_to_all x1, waiting for transfers between devices, spread(): return lax.all_to_all(copies, axis, split_axis=0, concat_axis=0, tiled=True)  9 us
    all_to_all x1, starting transfers between devices, spread(): return lax.all_to_all(copies, axis, split_axis=0, concat_axis=0, tiled=True)  7.25 us
    all_to_all x1, waiting for transfers between devices, on_device(): lax.all_to_all(partial.reshape(shards, own, student_width), 'vocab', spli...  4.82 us
    all_to_all x1, starting transfers between devices, on_device(): lax.all_to_all(partial.reshape(shards, own, student_width), 'vocab', spli...  3.4 us
    dot_general x1, matrix products, on_device(): lax.dot_general(jnp.concatenate([student_rows, student_other], axis=0), j...  1.69 us
  transfers between devices with their start and end apart: 4, of which 3 were waited for; matrix products, arithmetic and copies ran while one was open for 5% of the time, Pallas kernels for 0%

profile of v1, /device:TPU:0, one launch (start us, length us, event | category | flops | bytes accessed | tf_op | source)
XLA Modules:
  0.0 44.2 jit_solution(9952223145625940663)
XLA Ops:
  0.6 0.0 copy-start
  0.6 0.0 copy-start.1
  0.7 0.8 %and_select_fusion.1 = (s32[2]{0:T(128)S(1)}, s32[2]{0:T(128)S(1)}) fusion(s32[2]{0:T(128)} %param.9), kind=kLoop, calls=%fused_computation.28 | loop fusion | flops 38 | bytes 24 | tf_op jit(solution)/shard_map/jit(floor_divide)/jit(_where)/select_n | solution.py:22
  1.5 0.1 select_convert_fusion
  1.6 0.8 %pad_maximum_fusion = bf16[2,8320]{1,0:T(2,128)(2,1)S(1)} fusion(bf16[2,128]{1,0:T(2,128)(2,1)S(1)} %select_convert_fusion, bf16[2,3584]{1,0:T(2,128)(2,1)} %param.6, bf16[2,4608]{1,0:T(2,128)(2,1)} %param.5), kind=kLoop, calls=%fused_computation.6 | loop fusion | flops 99840 | bytes 66560 | tf_op jit(solution)/shard_map/concatenate | solution.py:23
  2.3 0.8 %broadcast_in_dim.61 = bf16[8,2,8320]{2,1,0:T(2,128)(2,1)} broadcast(bf16[2,8320]{1,0:T(2,128)(2,1)S(1)} %pad_maximum_fusion), dimensions={1,2} | broadcast | bytes 299520 | tf_op jit(solution)/shard_map/broadcast_in_dim | solution.py:12
  3.2 7.3 %all-to-all-start = ((bf16[8,2,8320]{2,1,0:T(2,128)(2,1)}), bf16[8,2,8320]{2,1,0:T(2,128)(2,1)S(1)}, u32[]{:S(2)}, u32[]{:S(2)}) async-start(bf16[8,2,8320]{2,1,0:T(2,128)(2,1)} %broadcast_in_dim.61), calls=%async_computation | async-start | bytes 532480 | tf_op jit(solution)/shard_map/all_to_all | solution.py:13
  10.4 9.0 %all-to-all-done = bf16[8,2,8320]{2,1,0:T(2,128)(2,1)S(1)} async-done(((bf16[8,2,8320]{2,1,0:T(2,128)(2,1)}), bf16[8,2,8320]{2,1,0:T(2,128)(2,1)S(1)}, u32[]{:S(2)}, u32[]{:S(2)}) %all-to-all-start) | async-done | bytes 266272 | tf_op jit(solution)/shard_map/all_to_all | solution.py:13
  19.4 0.1 reshape.24
  19.6 0.0 copy-done.1
  19.6 0.3 fusion.17
  19.9 0.0 copy-done
  19.9 0.4 fusion.16
  20.3 0.2 fusion.7
  20.5 0.2 select_reduce_fusion
  20.8 10.1 %all_to_all.15 = f32[8,16,6]{1,2,0:T(8,128)S(1)} all-to-all(f32[8,16,6]{1,2,0:T(8,128)S(1)} %broadcast_in_dim.69), channel_id=1, replica_groups=mesh['groups'=2,'vocab'=8,'rows'=2] {'vocab'}, dimensions={0} | all-to-all | bytes 6144 | tf_op jit(solution)/shard_map/all_to_all | solution.py:13
  30.9 0.1 subtract_convert_fusion
  31.0 0.3 fusion.18
  31.4 0.8 %reshape.25 = f32[8,2,3584]{2,1,0:T(2,128)} reshape(f32[16,3584]{1,0:T(8,128)S(1)} %fusion.18) | data formatting | bytes 458752 | tf_op jit(solution)/shard_map/reshape | solution.py:68
  32.2 3.4 %all-to-all-start.2 = ((f32[8,2,3584]{2,1,0:T(2,128)}), f32[8,2,3584]{2,1,0:T(2,128)S(1)}, u32[]{:S(2)}, u32[]{:S(2)}) async-start(f32[8,2,3584]{2,1,0:T(2,128)} %reshape.25), calls=%async_computation.2 | async-start | bytes 458752 | tf_op jit(solution)/shard_map/all_to_all | solution.py:68
  35.6 0.1 collective-permute-start
  35.7 0.5 %collective-permute-start.1 = (bf16[16,128]{1,0:T(8,128)(2,1)S(1)}, bf16[16,128]{1,0:T(8,128)(2,1)S(1)}, u32[]{:S(2)}, u32[]{:S(2)}) collective-permute-start(bf16[16,128]{1,0:T(8,128)(2,1)S(1)} %subtract_convert_fusion), channel_id=1, source_target_pairs={{0,1},{1,0},{2,3},{3,2},{4,5},{5,4},{6,7},{7,6},{8,9},{9,8},{10,11... | collective-permute-start | bytes 12296 | tf_op jit(solution)/shard_map/ppermute | solution.py:66
  36.2 0.6 %dynamic_slice.3 = f32[2]{0:T(128)} dynamic-slice(f32[16]{0:T(128)S(1)} %add_subtract_fusion, s32[]{:T(128)S(6)} %select_n.27), dynamic_slice_sizes={2} | dynamic-slice | bytes 20 | tf_op jit(solution)/shard_map/dynamic_slice | solution.py:61
  36.8 0.2 collective-permute-done.1
  37.0 0.0 collective-permute-done
  37.0 1.7 %fusion = f32[3584,128]{1,0:T(8,128)} fusion(bf16[16,3584]{1,0:T(8,128)(2,1)S(1)} %collective-permute-done, bf16[16,3584]{1,0:T(8,128)(2,1)S(1)} %slice.47, bf16[16,128]{1,0:T(8,128)(2,1)S(1)} %collective-permute-done.1, bf16[16,128]{1,0:T(8,128)(2,1)S(1)} %subtract_convert_fusion), kind=kOutput, calls=%fused_computation | convolution fusion | flops 29835264 | bytes 2072576 | tf_op jit(solution)/shard_map/dot_general | solution.py:70
  38.7 4.8 %all-to-all-done.2 = f32[8,2,3584]{2,1,0:T(2,128)S(1)} async-done(((f32[8,2,3584]{2,1,0:T(2,128)}), f32[8,2,3584]{2,1,0:T(2,128)S(1)}, u32[]{:S(2)}, u32[]{:S(2)}) %all-to-all-start.2) | async-done | bytes 229408 | tf_op jit(solution)/shard_map/all_to_all | solution.py:68
  43.6 0.7 %reduce_sum.89 = f32[2,3584]{1,0:T(2,128)} reduce(f32[8,2,3584]{2,1,0:T(2,128)S(1)} %all-to-all-done.2, f32[]{:T(128)} %constant.42.clone.1), dimensions={0}, to_apply=%region_12.13 | reduce | flops 50176 | bytes 258052 | tf_op jit(solution)/shard_map/reduce_sum | solution.py:69
  (11 shorter events, 0.2 us)
Async XLA Ops:
  0.6 19.3 %copy-start = (bf16[4608,128]{1,0:T(8,128)(2,1)S(1)}, bf16[4608,128]{1,0:T(8,128)(2,1)}, u32[]{:S(2)}) copy-start(bf16[4608,128]{1,0:T(8,128)(2,1)} %param.7) | copy-start | bytes 3538948
  0.6 18.9 %copy-start.1 = (bf16[3584,128]{1,0:T(8,128)(2,1)S(1)}, bf16[3584,128]{1,0:T(8,128)(2,1)}, u32[]{:S(2)}) copy-start(bf16[3584,128]{1,0:T(8,128)(2,1)} %param.8) | copy-start | bytes 2752516
  3.2 16.3 %all-to-all-start = ((bf16[8,2,8320]{2,1,0:T(2,128)(2,1)}), bf16[8,2,8320]{2,1,0:T(2,128)(2,1)S(1)}, u32[]{:S(2)}, u32[]{:S(2)}) async-start(bf16[8,2,8320]{2,1,0:T(2,128)(2,1)} %broadcast_in_dim.61), calls=%async_computation | async-start | bytes 532480 | tf_op jit(solution)/shard_map/all_to_all | solution.py:13
  32.2 11.3 %all-to-all-start.2 = ((f32[8,2,3584]{2,1,0:T(2,128)}), f32[8,2,3584]{2,1,0:T(2,128)S(1)}, u32[]{:S(2)}, u32[]{:S(2)}) async-start(f32[8,2,3584]{2,1,0:T(2,128)} %reshape.25), calls=%async_computation.2 | async-start | bytes 458752 | tf_op jit(solution)/shard_map/all_to_all | solution.py:68
  35.6 1.4 %collective-permute-start = (bf16[16,3584]{1,0:T(8,128)(2,1)S(1)}, bf16[16,3584]{1,0:T(8,128)(2,1)S(1)}, u32[]{:S(2)}, u32[]{:S(2)}) collective-permute-start(bf16[16,3584]{1,0:T(8,128)(2,1)S(1)} %slice.47), channel_id=1, source_target_pairs={{0,1},{1,0},{2,3},{3,2},{4,5},{5,4},{6,7},{7,6},{8,9},{9,8},{10,11... | collective-permute-start | bytes 344072 | tf_op jit(solution)/shard_map/ppermute | solution.py:30
  35.7 1.3 %collective-permute-start.1 = (bf16[16,128]{1,0:T(8,128)(2,1)S(1)}, bf16[16,128]{1,0:T(8,128)(2,1)S(1)}, u32[]{:S(2)}, u32[]{:S(2)}) collective-permute-start(bf16[16,128]{1,0:T(8,128)(2,1)S(1)} %subtract_convert_fusion), channel_id=1, source_target_pairs={{0,1},{1,0},{2,3},{3,2},{4,5},{5,4},{6,7},{7,6},{8,9},{9,8},{10,11... | collective-permute-start | bytes 12296 | tf_op jit(solution)/shard_map/ppermute | solution.py:66

commit v2 on v1

--- a/solution.py
+++ b/solution.py
@@ -6,11 +6,55 @@
 F32 = jnp.float32
 BF16 = jnp.bfloat16
 CODE = 128
+DIRECT = 16
 
 
-def spread(block, axis, size):
-    copies = jnp.broadcast_to(block[None], (size,) + block.shape)
-    return lax.all_to_all(copies, axis, split_axis=0, concat_axis=0, tiled=True)
+def spread(block, shards):
+    copies = jnp.broadcast_to(block[None], (shards,) + block.shape)
+    return lax.all_to_all(copies, "vocab", split_axis=0, concat_axis=0, tiled=True)
+
+
+def from_peers(blocks, shards):
+    return [blocks[0]] + [
+        lax.ppermute(blocks[k], "vocab", [(i, i ^ k) for i in range(shards)]) for k in range(1, shards)
+    ]
+
+
+def gather_tokens(block, shards):
+    if shards <= DIRECT:
+        return jnp.concatenate(from_peers([block] * shards, shards), axis=0)
+    return spread(block, shards).reshape(shards * block.shape[0], -1)
+
+
+def gather_stats(stats, shards):
+    if shards > DIRECT:
+        return spread(stats, shards)
+    own = stats.shape[0] // shards
+    return jnp.stack(
+        [
+            jnp.concatenate([block[(i ^ k) * own : (i ^ k) * own + own] for i in range(shards)], axis=0)
+            for k, block in enumerate(from_peers([stats] * shards, shards))
+        ]
+    )
+
+
+def own_tokens(array, shards):
+    own = array.shape[0] // shards
+    if shards <= DIRECT:
+        return array[:own]
+    return lax.dynamic_slice_in_dim(array, lax.axis_index("vocab") * own, own, 0)
+
+
+def sum_to_owner(partial, shards):
+    own = partial.shape[0] // shards
+    if shards > DIRECT:
+        blocks = partial.reshape(shards, own, -1)
+        return jnp.sum(lax.all_to_all(blocks, "vocab", split_axis=0, concat_axis=0, tiled=True), axis=0)
+    arrived = from_peers([partial[k * own : k * own + own] for k in range(shards)], shards)
+    total = arrived[0]
+    for block in arrived[1:]:
+        total = total + block
+    return total
 
 
 def on_device(teacher_hidden, student_hidden, teacher_head, student_head, labels, *, shards):
@@ -21,7 +65,7 @@
     lanes = lax.broadcasted_iota(jnp.int32, (own, CODE), 1)
     digits = jnp.where(lanes == 0, (labels // 128)[:, None], (labels % 128)[:, None])
     payload = jnp.concatenate([teacher_hidden, student_hidden, digits.astype(BF16)], axis=1)
-    rows = spread(payload, "vocab", shards).reshape(shards * own, -1)
+    rows = gather_tokens(payload, shards)
     teacher_rows = rows[:, :teacher_width]
     student_rows = rows[:, teacher_width : teacher_width + student_width]
     code = rows[:, teacher_width + student_width :].astype(jnp.int32)
@@ -48,7 +92,7 @@
         ],
         axis=1,
     )
-    every = spread(stats, "vocab", shards)
+    every = gather_stats(stats, shards)
     all_top_t = jnp.max(every[:, :, 0], axis=0)
     factor_t = jnp.exp(every[:, :, 0] - all_top_t[None])
     all_top_s = jnp.max(every[:, :, 3], axis=0)
@@ -58,15 +102,14 @@
     mass_s = jnp.sum(every[:, :, 4] * factor_s, axis=0)
     picked = jnp.sum(every[:, :, 5], axis=0)
     loss = cross / mass_t - all_top_t - jnp.log(mass_t) + 2.0 * (all_top_s + jnp.log(mass_s)) - picked
-    token_loss = lax.dynamic_slice_in_dim(loss, lax.axis_index("vocab") * own, own, 0)
+    token_loss = own_tokens(loss, shards)
 
     teacher_prob = jnp.exp(teacher_logits - all_top_t[:, None]) / mass_t[:, None]
     student_prob = jnp.exp(student_logits - all_top_s[:, None]) / mass_s[:, None]
     grad_rows = (2.0 * student_prob - teacher_prob - target.astype(F32)).astype(BF16)
     grad_other = lax.ppermute(grad_rows, "rows", other)
     partial = lax.dot_general(grad_rows, student_head, (((1,), (1,)), ((), ())), preferred_element_type=F32)
-    arrived = lax.all_to_all(partial.reshape(shards, own, student_width), "vocab", split_axis=0, concat_axis=0, tiled=True)
-    hidden_grad = jnp.sum(arrived, axis=0)
+    hidden_grad = sum_to_owner(partial, shards)
     head_grad = lax.dot_general(
         jnp.concatenate([student_rows, student_other], axis=0),
         jnp.concatenate([grad_rows, grad_other], axis=0),

time: 44.6 us -> 60.1 us (1.35)
  starting transfers between devices: 11.2 us -> 34.9 us
  blocking collectives: 10.1 us -> 0 us
  matrix products: 2.74 us -> 3.92 us
  other arithmetic: 3 us -> 3.64 us
    ppermute x0 -> x21, starting transfers between devices: none -> 34.4 us  [from_peers(): lax.ppermute(blocks[k], 'vocab', [(i, i ^ k) for i in range(shards)])]
    ppermute x0 -> x21, waiting for transfers between devices: none -> 14.1 us  [from_peers(): lax.ppermute(blocks[k], 'vocab', [(i, i ^ k) for i in range(shards)])]
    all_to_all x2 -> x0, waiting for transfers between devices: 13.8 us -> none  [the longest x1 9 us: spread(): return lax.all_to_all(copies, axis, split_axis=0, concat_axis=0, tiled=True)]
    all_to_all x2 -> x0, starting transfers between devices: 10.7 us -> none  [the longest x1 7.25 us: spread(): return lax.all_to_all(copies, axis, split_axis=0, concat_axis=0, tiled=True)]
    all_to_all x1 -> x0, blocking collectives: 10.1 us -> none  [spread(): return lax.all_to_all(copies, axis, split_axis=0, concat_axis=0, tiled=True)]
    concatenate x0 -> x5, local copies, waits for them, and re-layouts: none -> 1.87 us  [the longest x1 1.55 us: gather_tokens(): return jnp.concatenate(from_peers([block] * shards, shards), axis=0)]
    dot_general x1, matrix products: 0.34 us -> 1.52 us  [on_device(): jnp.dot(student_rows, student_head, preferred_element_type=F32)]
    reshape x2 -> x0, local copies, waits for them, and re-layouts: 0.92 us -> none  [the longest x1 0.82 us: on_device(): partial.reshape(shards, own, student_width)]
  transfers between devices with their start and end apart: 4 -> 23, of which waited for: 3 -> 9; matrix products, arithmetic and copies ran while one was open for 5% -> 4% of each run, Pallas kernels for 0% -> 0%
where the time goes in v2:
time: 60.1 us; the launch traced here: 59.9 us
  starting transfers between devices  34.9 us (58%)
  waiting for transfers between devices  14.1 us (23%)
  matrix products  3.92 us (7%)
  other arithmetic  3.64 us (6%)
  local copies, waits for them, and re-layouts  2.55 us (4%)
  between operations  0.77 us (1%)
    ppermute x21, starting transfers between devices, from_peers(): lax.ppermute(blocks[k], 'vocab', [(i, i ^ k) for i in range(shards)])  34.4 us
    ppermute x21, waiting for transfers between devices, from_peers(): lax.ppermute(blocks[k], 'vocab', [(i, i ^ k) for i in range(shards)])  14.1 us
    dot_general x1, matrix products, on_device(): lax.dot_general(jnp.concatenate([student_rows, student_other], axis=0), j...  1.69 us
    concatenate x1, local copies, waits for them, and re-layouts, gather_tokens(): return jnp.concatenate(from_peers([block] * shards, shards), axis=0)  1.55 us
    dot_general x1, matrix products, on_device(): jnp.dot(student_rows, student_head, preferred_element_type=F32)  1.52 us
  transfers between devices with their start and end apart: 23, of which 9 were waited for; matrix products, arithmetic and copies ran while one was open for 4% of the time, Pallas kernels for 0%

profile of v2, /device:TPU:0, one launch (start us, length us, event | category | flops | bytes accessed | tf_op | source)
XLA Modules:
  0.0 59.9 jit_solution(15522706678244486164)
XLA Ops:
  0.6 0.0 copy-start
  0.7 0.8 %and_select_fusion.1 = (s32[2]{0:T(128)S(1)}, s32[2]{0:T(128)S(1)}) fusion(s32[2]{0:T(128)} %param.9), kind=kLoop, calls=%fused_computation.46 | loop fusion | flops 38 | bytes 24 | tf_op jit(solution)/shard_map/jit(floor_divide)/jit(_where)/select_n | solution.py:66
  1.4 0.1 select_convert_fusion
  1.5 0.8 %pad_maximum_fusion = bf16[2,8320]{1,0:T(2,128)(2,1)S(1)} fusion(bf16[2,128]{1,0:T(2,128)(2,1)S(1)} %select_convert_fusion, bf16[2,3584]{1,0:T(2,128)(2,1)} %param.6, bf16[2,4608]{1,0:T(2,128)(2,1)} %param.5), kind=kLoop, calls=%fused_computation.6 | loop fusion | flops 99840 | bytes 66560 | tf_op jit(solution)/shard_map/concatenate | solution.py:67
  2.3 6.0 %collective-permute-start.6 = (bf16[2,8320]{1,0:T(2,128)(2,1)S(1)}, bf16[2,8320]{1,0:T(2,128)(2,1)S(1)}, u32[]{:S(2)}, u32[]{:S(2)}) collective-permute-start(bf16[2,8320]{1,0:T(2,128)(2,1)S(1)} %pad_maximum_fusion), channel_id=1, source_target_pairs={{0,14},{2,12},{4,10},{6,8},{8,6},{10,4},{12,2},{14,0},{1,15},{3,13... | collective-permute-start | bytes 99848 | tf_op jit(solution)/shard_map/ppermute | solution.py:19
  8.3 0.2 collective-permute-start.5
  8.5 0.8 %collective-permute-start.4 = (bf16[2,8320]{1,0:T(2,128)(2,1)S(1)}, bf16[2,8320]{1,0:T(2,128)(2,1)S(1)}, u32[]{:S(2)}, u32[]{:S(2)}) collective-permute-start(bf16[2,8320]{1,0:T(2,128)(2,1)S(1)} %pad_maximum_fusion), channel_id=1, source_target_pairs={{0,10},{2,8},{4,14},{6,12},{8,2},{10,0},{12,6},{14,4},{1,11},{3,9}... | collective-permute-start | bytes 99848 | tf_op jit(solution)/shard_map/ppermute | solution.py:19
  9.3 2.0 %collective-permute-start.3 = (bf16[2,8320]{1,0:T(2,128)(2,1)S(1)}, bf16[2,8320]{1,0:T(2,128)(2,1)S(1)}, u32[]{:S(2)}, u32[]{:S(2)}) collective-permute-start(bf16[2,8320]{1,0:T(2,128)(2,1)S(1)} %pad_maximum_fusion), channel_id=1, source_target_pairs={{0,8},{2,10},{4,12},{6,14},{8,0},{10,2},{12,4},{14,6},{1,9},{3,11}... | collective-permute-start | bytes 99848 | tf_op jit(solution)/shard_map/ppermute | solution.py:19
  11.3 2.3 %collective-permute-start.2 = (bf16[2,8320]{1,0:T(2,128)(2,1)S(1)}, bf16[2,8320]{1,0:T(2,128)(2,1)S(1)}, u32[]{:S(2)}, u32[]{:S(2)}) collective-permute-start(bf16[2,8320]{1,0:T(2,128)(2,1)S(1)} %pad_maximum_fusion), channel_id=1, source_target_pairs={{0,6},{2,4},{4,2},{6,0},{8,14},{10,12},{12,10},{14,8},{1,7},{3,5},... | collective-permute-start | bytes 99848 | tf_op jit(solution)/shard_map/ppermute | solution.py:19
  13.6 0.0 collective-permute-done.6
  13.6 0.8 %collective-permute-start.1 = (bf16[2,8320]{1,0:T(2,128)(2,1)S(1)}, bf16[2,8320]{1,0:T(2,128)(2,1)S(1)}, u32[]{:S(2)}, u32[]{:S(2)}) collective-permute-start(bf16[2,8320]{1,0:T(2,128)(2,1)S(1)} %pad_maximum_fusion), channel_id=1, source_target_pairs={{0,4},{2,6},{4,0},{6,2},{8,12},{10,14},{12,8},{14,10},{1,5},{3,7},... | collective-permute-start | bytes 99848 | tf_op jit(solution)/shard_map/ppermute | solution.py:19
  14.4 0.0 collective-permute-done.5
  14.4 0.4 collective-permute-start
  14.8 0.3 collective-permute-done.3
  15.1 1.0 %collective-permute-done.2 = bf16[2,8320]{1,0:T(2,128)(2,1)S(1)} collective-permute-done((bf16[2,8320]{1,0:T(2,128)(2,1)S(1)}, bf16[2,8320]{1,0:T(2,128)(2,1)S(1)}, u32[]{:S(2)}, u32[]{:S(2)}) %collective-permute-start.2) | collective-permute-done | bytes 33312 | tf_op jit(solution)/shard_map/ppermute | solution.py:19
  16.1 1.4 %collective-permute-done.1 = bf16[2,8320]{1,0:T(2,128)(2,1)S(1)} collective-permute-done((bf16[2,8320]{1,0:T(2,128)(2,1)S(1)}, bf16[2,8320]{1,0:T(2,128)(2,1)S(1)}, u32[]{:S(2)}, u32[]{:S(2)}) %collective-permute-start.1) | collective-permute-done | bytes 33312 | tf_op jit(solution)/shard_map/ppermute | solution.py:19
  17.5 0.8 %collective-permute-done = bf16[2,8320]{1,0:T(2,128)(2,1)S(1)} collective-permute-done((bf16[2,8320]{1,0:T(2,128)(2,1)S(1)}, bf16[2,8320]{1,0:T(2,128)(2,1)S(1)}, u32[]{:S(2)}, u32[]{:S(2)}) %collective-permute-start) | collective-permute-done | bytes 33312 | tf_op jit(solution)/shard_map/ppermute | solution.py:19
  18.3 1.5 %concatenate.42 = bf16[16,8320]{1,0:T(8,128)(2,1)S(1)} concatenate(bf16[2,8320]{1,0:T(2,128)(2,1)S(1)} %pad_maximum_fusion, bf16[2,8320]{1,0:T(2,128)(2,1)S(1)} %collective-permute-done, bf16[2,8320]{1,0:T(2,128)(2,1)S(1)} %collective-permute-done.1, bf16[2,8320]{1,0:T(2,128)(2,1)S(1)} %collective-permute-done.2, bf16[2,8320]{1,0:T(2,128)(2,1)S(1)} %collective-permute-done.3, ...), dimensions={0} | concatenate | bytes 532480 | tf_op jit(solution)/shard_map/concatenate | solution.py:25
  19.9 1.5 %fusion.30 = (f32[16]{0:T(128)S(1)}, f32[16,128]{1,0:T(8,128)S(1)}) fusion(bf16[3584,128]{1,0:T(8,128)(2,1)} %param.8, bf16[16,8320]{1,0:T(8,128)(2,1)S(1)} %concatenate.42), kind=kOutput, calls=%fused_computation.67 | convolution fusion | flops 14682096 | bytes 1040448 | tf_op jit(solution)/shard_map/dot_general | solution.py:77
  21.4 0.0 copy-start.1
  21.4 0.4 fusion.29
  21.8 0.2 fusion.13
  22.0 0.2 select_reduce_fusion
  22.3 3.6 %collective-permute-start.13 = (f32[16,6]{0,1:T(8,128)S(1)}, f32[16,6]{0,1:T(8,128)S(1)}, u32[]{:S(2)}, u32[]{:S(2)}) collective-permute-start(f32[16,6]{0,1:T(8,128)S(1)} %concatenate.43), channel_id=1, source_target_pairs={{0,14},{2,12},{4,10},{6,8},{8,6},{10,4},{12,2},{14,0},{1,15},{3,13... | collective-permute-start | bytes 1160 | tf_op jit(solution)/shard_map/ppermute | solution.py:19
  25.9 0.1 collective-permute-start.12
  26.0 1.5 %collective-permute-start.11 = (f32[16,6]{0,1:T(8,128)S(1)}, f32[16,6]{0,1:T(8,128)S(1)}, u32[]{:S(2)}, u32[]{:S(2)}) collective-permute-start(f32[16,6]{0,1:T(8,128)S(1)} %concatenate.43), channel_id=1, source_target_pairs={{0,10},{2,8},{4,14},{6,12},{8,2},{10,0},{12,6},{14,4},{1,11},{3,9}... | collective-permute-start | bytes 1160 | tf_op jit(solution)/shard_map/ppermute | solution.py:19
  27.5 2.5 %collective-permute-start.10 = (f32[16,6]{0,1:T(8,128)S(1)}, f32[16,6]{0,1:T(8,128)S(1)}, u32[]{:S(2)}, u32[]{:S(2)}) collective-permute-start(f32[16,6]{0,1:T(8,128)S(1)} %concatenate.43), channel_id=1, source_target_pairs={{0,8},{2,10},{4,12},{6,14},{8,0},{10,2},{12,4},{14,6},{1,9},{3,11}... | collective-permute-start | bytes 1160 | tf_op jit(solution)/shard_map/ppermute | solution.py:19
  30.0 0.4 collective-permute-start.7
  30.4 3.2 %collective-permute-done.7 = f32[16,6]{0,1:T(8,128)S(1)} collective-permute-done((f32[16,6]{0,1:T(8,128)S(1)}, f32[16,6]{0,1:T(8,128)S(1)}, u32[]{:S(2)}, u32[]{:S(2)}) %collective-permute-start.7) | collective-permute-done | bytes 416 | tf_op jit(solution)/shard_map/ppermute | solution.py:19
  33.6 1.2 %collective-permute-start.8 = (f32[16,6]{0,1:T(8,128)S(1)}, f32[16,6]{0,1:T(8,128)S(1)}, u32[]{:S(2)}, u32[]{:S(2)}) collective-permute-start(f32[16,6]{0,1:T(8,128)S(1)} %concatenate.43), channel_id=1, source_target_pairs={{0,4},{2,6},{4,0},{6,2},{8,12},{10,14},{12,8},{14,10},{1,5},{3,7},... | collective-permute-start | bytes 1160 | tf_op jit(solution)/shard_map/ppermute | solution.py:19
  34.8 0.1 fusion.28
  34.9 0.1 concatenate.44
  35.0 2.2 %collective-permute-done.8 = f32[16,6]{0,1:T(8,128)S(1)} collective-permute-done((f32[16,6]{0,1:T(8,128)S(1)}, f32[16,6]{0,1:T(8,128)S(1)}, u32[]{:S(2)}, u32[]{:S(2)}) %collective-permute-start.8) | collective-permute-done | bytes 416 | tf_op jit(solution)/shard_map/ppermute | solution.py:19
  37.2 1.2 %collective-permute-start.9 = (f32[16,6]{0,1:T(8,128)S(1)}, f32[16,6]{0,1:T(8,128)S(1)}, u32[]{:S(2)}, u32[]{:S(2)}) collective-permute-start(f32[16,6]{0,1:T(8,128)S(1)} %concatenate.43), channel_id=1, source_target_pairs={{0,6},{2,4},{4,2},{6,0},{8,14},{10,12},{12,10},{14,8},{1,7},{3,5},... | collective-permute-start | bytes 1160 | tf_op jit(solution)/shard_map/ppermute | solution.py:19
  38.4 0.1 fusion.27
  38.5 0.1 constant_dynamic-update-slice_fusion.5
  38.6 3.1 %collective-permute-done.9 = f32[16,6]{0,1:T(8,128)S(1)} collective-permute-done((f32[16,6]{0,1:T(8,128)S(1)}, f32[16,6]{0,1:T(8,128)S(1)}, u32[]{:S(2)}, u32[]{:S(2)}) %collective-permute-start.9) | collective-permute-done | bytes 416 | tf_op jit(solution)/shard_map/ppermute | solution.py:19
  41.7 0.1 fusion.26
  41.8 0.1 concatenate.46
  41.9 0.0 collective-permute-done.10
  41.9 0.1 fusion.25
  41.9 0.1 constant_dynamic-update-slice_fusion.3
  42.0 0.1 fusion.24
  42.1 0.1 concatenate.48
  42.2 0.1 fusion.23
  42.3 0.1 constant_dynamic-update-slice_fusion.1
  42.3 0.1 fusion.22
  42.4 0.1 concatenate.50
  42.6 0.1 subtract_convert_fusion
  42.7 0.3 fusion.31
  43.0 0.1 fusion.21
  43.1 0.5 collective-permute-start.14
  43.6 4.6 %collective-permute-start.20 = (f32[2,3584]{1,0:T(2,128)S(1)}, f32[2,3584]{1,0:T(2,128)S(1)}, u32[]{:S(2)}, u32[]{:S(2)}) collective-permute-start(f32[2,3584]{1,0:T(2,128)S(1)} %get-tuple-element.15), channel_id=1, source_target_pairs={{0,14},{2,12},{4,10},{6,8},{8,6},{10,4},{12,2},{14,0},{1,15},{3,13... | collective-permute-start | bytes 86024 | tf_op jit(solution)/shard_map/ppermute | solution.py:19
  48.3 0.3 collective-permute-start.19
  48.6 0.3 collective-permute-start.18
  48.9 2.4 %collective-permute-start.17 = (f32[2,3584]{1,0:T(2,128)S(1)}, f32[2,3584]{1,0:T(2,128)S(1)}, u32[]{:S(2)}, u32[]{:S(2)}) collective-permute-start(f32[2,3584]{1,0:T(2,128)S(1)} %get-tuple-element.18), channel_id=1, source_target_pairs={{0,8},{2,10},{4,12},{6,14},{8,0},{10,2},{12,4},{14,6},{1,9},{3,11}... | collective-permute-start | bytes 86024 | tf_op jit(solution)/shard_map/ppermute | solution.py:19
  51.4 2.3 %collective-permute-start.16 = (f32[2,3584]{1,0:T(2,128)S(1)}, f32[2,3584]{1,0:T(2,128)S(1)}, u32[]{:S(2)}, u32[]{:S(2)}) collective-permute-start(f32[2,3584]{1,0:T(2,128)S(1)} %get-tuple-element.19), channel_id=1, source_target_pairs={{0,6},{2,4},{4,2},{6,0},{8,14},{10,12},{12,10},{14,8},{1,7},{3,5},... | collective-permute-start | bytes 86024 | tf_op jit(solution)/shard_map/ppermute | solution.py:19
  53.6 0.8 %collective-permute-start.15 = (f32[2,3584]{1,0:T(2,128)S(1)}, f32[2,3584]{1,0:T(2,128)S(1)}, u32[]{:S(2)}, u32[]{:S(2)}) collective-permute-start(f32[2,3584]{1,0:T(2,128)S(1)} %get-tuple-element.20), channel_id=1, source_target_pairs={{0,4},{2,6},{4,0},{6,2},{8,12},{10,14},{12,8},{14,10},{1,5},{3,7},... | collective-permute-start | bytes 86024 | tf_op jit(solution)/shard_map/ppermute | solution.py:19
  54.4 0.5 add_subtract_fusion
  55.0 0.5 collective-permute-start.22
  55.5 0.7 %collective-permute-done.16 = f32[2,3584]{1,0:T(2,128)S(1)} collective-permute-done((f32[2,3584]{1,0:T(2,128)S(1)}, f32[2,3584]{1,0:T(2,128)S(1)}, u32[]{:S(2)}, u32[]{:S(2)}) %collective-permute-start.16) | collective-permute-done | bytes 28704 | tf_op jit(solution)/shard_map/ppermute | solution.py:19
  56.1 1.4 %collective-permute-done.15 = f32[2,3584]{1,0:T(2,128)S(1)} collective-permute-done((f32[2,3584]{1,0:T(2,128)S(1)}, f32[2,3584]{1,0:T(2,128)S(1)}, u32[]{:S(2)}, u32[]{:S(2)}) %collective-permute-start.15) | collective-permute-done | bytes 28704 | tf_op jit(solution)/shard_map/ppermute | solution.py:19
  57.5 0.7 %fusion.11 = f32[2,3584]{1,0:T(2,128)} fusion(f32[2,3584]{1,0:T(2,128)S(1)} %collective-permute-done.20, f32[2,3584]{1,0:T(2,128)S(1)} %collective-permute-done.19, f32[2,3584]{1,0:T(2,128)S(1)} %collective-permute-done.18, f32[2,3584]{1,0:T(2,128)S(1)} %collective-permute-done.17, f32[2,3584]{1,0:T(2,128)S(1)} %collective-permute-done.16, ...), kind=kLoop, calls=%fused_computation.13 | loop fusion | flops 50176 | bytes 258048 | tf_op jit(solution)/shard_map/add | solution.py:56
  58.2 1.7 %fusion = f32[3584,128]{1,0:T(8,128)} fusion(bf16[16,3584]{1,0:T(8,128)(2,1)S(1)} %collective-permute-done.21, bf16[16,3584]{1,0:T(8,128)(2,1)S(1)} %slice.284, bf16[16,128]{1,0:T(8,128)(2,1)S(1)} %collective-permute-done.22, bf16[16,128]{1,0:T(8,128)(2,1)S(1)} %subtract_convert_fusion), kind=kOutput, calls=%fused_computation | convolution fusion | flops 29835264 | bytes 2072576 | tf_op jit(solution)/shard_map/dot_general | solution.py:113
  (26 shorter events, 0.2 us)
Async XLA Ops:
  0.6 20.8 %copy-start = (bf16[4608,128]{1,0:T(8,128)(2,1)S(1)}, bf16[4608,128]{1,0:T(8,128)(2,1)}, u32[]{:S(2)}) copy-start(bf16[4608,128]{1,0:T(8,128)(2,1)} %param.7) | copy-start | bytes 3538948
  2.3 11.3 %collective-permute-start.6 = (bf16[2,8320]{1,0:T(2,128)(2,1)S(1)}, bf16[2,8320]{1,0:T(2,128)(2,1)S(1)}, u32[]{:S(2)}, u32[]{:S(2)}) collective-permute-start(bf16[2,8320]{1,0:T(2,128)(2,1)S(1)} %pad_maximum_fusion), channel_id=1, source_target_pairs={{0,14},{2,12},{4,10},{6,8},{8,6},{10,4},{12,2},{14,0},{1,15},{3,13... | collective-permute-start | bytes 99848 | tf_op jit(solution)/shard_map/ppermute | solution.py:19
  8.3 6.1 %collective-permute-start.5 = (bf16[2,8320]{1,0:T(2,128)(2,1)S(1)}, bf16[2,8320]{1,0:T(2,128)(2,1)S(1)}, u32[]{:S(2)}, u32[]{:S(2)}) collective-permute-start(bf16[2,8320]{1,0:T(2,128)(2,1)S(1)} %pad_maximum_fusion), channel_id=1, source_target_pairs={{0,12},{2,14},{4,8},{6,10},{8,4},{10,6},{12,0},{14,2},{1,13},{3,15... | collective-permute-start | bytes 99848 | tf_op jit(solution)/shard_map/ppermute | solution.py:19
  8.5 6.3 %collective-permute-start.4 = (bf16[2,8320]{1,0:T(2,128)(2,1)S(1)}, bf16[2,8320]{1,0:T(2,128)(2,1)S(1)}, u32[]{:S(2)}, u32[]{:S(2)}) collective-permute-start(bf16[2,8320]{1,0:T(2,128)(2,1)S(1)} %pad_maximum_fusion), channel_id=1, source_target_pairs={{0,10},{2,8},{4,14},{6,12},{8,2},{10,0},{12,6},{14,4},{1,11},{3,9}... | collective-permute-start | bytes 99848 | tf_op jit(solution)/shard_map/ppermute | solution.py:19
  9.3 5.8 %collective-permute-start.3 = (bf16[2,8320]{1,0:T(2,128)(2,1)S(1)}, bf16[2,8320]{1,0:T(2,128)(2,1)S(1)}, u32[]{:S(2)}, u32[]{:S(2)}) collective-permute-start(bf16[2,8320]{1,0:T(2,128)(2,1)S(1)} %pad_maximum_fusion), channel_id=1, source_target_pairs={{0,8},{2,10},{4,12},{6,14},{8,0},{10,2},{12,4},{14,6},{1,9},{3,11}... | collective-permute-start | bytes 99848 | tf_op jit(solution)/shard_map/ppermute | solution.py:19
  11.3 4.8 %collective-permute-start.2 = (bf16[2,8320]{1,0:T(2,128)(2,1)S(1)}, bf16[2,8320]{1,0:T(2,128)(2,1)S(1)}, u32[]{:S(2)}, u32[]{:S(2)}) collective-permute-start(bf16[2,8320]{1,0:T(2,128)(2,1)S(1)} %pad_maximum_fusion), channel_id=1, source_target_pairs={{0,6},{2,4},{4,2},{6,0},{8,14},{10,12},{12,10},{14,8},{1,7},{3,5},... | collective-permute-start | bytes 99848 | tf_op jit(solution)/shard_map/ppermute | solution.py:19
  13.6 3.9 %collective-permute-start.1 = (bf16[2,8320]{1,0:T(2,128)(2,1)S(1)}, bf16[2,8320]{1,0:T(2,128)(2,1)S(1)}, u32[]{:S(2)}, u32[]{:S(2)}) collective-permute-start(bf16[2,8320]{1,0:T(2,128)(2,1)S(1)} %pad_maximum_fusion), channel_id=1, source_target_pairs={{0,4},{2,6},{4,0},{6,2},{8,12},{10,14},{12,8},{14,10},{1,5},{3,7},... | collective-permute-start | bytes 99848 | tf_op jit(solution)/shard_map/ppermute | solution.py:19
  14.4 3.9 %collective-permute-start = (bf16[2,8320]{1,0:T(2,128)(2,1)S(1)}, bf16[2,8320]{1,0:T(2,128)(2,1)S(1)}, u32[]{:S(2)}, u32[]{:S(2)}) collective-permute-start(bf16[2,8320]{1,0:T(2,128)(2,1)S(1)} %pad_maximum_fusion), channel_id=1, source_target_pairs={{0,2},{2,0},{4,6},{6,4},{8,10},{10,8},{12,14},{14,12},{1,3},{3,1},... | collective-permute-start | bytes 99848 | tf_op jit(solution)/shard_map/ppermute | solution.py:19
  21.4 21.3 %copy-start.1 = (bf16[3584,128]{1,0:T(8,128)(2,1)S(1)}, bf16[3584,128]{1,0:T(8,128)(2,1)}, u32[]{:S(2)}) copy-start(bf16[3584,128]{1,0:T(8,128)(2,1)} %param.8) | copy-start | bytes 2752516
  22.3 20.1 %collective-permute-start.13 = (f32[16,6]{0,1:T(8,128)S(1)}, f32[16,6]{0,1:T(8,128)S(1)}, u32[]{:S(2)}, u32[]{:S(2)}) collective-permute-start(f32[16,6]{0,1:T(8,128)S(1)} %concatenate.43), channel_id=1, source_target_pairs={{0,14},{2,12},{4,10},{6,8},{8,6},{10,4},{12,2},{14,0},{1,15},{3,13... | collective-permute-start | bytes 1160 | tf_op jit(solution)/shard_map/ppermute | solution.py:19
  25.9 16.3 %collective-permute-start.12 = (f32[16,6]{0,1:T(8,128)S(1)}, f32[16,6]{0,1:T(8,128)S(1)}, u32[]{:S(2)}, u32[]{:S(2)}) collective-permute-start(f32[16,6]{0,1:T(8,128)S(1)} %concatenate.43), channel_id=1, source_target_pairs={{0,12},{2,14},{4,8},{6,10},{8,4},{10,6},{12,0},{14,2},{1,13},{3,15... | collective-permute-start | bytes 1160 | tf_op jit(solution)/shard_map/ppermute | solution.py:19
  26.0 16.0 %collective-permute-start.11 = (f32[16,6]{0,1:T(8,128)S(1)}, f32[16,6]{0,1:T(8,128)S(1)}, u32[]{:S(2)}, u32[]{:S(2)}) collective-permute-start(f32[16,6]{0,1:T(8,128)S(1)} %concatenate.43), channel_id=1, source_target_pairs={{0,10},{2,8},{4,14},{6,12},{8,2},{10,0},{12,6},{14,4},{1,11},{3,9}... | collective-permute-start | bytes 1160 | tf_op jit(solution)/shard_map/ppermute | solution.py:19
  27.5 14.4 %collective-permute-start.10 = (f32[16,6]{0,1:T(8,128)S(1)}, f32[16,6]{0,1:T(8,128)S(1)}, u32[]{:S(2)}, u32[]{:S(2)}) collective-permute-start(f32[16,6]{0,1:T(8,128)S(1)} %concatenate.43), channel_id=1, source_target_pairs={{0,8},{2,10},{4,12},{6,14},{8,0},{10,2},{12,4},{14,6},{1,9},{3,11}... | collective-permute-start | bytes 1160 | tf_op jit(solution)/shard_map/ppermute | solution.py:19
  30.0 3.6 %collective-permute-start.7 = (f32[16,6]{0,1:T(8,128)S(1)}, f32[16,6]{0,1:T(8,128)S(1)}, u32[]{:S(2)}, u32[]{:S(2)}) collective-permute-start(f32[16,6]{0,1:T(8,128)S(1)} %concatenate.43), channel_id=1, source_target_pairs={{0,2},{2,0},{4,6},{6,4},{8,10},{10,8},{12,14},{14,12},{1,3},{3,1},... | collective-permute-start | bytes 1160 | tf_op jit(solution)/shard_map/ppermute | solution.py:19
  33.6 3.6 %collective-permute-start.8 = (f32[16,6]{0,1:T(8,128)S(1)}, f32[16,6]{0,1:T(8,128)S(1)}, u32[]{:S(2)}, u32[]{:S(2)}) collective-permute-start(f32[16,6]{0,1:T(8,128)S(1)} %concatenate.43), channel_id=1, source_target_pairs={{0,4},{2,6},{4,0},{6,2},{8,12},{10,14},{12,8},{14,10},{1,5},{3,7},... | collective-permute-start | bytes 1160 | tf_op jit(solution)/shard_map/ppermute | solution.py:19
  37.2 4.5 %collective-permute-start.9 = (f32[16,6]{0,1:T(8,128)S(1)}, f32[16,6]{0,1:T(8,128)S(1)}, u32[]{:S(2)}, u32[]{:S(2)}) collective-permute-start(f32[16,6]{0,1:T(8,128)S(1)} %concatenate.43), channel_id=1, source_target_pairs={{0,6},{2,4},{4,2},{6,0},{8,14},{10,12},{12,10},{14,8},{1,7},{3,5},... | collective-permute-start | bytes 1160 | tf_op jit(solution)/shard_map/ppermute | solution.py:19
  43.1 8.2 %collective-permute-start.14 = (f32[2,3584]{1,0:T(2,128)S(1)}, f32[2,3584]{1,0:T(2,128)S(1)}, u32[]{:S(2)}, u32[]{:S(2)}) collective-permute-start(f32[2,3584]{1,0:T(2,128)S(1)} %get-tuple-element.14), channel_id=1, source_target_pairs={{0,2},{2,0},{4,6},{6,4},{8,10},{10,8},{12,14},{14,12},{1,3},{3,1},... | collective-permute-start | bytes 86024 | tf_op jit(solution)/shard_map/ppermute | solution.py:19
  43.6 10.0 %collective-permute-start.20 = (f32[2,3584]{1,0:T(2,128)S(1)}, f32[2,3584]{1,0:T(2,128)S(1)}, u32[]{:S(2)}, u32[]{:S(2)}) collective-permute-start(f32[2,3584]{1,0:T(2,128)S(1)} %get-tuple-element.15), channel_id=1, source_target_pairs={{0,14},{2,12},{4,10},{6,8},{8,6},{10,4},{12,2},{14,0},{1,15},{3,13... | collective-permute-start | bytes 86024 | tf_op jit(solution)/shard_map/ppermute | solution.py:19
  48.3 6.7 %collective-permute-start.19 = (f32[2,3584]{1,0:T(2,128)S(1)}, f32[2,3584]{1,0:T(2,128)S(1)}, u32[]{:S(2)}, u32[]{:S(2)}) collective-permute-start(f32[2,3584]{1,0:T(2,128)S(1)} %get-tuple-element.16), channel_id=1, source_target_pairs={{0,12},{2,14},{4,8},{6,10},{8,4},{10,6},{12,0},{14,2},{1,13},{3,15... | collective-permute-start | bytes 86024 | tf_op jit(solution)/shard_map/ppermute | solution.py:19
  48.6 6.4 %collective-permute-start.18 = (f32[2,3584]{1,0:T(2,128)S(1)}, f32[2,3584]{1,0:T(2,128)S(1)}, u32[]{:S(2)}, u32[]{:S(2)}) collective-permute-start(f32[2,3584]{1,0:T(2,128)S(1)} %get-tuple-element.17), channel_id=1, source_target_pairs={{0,10},{2,8},{4,14},{6,12},{8,2},{10,0},{12,6},{14,4},{1,11},{3,9}... | collective-permute-start | bytes 86024 | tf_op jit(solution)/shard_map/ppermute | solution.py:19
  48.9 6.6 %collective-permute-start.17 = (f32[2,3584]{1,0:T(2,128)S(1)}, f32[2,3584]{1,0:T(2,128)S(1)}, u32[]{:S(2)}, u32[]{:S(2)}) collective-permute-start(f32[2,3584]{1,0:T(2,128)S(1)} %get-tuple-element.18), channel_id=1, source_target_pairs={{0,8},{2,10},{4,12},{6,14},{8,0},{10,2},{12,4},{14,6},{1,9},{3,11}... | collective-permute-start | bytes 86024 | tf_op jit(solution)/shard_map/ppermute | solution.py:19
  51.4 4.8 %collective-permute-start.16 = (f32[2,3584]{1,0:T(2,128)S(1)}, f32[2,3584]{1,0:T(2,128)S(1)}, u32[]{:S(2)}, u32[]{:S(2)}) collective-permute-start(f32[2,3584]{1,0:T(2,128)S(1)} %get-tuple-element.19), channel_id=1, source_target_pairs={{0,6},{2,4},{4,2},{6,0},{8,14},{10,12},{12,10},{14,8},{1,7},{3,5},... | collective-permute-start | bytes 86024 | tf_op jit(solution)/shard_map/ppermute | solution.py:19
  53.6 3.9 %collective-permute-start.15 = (f32[2,3584]{1,0:T(2,128)S(1)}, f32[2,3584]{1,0:T(2,128)S(1)}, u32[]{:S(2)}, u32[]{:S(2)}) collective-permute-start(f32[2,3584]{1,0:T(2,128)S(1)} %get-tuple-element.20), channel_id=1, source_target_pairs={{0,4},{2,6},{4,0},{6,2},{8,12},{10,14},{12,8},{14,10},{1,5},{3,7},... | collective-permute-start | bytes 86024 | tf_op jit(solution)/shard_map/ppermute | solution.py:19
  55.0 3.2 %collective-permute-start.21 = (bf16[16,3584]{1,0:T(8,128)(2,1)S(1)}, bf16[16,3584]{1,0:T(8,128)(2,1)S(1)}, u32[]{:S(2)}, u32[]{:S(2)}) collective-permute-start(bf16[16,3584]{1,0:T(8,128)(2,1)S(1)} %slice.284), channel_id=1, source_target_pairs={{0,1},{1,0},{2,3},{3,2},{4,5},{5,4},{6,7},{7,6},{8,9},{9,8},{10,11... | collective-permute-start | bytes 344072 | tf_op jit(solution)/shard_map/ppermute | solution.py:74
  55.0 3.2 %collective-permute-start.22 = (bf16[16,128]{1,0:T(8,128)(2,1)S(1)}, bf16[16,128]{1,0:T(8,128)(2,1)S(1)}, u32[]{:S(2)}, u32[]{:S(2)}) collective-permute-start(bf16[16,128]{1,0:T(8,128)(2,1)S(1)} %subtract_convert_fusion), channel_id=1, source_target_pairs={{0,1},{1,0},{2,3},{3,2},{4,5},{5,4},{6,7},{7,6},{8,9},{9,8},{10,11... | collective-permute-start | bytes 12296 | tf_op jit(solution)/shard_map/ppermute | solution.py:110

commit v3 on v1

--- a/solution.py
+++ b/solution.py
@@ -48,15 +48,18 @@
         ],
         axis=1,
     )
-    every = spread(stats, "vocab", shards)
-    all_top_t = jnp.max(every[:, :, 0], axis=0)
-    factor_t = jnp.exp(every[:, :, 0] - all_top_t[None])
-    all_top_s = jnp.max(every[:, :, 3], axis=0)
-    factor_s = jnp.exp(every[:, :, 3] - all_top_s[None])
-    mass_t = jnp.sum(every[:, :, 1] * factor_t, axis=0)
-    cross = jnp.sum(every[:, :, 2] * factor_t, axis=0)
-    mass_s = jnp.sum(every[:, :, 4] * factor_s, axis=0)
-    picked = jnp.sum(every[:, :, 5], axis=0)
+    here = lax.axis_index("vocab")
+    flat = stats.T.reshape(1, -1)
+    mine = lax.broadcasted_iota(jnp.int32, (shards, 1), 0) == here
+    every = lax.psum(jnp.where(mine, flat, 0.0), "vocab").reshape(shards, 6, shards * own)
+    all_top_t = jnp.max(every[:, 0], axis=0)
+    factor_t = jnp.exp(every[:, 0] - all_top_t[None])
+    all_top_s = jnp.max(every[:, 3], axis=0)
+    factor_s = jnp.exp(every[:, 3] - all_top_s[None])
+    mass_t = jnp.sum(every[:, 1] * factor_t, axis=0)
+    cross = jnp.sum(every[:, 2] * factor_t, axis=0)
+    mass_s = jnp.sum(every[:, 4] * factor_s, axis=0)
+    picked = jnp.sum(every[:, 5], axis=0)
     loss = cross / mass_t - all_top_t - jnp.log(mass_t) + 2.0 * (all_top_s + jnp.log(mass_s)) - picked
     token_loss = lax.dynamic_slice_in_dim(loss, lax.axis_index("vocab") * own, own, 0)
 
@@ -65,8 +68,11 @@
     grad_rows = (2.0 * student_prob - teacher_prob - target.astype(F32)).astype(BF16)
     grad_other = lax.ppermute(grad_rows, "rows", other)
     partial = lax.dot_general(grad_rows, student_head, (((1,), (1,)), ((), ())), preferred_element_type=F32)
-    arrived = lax.all_to_all(partial.reshape(shards, own, student_width), "vocab", split_axis=0, concat_axis=0, tiled=True)
-    hidden_grad = jnp.sum(arrived, axis=0)
+    arrived = lax.all_to_all(
+        partial.astype(BF16).reshape(shards, own, student_width), "vocab", split_axis=0, concat_axis=0, tiled=True
+    )
+    own_partial = lax.dynamic_slice_in_dim(partial, here * own, own, 0)
+    hidden_grad = own_partial + jnp.sum(jnp.where(mine[:, :, None], 0.0, arrived.astype(F32)), axis=0)
     head_grad = lax.dot_general(
         jnp.concatenate([student_rows, student_other], axis=0),
         jnp.concatenate([grad_rows, grad_other], axis=0),

time: 44.6 us -> 69.8 us (1.57)
  blocking collectives: 10.1 us -> 35.2 us
    psum x0 -> x1, blocking collectives: none -> 35.2 us  [on_device(): lax.psum(jnp.where(mine, flat, 0.0), 'vocab')]
    all_to_all x1 -> x0, blocking collectives: 10.1 us -> none  [spread(): return lax.all_to_all(copies, axis, split_axis=0, concat_axis=0, tiled=True)]
  transfers between devices with their start and end apart: 4 -> 4, of which waited for: 3 -> 2; matrix products, arithmetic and copies ran while one was open for 5% -> 5% of each run, Pallas kernels for 0% -> 0%
where the time goes in v3:
time: 69.8 us; the launch traced here: 69.3 us
  blocking collectives  35.2 us (50%)
  waiting for transfers between devices  13.9 us (20%)
  starting transfers between devices  11.2 us (16%)
  other arithmetic  3.18 us (5%)
  matrix products  2.74 us (4%)
  local copies, waits for them, and re-layouts  2.42 us (3%)
  between operations  0.74 us (1%)
    psum x1, blocking collectives, on_device(): lax.psum(jnp.where(mine, flat, 0.0), 'vocab')  35.2 us
    all_to_all x1, waiting for transfers between devices, spread(): return lax.all_to_all(copies, axis, split_axis=0, concat_axis=0, tiled=True)  9 us
    all_to_all x1, starting transfers between devices, spread(): return lax.all_to_all(copies, axis, split_axis=0, concat_axis=0, tiled=True)  7.25 us
    all_to_all x1, waiting for transfers between devices, on_device(): lax.all_to_all(partial.astype(BF16).reshape(shards, own, student_width),...  4.86 us
    all_to_all x1, starting transfers between devices, on_device(): lax.all_to_all(partial.astype(BF16).reshape(shards, own, student_width),...  3.37 us
    dot_general x1, matrix products, on_device(): lax.dot_general(jnp.concatenate([student_rows, student_other], axis=0), j...  1.69 us
  transfers between devices with their start and end apart: 4, of which 2 were waited for; matrix products, arithmetic and copies ran while one was open for 5% of the time, Pallas kernels for 0%

profile of v3, /device:TPU:0, one launch (start us, length us, event | category | flops | bytes accessed | tf_op | source)
XLA Modules:
  0.0 69.3 jit_solution(7640510323302191627)
XLA Ops:
  0.6 0.0 copy-start
  0.6 0.0 copy-start.1
  0.7 0.8 %and_select_fusion.1 = (s32[2]{0:T(128)S(1)}, s32[2]{0:T(128)S(1)}) fusion(s32[2]{0:T(128)} %param.9), kind=kLoop, calls=%fused_computation.31 | loop fusion | flops 38 | bytes 24 | tf_op jit(solution)/shard_map/jit(floor_divide)/jit(_where)/select_n | solution.py:22
  1.5 0.1 select_convert_fusion
  1.6 0.8 %pad_maximum_fusion = bf16[2,8320]{1,0:T(2,128)(2,1)S(1)} fusion(bf16[2,128]{1,0:T(2,128)(2,1)S(1)} %select_convert_fusion, bf16[2,3584]{1,0:T(2,128)(2,1)} %param.6, bf16[2,4608]{1,0:T(2,128)(2,1)} %param.5), kind=kLoop, calls=%fused_computation.7 | loop fusion | flops 99840 | bytes 66560 | tf_op jit(solution)/shard_map/concatenate | solution.py:23
  2.3 0.8 %broadcast_in_dim.91 = bf16[8,2,8320]{2,1,0:T(2,128)(2,1)} broadcast(bf16[2,8320]{1,0:T(2,128)(2,1)S(1)} %pad_maximum_fusion), dimensions={1,2} | broadcast | bytes 299520 | tf_op jit(solution)/shard_map/broadcast_in_dim | solution.py:12
  3.2 7.3 %all-to-all-start = ((bf16[8,2,8320]{2,1,0:T(2,128)(2,1)}), bf16[8,2,8320]{2,1,0:T(2,128)(2,1)S(1)}, u32[]{:S(2)}, u32[]{:S(2)}) async-start(bf16[8,2,8320]{2,1,0:T(2,128)(2,1)} %broadcast_in_dim.91), calls=%async_computation | async-start | bytes 532480 | tf_op jit(solution)/shard_map/all_to_all | solution.py:13
  10.4 9.0 %all-to-all-done = bf16[8,2,8320]{2,1,0:T(2,128)(2,1)S(1)} async-done(((bf16[8,2,8320]{2,1,0:T(2,128)(2,1)}), bf16[8,2,8320]{2,1,0:T(2,128)(2,1)S(1)}, u32[]{:S(2)}, u32[]{:S(2)}) %all-to-all-start) | async-done | bytes 266272 | tf_op jit(solution)/shard_map/all_to_all | solution.py:13
  19.4 0.1 reshape.37
  19.6 0.0 copy-done.1
  19.6 0.3 fusion.16
  19.9 0.0 copy-done
  19.9 0.4 fusion.15
  20.3 0.2 fusion.7
  20.5 0.2 select_reduce_fusion.1
  20.8 0.1 broadcast_in_dim.99
  20.8 0.1 broadcast_select_fusion
  20.9 0.1 reshape.38
  21.0 35.2 %psum.7 = f32[8,6,16]{2,1,0:T(8,128)S(1)} all-reduce(f32[8,6,16]{2,1,0:T(8,128)S(1)} %reshape.38), channel_id=1, replica_groups=mesh['groups'=2,'vocab'=8,'rows'=2] {'vocab'}, use_global_device_ids=true, to_apply=%region_6.7 | all-reduce | flops 768 | bytes 6144 | tf_op jit(solution)/shard_map/psum | solution.py:54
  56.2 0.1 subtract_convert_fusion
  56.3 0.1 collective-permute-start.1
  56.4 0.3 fusion.17
  56.8 0.5 collective-permute-start
  57.3 0.7 reshape.39
  58.0 3.4 %all-to-all-start.1 = ((bf16[8,2,3584]{2,1,0:T(2,128)(2,1)}), bf16[8,2,3584]{2,1,0:T(2,128)(2,1)S(1)}, u32[]{:S(2)}, u32[]{:S(2)}) async-start(bf16[8,2,3584]{2,1,0:T(2,128)(2,1)} %reshape.39), calls=%async_computation.1 | async-start | bytes 229376 | tf_op jit(solution)/shard_map/all_to_all | solution.py:71
  61.4 0.6 dynamic_slice.6
  62.0 0.0 collective-permute-done.1
  62.0 0.0 collective-permute-done
  62.0 1.7 %fusion = f32[3584,128]{1,0:T(8,128)} fusion(bf16[16,3584]{1,0:T(8,128)(2,1)S(1)} %collective-permute-done, bf16[16,3584]{1,0:T(8,128)(2,1)S(1)} %slice.47, bf16[16,128]{1,0:T(8,128)(2,1)S(1)} %collective-permute-done.1, bf16[16,128]{1,0:T(8,128)(2,1)S(1)} %subtract_convert_fusion), kind=kOutput, calls=%fused_computation | convolution fusion | flops 29835264 | bytes 2072576 | tf_op jit(solution)/shard_map/dot_general | solution.py:76
  63.7 4.9 %all-to-all-done.1 = bf16[8,2,3584]{2,1,0:T(2,128)(2,1)S(1)} async-done(((bf16[8,2,3584]{2,1,0:T(2,128)(2,1)}), bf16[8,2,3584]{2,1,0:T(2,128)(2,1)S(1)}, u32[]{:S(2)}, u32[]{:S(2)}) %all-to-all-start.1) | async-done | bytes 114720 | tf_op jit(solution)/shard_map/all_to_all | solution.py:71
  68.5 0.2 select_reduce_fusion
  68.7 0.6 dynamic-slice_add_fusion
  (9 shorter events, 0.2 us)
Async XLA Ops:
  0.6 19.3 %copy-start = (bf16[4608,128]{1,0:T(8,128)(2,1)S(1)}, bf16[4608,128]{1,0:T(8,128)(2,1)}, u32[]{:S(2)}) copy-start(bf16[4608,128]{1,0:T(8,128)(2,1)} %param.7) | copy-start | bytes 3538948
  0.6 18.9 %copy-start.1 = (bf16[3584,128]{1,0:T(8,128)(2,1)S(1)}, bf16[3584,128]{1,0:T(8,128)(2,1)}, u32[]{:S(2)}) copy-start(bf16[3584,128]{1,0:T(8,128)(2,1)} %param.8) | copy-start | bytes 2752516
  3.2 16.3 %all-to-all-start = ((bf16[8,2,8320]{2,1,0:T(2,128)(2,1)}), bf16[8,2,8320]{2,1,0:T(2,128)(2,1)S(1)}, u32[]{:S(2)}, u32[]{:S(2)}) async-start(bf16[8,2,8320]{2,1,0:T(2,128)(2,1)} %broadcast_in_dim.91), calls=%async_computation | async-start | bytes 532480 | tf_op jit(solution)/shard_map/all_to_all | solution.py:13
  56.3 5.6 %collective-permute-start.1 = (bf16[16,128]{1,0:T(8,128)(2,1)S(1)}, bf16[16,128]{1,0:T(8,128)(2,1)S(1)}, u32[]{:S(2)}, u32[]{:S(2)}) collective-permute-start(bf16[16,128]{1,0:T(8,128)(2,1)S(1)} %subtract_convert_fusion), channel_id=1, source_target_pairs={{0,1},{1,0},{2,3},{3,2},{4,5},{5,4},{6,7},{7,6},{8,9},{9,8},{10,11... | collective-permute-start | bytes 12296 | tf_op jit(solution)/shard_map/ppermute | solution.py:69
  56.8 5.2 %collective-permute-start = (bf16[16,3584]{1,0:T(8,128)(2,1)S(1)}, bf16[16,3584]{1,0:T(8,128)(2,1)S(1)}, u32[]{:S(2)}, u32[]{:S(2)}) collective-permute-start(bf16[16,3584]{1,0:T(8,128)(2,1)S(1)} %slice.47), channel_id=1, source_target_pairs={{0,1},{1,0},{2,3},{3,2},{4,5},{5,4},{6,7},{7,6},{8,9},{9,8},{10,11... | collective-permute-start | bytes 344072 | tf_op jit(solution)/shard_map/ppermute | solution.py:30
  58.0 10.5 %all-to-all-start.1 = ((bf16[8,2,3584]{2,1,0:T(2,128)(2,1)}), bf16[8,2,3584]{2,1,0:T(2,128)(2,1)S(1)}, u32[]{:S(2)}, u32[]{:S(2)}) async-start(bf16[8,2,3584]{2,1,0:T(2,128)(2,1)} %reshape.39), calls=%async_computation.1 | async-start | bytes 229376 | tf_op jit(solution)/shard_map/all_to_all | solution.py:71

commit v4 on v3

v4 whole, which is shorter than its diff:
```python
import jax
import jax.numpy as jnp
from jax import lax
from jax.experimental import pallas as pl
from jax.experimental.pallas import tpu as pltpu
from jax.sharding import PartitionSpec as P

F32 = jnp.float32
BF16 = jnp.bfloat16
CODE = 128


UNROLL = 16
SMEM = pl.BlockSpec(memory_space=pltpu.SMEM)
VMEM = pl.BlockSpec(memory_space=pltpu.VMEM)


def over_shards(shards, body):
    if shards <= UNROLL:
        for shard in range(shards):
            body(shard)
    else:
        pl.loop(0, shards)(body)


def swap(blocks):
    return lax.all_to_all(blocks, "vocab", split_axis=0, concat_axis=0, tiled=True)


def payload_kernel(labels_ref, teacher_ref, student_ref, out_ref):
    shards, own, _ = out_ref.shape
    teacher_width, student_width = teacher_ref.shape[1], student_ref.shape[1]
    row = lax.broadcasted_iota(jnp.int32, (own, CODE), 0)
    lane = lax.broadcasted_iota(jnp.int32, (own, CODE), 1)
    digits = jnp.zeros((own, CODE), jnp.int32)
    for token in range(own):
        label = labels_ref[token]
        pair = jnp.where(lane == 0, label >> 7, label & 127)
        digits = jnp.where(row == token, pair, digits)
    teacher = teacher_ref[...]
    student = student_ref[...]
    code = digits.astype(F32).astype(BF16)

    def write(shard):
        out_ref[shard, :, :teacher_width] = teacher
        out_ref[shard, :, teacher_width : teacher_width + student_width] = student
        out_ref[shard, :, teacher_width + student_width :] = code

    over_shards(shards, write)


def partial_kernel(here_ref, grad_ref, head_ref, out_ref, own_ref, total_ref):
    shards, own, _ = out_ref.shape
    total_ref[...] = lax.dot_general(
        grad_ref[...], head_ref[...], (((1,), (1,)), ((), ())), preferred_element_type=F32
    )

    together = 8 // own

    def write(group):
        start = group * 8 if isinstance(group, int) else pl.multiple_of(group * 8, 8)
        rows = total_ref[pl.ds(start, 8), :]
        for place in range(together):
            shard = group * together + place
            block = rows[place * own : place * own + own]
            out_ref[shard] = block.astype(BF16)

            @pl.when(shard == here_ref[0])
            def _():
                own_ref[...] = block

    over_shards(shards // together, write)


def sum_kernel(here_ref, arrived_ref, own_ref, out_ref):
    out_ref[...] = own_ref[...]

    def add(shard):
        block = arrived_ref[shard].astype(F32)
        out_ref[...] += jnp.where(shard == here_ref[0], jnp.zeros_like(block), block)

    over_shards(arrived_ref.shape[0], add)


def on_device(teacher_hidden, student_hidden, teacher_head, student_head, labels, *, shards):
    own, teacher_width = teacher_hidden.shape
    student_width = student_hidden.shape[1]
    columns_here = student_head.shape[1]
    first_column = lax.axis_index("vocab") * columns_here
    here = lax.axis_index("vocab").astype(jnp.int32)[None]
    payload = pl.pallas_call(
        payload_kernel,
        out_shape=jax.ShapeDtypeStruct((shards, own, teacher_width + student_width + CODE), BF16),
        in_specs=[SMEM, VMEM, VMEM],
        out_specs=VMEM,
    )(labels, teacher_hidden, student_hidden)
    rows = swap(payload).reshape(shards * own, -1)
    teacher_rows = rows[:, :teacher_width]
    student_rows = rows[:, teacher_width : teacher_width + student_width]
    code = rows[:, teacher_width + student_width :].astype(jnp.int32)
    label_rows = code[:, 0] * 128 + code[:, 1]
    other = [(0, 1), (1, 0)]
    student_other = lax.ppermute(student_rows, "rows", other)

    teacher_logits = jnp.dot(teacher_rows, teacher_head, preferred_element_type=F32)
    student_logits = jnp.dot(student_rows, student_head, preferred_element_type=F32)
    columns = lax.broadcasted_iota(jnp.int32, student_logits.shape, 1)
    target = (label_rows - first_column)[:, None] == columns
    top_t = jnp.max(teacher_logits, axis=1, keepdims=True)
    exp_t = jnp.exp(teacher_logits - top_t)
    top_s = jnp.max(student_logits, axis=1, keepdims=True)
    exp_s = jnp.exp(student_logits - top_s)
    stats = jnp.stack(
        [
            top_t[:, 0],
            jnp.sum(exp_t, axis=1),
            jnp.sum(exp_t * (teacher_logits - student_logits), axis=1),
            top_s[:, 0],
            jnp.sum(exp_s, axis=1),
            jnp.sum(jnp.where(target, student_logits, 0.0), axis=1),
        ]
    )
    lanes = -(-shards * own // 128) * 128
    stats = jnp.pad(stats, ((0, 2), (0, lanes - shards * own)))
    every = swap(jnp.broadcast_to(stats[None], (shards,) + stats.shape))[:, :, : shards * own]
    all_top_t = jnp.max(every[:, 0], axis=0)
    factor_t = jnp.exp(every[:, 0] - all_top_t[None])
    all_top_s = jnp.max(every[:, 3], axis=0)
    factor_s = jnp.exp(every[:, 3] - all_top_s[None])
    mass_t = jnp.sum(every[:, 1] * factor_t, axis=0)
    cross = jnp.sum(every[:, 2] * factor_t, axis=0)
    mass_s = jnp.sum(every[:, 4] * factor_s, axis=0)
    picked = jnp.sum(every[:, 5], axis=0)
    loss = cross / mass_t - all_top_t - jnp.log(mass_t) + 2.0 * (all_top_s + jnp.log(mass_s)) - picked
    token_loss = lax.dynamic_slice_in_dim(loss, lax.axis_index("vocab") * own, own, 0)

    teacher_prob = jnp.exp(teacher_logits - all_top_t[:, None]) / mass_t[:, None]
    student_prob = jnp.exp(student_logits - all_top_s[:, None]) / mass_s[:, None]
    grad_rows = (2.0 * student_prob - teacher_prob - target.astype(F32)).astype(BF16)
    grad_other = lax.ppermute(grad_rows, "rows", other)
    block = (shards, own, student_width)
    partials, own_partial = pl.pallas_call(
        partial_kernel,
        out_shape=(jax.ShapeDtypeStruct(block, BF16), jax.ShapeDtypeStruct(block[1:], F32)),
        in_specs=[SMEM, VMEM, VMEM],
        out_specs=(VMEM, VMEM),
        scratch_shapes=[pltpu.VMEM((shards * own, student_width), F32)],
    )(here, grad_rows, student_head)
    hidden_grad = pl.pallas_call(
        sum_kernel,
        out_shape=jax.ShapeDtypeStruct(block[1:], F32),
        in_specs=[SMEM, VMEM, VMEM],
        out_specs=VMEM,
    )(here, swap(partials), own_partial)
    head_grad = lax.dot_general(
        jnp.concatenate([student_rows, student_other], axis=0),
        jnp.concatenate([grad_rows, grad_other], axis=0),
        (((0,), (0,)), ((), ())),
        preferred_element_type=F32,
    )
    return (token_loss, hidden_grad, head_grad)


def solution(mesh):
    tokens = ("groups", "vocab", "rows")
    in_specs = (P(tokens, None), P(tokens, None), P(None, "vocab"), P(None, "vocab"), P(tokens))
    out_specs = (P(tokens), P(tokens, None), P("groups", "vocab"))

    def body(*arrays):
        return on_device(*arrays, shards=mesh.shape["vocab"])

    return jax.shard_map(body, mesh=mesh, in_specs=in_specs, out_specs=out_specs, check_vma=False)
```

time: 69.8 us -> 47 us (0.67)
  blocking collectives: 35.2 us -> 0 us
  waiting for transfers between devices: 13.9 us -> 19.8 us
  Pallas kernels: 0 us -> 5.41 us
  starting transfers between devices: 11.2 us -> 14.3 us
  other arithmetic: 3.18 us -> 0.48 us
    psum x1 -> x0, blocking collectives: 35.2 us -> none  [on_device(): lax.psum(jnp.where(mine, flat, 0.0), 'vocab')]
    all_to_all x2 -> x3, waiting for transfers between devices: 13.9 us -> 19.8 us  [swap(): lax.all_to_all(blocks, 'vocab', split_axis=0, concat_axis=0, tiled=True)]
    pallas_call x0 -> x3, Pallas kernels: none -> 5.41 us  [the longest x1 2.25 us: on_device(): pl.pallas_call(partial_kernel, out_shape=(jax.ShapeDtypeStruct(block, BF1...]
    all_to_all x2 -> x3, starting transfers between devices: 10.6 us -> 14.2 us  [swap(): lax.all_to_all(blocks, 'vocab', split_axis=0, concat_axis=0, tiled=True)]
    unnamed x4 -> x9, local copies, waits for them, and re-layouts: 0.01 us -> 1.28 us
    select_n x2 -> x0, other arithmetic: 0.88 us -> none  [the longest x1 0.81 us: on_device(): labels // 128]
    concatenate x1 -> x0, other arithmetic: 0.77 us -> none  [on_device(): jnp.concatenate([teacher_hidden, student_hidden, digits.astype(BF16)], ax...]
    reshape x3 -> x1, local copies, waits for them, and re-layouts: 0.86 us -> 0.1 us  [on_device(): rows = swap(payload).reshape(shards * own, -1)]
  transfers between devices with their start and end apart: 4 -> 5, of which waited for: 2 -> 3; matrix products, arithmetic and copies ran while one was open for 5% -> 7% of each run, Pallas kernels for 0% -> 5%
where the time goes in v4:
time: 47 us; the launch traced here: 46.5 us
  waiting for transfers between devices  19.8 us (42%)
  starting transfers between devices  14.3 us (30%)
  Pallas kernels  5.41 us (12%)
  matrix products  3.09 us (7%)
  local copies, waits for them, and re-layouts  2.64 us (6%)
  between operations  0.77 us (2%)
  other arithmetic  0.48 us (1%)
    all_to_all x3, waiting for transfers between devices, swap(): lax.all_to_all(blocks, 'vocab', split_axis=0, concat_axis=0, tiled=True)  19.8 us
    all_to_all x3, starting transfers between devices, swap(): lax.all_to_all(blocks, 'vocab', split_axis=0, concat_axis=0, tiled=True)  14.2 us
    dot_general x1, matrix products, on_device(): lax.dot_general(jnp.concatenate([student_rows, student_other], axis=0), j...  2.37 us
    pallas_call x1, Pallas kernels, on_device(): pl.pallas_call(partial_kernel, out_shape=(jax.ShapeDtypeStruct(block, BF1...  2.25 us
    pallas_call x1, Pallas kernels, on_device(): pl.pallas_call(payload_kernel, out_shape=jax.ShapeDtypeStruct((shards, ow...  1.62 us
    pallas_call x1, Pallas kernels, on_device(): pl.pallas_call(sum_kernel, out_shape=jax.ShapeDtypeStruct(block[1:], F32)...  1.54 us
    unnamed x9, local copies, waits for them, and re-layouts  1.28 us
  transfers between devices with their start and end apart: 5, of which 3 were waited for; matrix products, arithmetic and copies ran while one was open for 7% of the time, Pallas kernels for 5%

profile of v4, /device:TPU:0, one launch (start us, length us, event | category | flops | bytes accessed | tf_op | source)
XLA Modules:
  0.0 46.5 jit_solution(13576182688352537532)
XLA Ops:
  0.6 0.0 copy-start
  0.6 0.0 copy-start.1
  0.7 1.6 %shard_map.76 = bf16[8,2,8320]{2,1,0:T(2,128)(2,1)} custom-call(s32[2]{0:T(128)} %labels_ref.1, bf16[2,4608]{1,0:T(2,128)(2,1)} %teacher_ref.1, bf16[2,3584]{1,0:T(2,128)(2,1)} %student_ref.1), custom_call_target="tpu_custom_call" | custom-call | tf_op jit(solution)/shard_map/pallas_call | solution.py:91
  2.3 7.3 %all-to-all-start = ((bf16[8,2,8320]{2,1,0:T(2,128)(2,1)}), bf16[8,2,8320]{2,1,0:T(2,128)(2,1)S(1)}, u32[]{:S(2)}, u32[]{:S(2)}) async-start(bf16[8,2,8320]{2,1,0:T(2,128)(2,1)} %shard_map.76), calls=%async_computation | async-start | bytes 532480 | tf_op jit(solution)/shard_map/all_to_all | solution.py:27
  9.5 9.0 %all-to-all-done = bf16[8,2,8320]{2,1,0:T(2,128)(2,1)S(1)} async-done(((bf16[8,2,8320]{2,1,0:T(2,128)(2,1)}), bf16[8,2,8320]{2,1,0:T(2,128)(2,1)S(1)}, u32[]{:S(2)}, u32[]{:S(2)}) %all-to-all-start) | async-done | bytes 266272 | tf_op jit(solution)/shard_map/all_to_all | solution.py:27
  18.5 0.1 reshape.18
  18.7 0.0 copy-done.1
  18.7 0.3 fusion.17
  19.0 0.0 copy-done
  19.0 0.4 fusion.16
  19.4 0.1 copy.15
  19.6 0.2 select_reduce_fusion
  19.8 0.6 %broadcast_in_dim.9 = f32[8,8,128]{2,1,0:T(8,128)} broadcast(f32[8,128]{1,0:T(8,128)S(1)} %pad.4), dimensions={1,2} | broadcast | bytes 36864 | tf_op jit(solution)/shard_map/broadcast_in_dim | solution.py:125
  20.5 3.6 %all-to-all-start.1 = ((f32[8,8,128]{2,1,0:T(8,128)}), f32[8,8,128]{2,1,0:T(8,128)S(1)}, u32[]{:S(2)}, u32[]{:S(2)}) async-start(f32[8,8,128]{2,1,0:T(8,128)} %broadcast_in_dim.9), calls=%async_computation.1 | async-start | bytes 65536 | tf_op jit(solution)/shard_map/all_to_all | solution.py:27
  24.1 0.1 collective-permute-start
  24.1 6.6 %all-to-all-done.1 = f32[8,8,128]{2,1,0:T(8,128)S(1)} async-done(((f32[8,8,128]{2,1,0:T(8,128)}), f32[8,8,128]{2,1,0:T(8,128)S(1)}, u32[]{:S(2)}, u32[]{:S(2)}) %all-to-all-start.1) | async-done | bytes 32800 | tf_op jit(solution)/shard_map/all_to_all | solution.py:27
  30.9 0.1 subtract_convert_fusion.grad_ref
  31.0 0.0 copy-start.3
  31.0 0.1 collective-permute-start.1
  31.0 0.5 %copy-done.3 = bf16[16,128]{1,0:T(8,128)(2,1)} copy-done((bf16[16,128]{1,0:T(8,128)(2,1)}, bf16[16,128]{1,0:T(8,128)(2,1)S(1)}, u32[]{:S(2)}) %copy-start.3) | copy-done | bytes 4120
  31.5 2.3 %shard_map.77 = (bf16[8,2,3584]{2,1,0:T(2,128)(2,1)}, f32[2,3584]{1,0:T(2,128)}) custom-call(s32[1]{0:T(128)} %bitcast.12.here_ref, bf16[16,128]{1,0:T(8,128)(2,1)} %copy-done.3, bf16[3584,128]{1,0:T(8,128)(2,1)} %head_ref.1), custom_call_target="tpu_custom_call" | custom-call | tf_op jit(solution)/shard_map/pallas_call | solution.py:142
  33.8 3.4 %all-to-all-start.2 = ((bf16[8,2,3584]{2,1,0:T(2,128)(2,1)}), bf16[8,2,3584]{2,1,0:T(2,128)(2,1)S(1)}, u32[]{:S(2)}, u32[]{:S(2)}) async-start(bf16[8,2,3584]{2,1,0:T(2,128)(2,1)} %get-tuple-element.5), calls=%async_computation.2 | async-start | bytes 229376 | tf_op jit(solution)/shard_map/all_to_all | solution.py:27
  37.2 0.6 %dynamic_slice.3 = f32[2]{0:T(128)} dynamic-slice(f32[16]{0:T(128)S(1)} %add_subtract_fusion, s32[]{:T(128)S(6)} %select_n.8), dynamic_slice_sizes={2} | dynamic-slice | bytes 20 | tf_op jit(solution)/shard_map/dynamic_slice | solution.py:135
  37.8 0.0 collective-permute-done.1
  37.8 0.0 collective-permute-done
  37.8 2.4 %fusion = f32[3584,128]{1,0:T(8,128)} fusion(bf16[16,3584]{1,0:T(8,128)(2,1)S(1)} %collective-permute-done, bf16[16,3584]{1,0:T(8,128)(2,1)S(1)} %slice.54, bf16[16,128]{1,0:T(8,128)(2,1)S(1)} %collective-permute-done.1, bf16[16,128]{1,0:T(8,128)(2,1)} %copy-done.3), kind=kOutput, calls=%fused_computation | convolution fusion | flops 29835264 | bytes 2072576 | tf_op jit(solution)/shard_map/dot_general | solution.py:155
  40.2 4.2 %all-to-all-done.2.arrived_ref = bf16[8,2,3584]{2,1,0:T(2,128)(2,1)S(1)} async-done(((bf16[8,2,3584]{2,1,0:T(2,128)(2,1)}), bf16[8,2,3584]{2,1,0:T(2,128)(2,1)S(1)}, u32[]{:S(2)}, u32[]{:S(2)}) %all-to-all-start.2) | async-done | bytes 114720 | tf_op jit(solution)/shard_map/all_to_all | solution.py:27
  44.3 0.0 copy-start.2
  44.3 0.6 %copy-done.2 = bf16[8,2,3584]{2,1,0:T(2,128)(2,1)} copy-done((bf16[8,2,3584]{2,1,0:T(2,128)(2,1)}, bf16[8,2,3584]{2,1,0:T(2,128)(2,1)S(1)}, u32[]{:S(2)}) %copy-start.2) | copy-done | bytes 114712
  45.0 1.5 %shard_map.78 = f32[2,3584]{1,0:T(2,128)} custom-call(s32[1]{0:T(128)} %bitcast.12.here_ref, bf16[8,2,3584]{2,1,0:T(2,128)(2,1)} %copy-done.2, f32[2,3584]{1,0:T(2,128)} %get-tuple-element.6.own_ref), custom_call_target="tpu_custom_call" | custom-call | tf_op jit(solution)/shard_map/pallas_call | solution.py:149
  (12 shorter events, 0.2 us)
Async XLA Ops:
  0.6 18.4 %copy-start = (bf16[4608,128]{1,0:T(8,128)(2,1)S(1)}, bf16[4608,128]{1,0:T(8,128)(2,1)}, u32[]{:S(2)}) copy-start(bf16[4608,128]{1,0:T(8,128)(2,1)} %param.7) | copy-start | bytes 3538948
  0.6 18.0 %copy-start.1 = (bf16[3584,128]{1,0:T(8,128)(2,1)S(1)}, bf16[3584,128]{1,0:T(8,128)(2,1)}, u32[]{:S(2)}) copy-start(bf16[3584,128]{1,0:T(8,128)(2,1)} %head_ref.1) | copy-start | bytes 2752516
  2.3 16.3 %all-to-all-start = ((bf16[8,2,8320]{2,1,0:T(2,128)(2,1)}), bf16[8,2,8320]{2,1,0:T(2,128)(2,1)S(1)}, u32[]{:S(2)}, u32[]{:S(2)}) async-start(bf16[8,2,8320]{2,1,0:T(2,128)(2,1)} %shard_map.76), calls=%async_computation | async-start | bytes 532480 | tf_op jit(solution)/shard_map/all_to_all | solution.py:27
  20.5 10.3 %all-to-all-start.1 = ((f32[8,8,128]{2,1,0:T(8,128)}), f32[8,8,128]{2,1,0:T(8,128)S(1)}, u32[]{:S(2)}, u32[]{:S(2)}) async-start(f32[8,8,128]{2,1,0:T(8,128)} %broadcast_in_dim.9), calls=%async_computation.1 | async-start | bytes 65536 | tf_op jit(solution)/shard_map/all_to_all | solution.py:27
  24.1 13.7 %collective-permute-start = (bf16[16,3584]{1,0:T(8,128)(2,1)S(1)}, bf16[16,3584]{1,0:T(8,128)(2,1)S(1)}, u32[]{:S(2)}, u32[]{:S(2)}) collective-permute-start(bf16[16,3584]{1,0:T(8,128)(2,1)S(1)} %slice.54), channel_id=1, source_target_pairs={{0,1},{1,0},{2,3},{3,2},{4,5},{5,4},{6,7},{7,6},{8,9},{9,8},{10,11... | collective-permute-start | bytes 344072 | tf_op jit(solution)/shard_map/ppermute | solution.py:103
  31.0 0.6 %copy-start.3 = (bf16[16,128]{1,0:T(8,128)(2,1)}, bf16[16,128]{1,0:T(8,128)(2,1)S(1)}, u32[]{:S(2)}) copy-start(bf16[16,128]{1,0:T(8,128)(2,1)S(1)} %subtract_convert_fusion.grad_ref) | copy-start | bytes 12292
  31.0 6.8 %collective-permute-start.1 = (bf16[16,128]{1,0:T(8,128)(2,1)S(1)}, bf16[16,128]{1,0:T(8,128)(2,1)S(1)}, u32[]{:S(2)}, u32[]{:S(2)}) collective-permute-start(bf16[16,128]{1,0:T(8,128)(2,1)S(1)} %subtract_convert_fusion.grad_ref), channel_id=1, source_target_pairs={{0,1},{1,0},{2,3},{3,2},{4,5},{5,4},{6,7},{7,6},{8,9},{9,8},{10,11... | collective-permute-start | bytes 12296 | tf_op jit(solution)/shard_map/ppermute | solution.py:140
  33.8 10.5 %all-to-all-start.2 = ((bf16[8,2,3584]{2,1,0:T(2,128)(2,1)}), bf16[8,2,3584]{2,1,0:T(2,128)(2,1)S(1)}, u32[]{:S(2)}, u32[]{:S(2)}) async-start(bf16[8,2,3584]{2,1,0:T(2,128)(2,1)} %get-tuple-element.5), calls=%async_computation.2 | async-start | bytes 229376 | tf_op jit(solution)/shard_map/all_to_all | solution.py:27
  44.3 0.6 %copy-start.2 = (bf16[8,2,3584]{2,1,0:T(2,128)(2,1)}, bf16[8,2,3584]{2,1,0:T(2,128)(2,1)S(1)}, u32[]{:S(2)}) copy-start(bf16[8,2,3584]{2,1,0:T(2,128)(2,1)S(1)} %all-to-all-done.2.arrived_ref) | copy-start | bytes 344068

commit v5 on v4

--- a/solution.py
+++ b/solution.py
@@ -49,37 +49,14 @@
     over_shards(shards, write)
 
 
-def partial_kernel(here_ref, grad_ref, head_ref, out_ref, own_ref, total_ref):
-    shards, own, _ = out_ref.shape
-    total_ref[...] = lax.dot_general(
-        grad_ref[...], head_ref[...], (((1,), (1,)), ((), ())), preferred_element_type=F32
-    )
-
-    together = 8 // own
-
-    def write(group):
-        start = group * 8 if isinstance(group, int) else pl.multiple_of(group * 8, 8)
-        rows = total_ref[pl.ds(start, 8), :]
-        for place in range(together):
-            shard = group * together + place
-            block = rows[place * own : place * own + own]
-            out_ref[shard] = block.astype(BF16)
-
-            @pl.when(shard == here_ref[0])
-            def _():
-                own_ref[...] = block
-
-    over_shards(shards // together, write)
-
-
-def sum_kernel(here_ref, arrived_ref, own_ref, out_ref):
-    out_ref[...] = own_ref[...]
-
-    def add(shard):
-        block = arrived_ref[shard].astype(F32)
-        out_ref[...] += jnp.where(shard == here_ref[0], jnp.zeros_like(block), block)
-
-    over_shards(arrived_ref.shape[0], add)
+def gather_stats(block, shards):
+    held = block[None]
+    bit = 1
+    while bit < shards:
+        arrived = lax.ppermute(held, "vocab", [(i, i ^ bit) for i in range(shards)])
+        held = jnp.concatenate([held, arrived], axis=0)
+        bit *= 2
+    return held
 
 
 def on_device(teacher_hidden, student_hidden, teacher_head, student_head, labels, *, shards):
@@ -122,7 +99,7 @@
     )
     lanes = -(-shards * own // 128) * 128
     stats = jnp.pad(stats, ((0, 2), (0, lanes - shards * own)))
-    every = swap(jnp.broadcast_to(stats[None], (shards,) + stats.shape))[:, :, : shards * own]
+    every = gather_stats(stats, shards)[:, :, : shards * own]
     all_top_t = jnp.max(every[:, 0], axis=0)
     factor_t = jnp.exp(every[:, 0] - all_top_t[None])
     all_top_s = jnp.max(every[:, 3], axis=0)
@@ -138,20 +115,12 @@
     student_prob = jnp.exp(student_logits - all_top_s[:, None]) / mass_s[:, None]
     grad_rows = (2.0 * student_prob - teacher_prob - target.astype(F32)).astype(BF16)
     grad_other = lax.ppermute(grad_rows, "rows", other)
-    block = (shards, own, student_width)
-    partials, own_partial = pl.pallas_call(
-        partial_kernel,
-        out_shape=(jax.ShapeDtypeStruct(block, BF16), jax.ShapeDtypeStruct(block[1:], F32)),
-        in_specs=[SMEM, VMEM, VMEM],
-        out_specs=(VMEM, VMEM),
-        scratch_shapes=[pltpu.VMEM((shards * own, student_width), F32)],
-    )(here, grad_rows, student_head)
-    hidden_grad = pl.pallas_call(
-        sum_kernel,
-        out_shape=jax.ShapeDtypeStruct(block[1:], F32),
-        in_specs=[SMEM, VMEM, VMEM],
-        out_specs=VMEM,
-    )(here, swap(partials), own_partial)
+    partial = lax.dot_general(grad_rows, student_head, (((1,), (1,)), ((), ())), preferred_element_type=F32)
+    arrived = swap(partial.astype(BF16).reshape(shards, own, student_width)).astype(F32)
+    own_grad = lax.dynamic_slice_in_dim(grad_rows, here[0] * own, own, 0)
+    own_partial = lax.dot_general(own_grad, student_head, (((1,), (1,)), ((), ())), preferred_element_type=F32)
+    others = lax.broadcasted_iota(jnp.int32, (shards, 1, 1), 0) != here[0]
+    hidden_grad = own_partial + jnp.sum(jnp.where(others, arrived, 0.0), axis=0)
     head_grad = lax.dot_general(
         jnp.concatenate([student_rows, student_other], axis=0),
         jnp.concatenate([grad_rows, grad_other], axis=0),

time: 47 us -> 45.7 us (0.972)
  Pallas kernels: 5.41 us -> 1.57 us
  waiting for transfers between devices: 19.8 us -> 22.4 us
  local copies, waits for them, and re-layouts: 2.64 us -> 1.58 us
  matrix products: 3.09 us -> 3.7 us
    ppermute x0 -> x3, waiting for transfers between devices: none -> 8.27 us  [gather_stats(): arrived = lax.ppermute(held, 'vocab', [(i, i ^ bit) for i in range(shards)])]
    all_to_all x3 -> x2, waiting for transfers between devices: 19.8 us -> 14.1 us  [swap(): lax.all_to_all(blocks, 'vocab', split_axis=0, concat_axis=0, tiled=True)]
    pallas_call x2 -> x0, Pallas kernels: 3.79 us -> none  [the longest x1 2.25 us: on_device(): pl.pallas_call(partial_kernel, out_shape=(jax.ShapeDtypeStruct(block, BF1...]
    ppermute x0 -> x3, starting transfers between devices: none -> 3.6 us  [gather_stats(): arrived = lax.ppermute(held, 'vocab', [(i, i ^ bit) for i in range(shards)])]
    all_to_all x3 -> x2, starting transfers between devices: 14.2 us -> 11 us  [swap(): lax.all_to_all(blocks, 'vocab', split_axis=0, concat_axis=0, tiled=True)]
    dot_general x0 -> x2, matrix products: none -> 1.3 us  [the longest x1 0.96 us: on_device(): lax.dot_general(own_grad, student_head, (((1,), (1,)), ((), ())), preferr...]
    unnamed x9 -> x5, local copies, waits for them, and re-layouts: 1.28 us -> 0.14 us
    reshape x0 -> x1, local copies, waits for them, and re-layouts: none -> 0.71 us  [on_device(): partial.astype(BF16).reshape(shards, own, student_width)]
  transfers between devices with their start and end apart: 5 -> 7, of which waited for: 3 -> 5; matrix products, arithmetic and copies ran while one was open for 7% -> 8% of each run, Pallas kernels for 5% -> 0%
where the time goes in v5:
time: 45.7 us; the launch traced here: 45.3 us
  waiting for transfers between devices  22.4 us (49%)
  starting transfers between devices  14.7 us (32%)
  matrix products  3.7 us (8%)
  local copies, waits for them, and re-layouts  1.58 us (3%)
  Pallas kernels  1.57 us (3%)
  between operations  0.73 us (2%)
  other arithmetic  0.66 us (1%)
    all_to_all x2, waiting for transfers between devices, swap(): lax.all_to_all(blocks, 'vocab', split_axis=0, concat_axis=0, tiled=True)  14.1 us
    all_to_all x2, starting transfers between devices, swap(): lax.all_to_all(blocks, 'vocab', split_axis=0, concat_axis=0, tiled=True)  11 us
    ppermute x3, waiting for transfers between devices, gather_stats(): arrived = lax.ppermute(held, 'vocab', [(i, i ^ bit) for i in range(shards)])  8.27 us
    ppermute x3, starting transfers between devices, gather_stats(): arrived = lax.ppermute(held, 'vocab', [(i, i ^ bit) for i in range(shards)])  3.6 us
    dot_general x1, matrix products, on_device(): lax.dot_general(jnp.concatenate([student_rows, student_other], axis=0), j...  1.69 us
    pallas_call x1, Pallas kernels, on_device(): pl.pallas_call(payload_kernel, out_shape=jax.ShapeDtypeStruct((shards, ow...  1.57 us
    dot_general x1, matrix products, on_device(): lax.dot_general(own_grad, student_head, (((1,), (1,)), ((), ())), preferr...  0.96 us
  transfers between devices with their start and end apart: 7, of which 5 were waited for; matrix products, arithmetic and copies ran while one was open for 8% of the time, Pallas kernels for 0%

profile of v5, /device:TPU:0, one launch (start us, length us, event | category | flops | bytes accessed | tf_op | source)
XLA Modules:
  0.0 45.3 jit_solution(10249737534974728477)
XLA Ops:
  0.6 0.0 copy-start
  0.6 1.6 %shard_map.76 = bf16[8,2,8320]{2,1,0:T(2,128)(2,1)} custom-call(s32[2]{0:T(128)} %labels_ref.1, bf16[2,4608]{1,0:T(2,128)(2,1)} %teacher_ref.1, bf16[2,3584]{1,0:T(2,128)(2,1)} %student_ref.1), custom_call_target="tpu_custom_call" | custom-call | tf_op jit(solution)/shard_map/pallas_call | solution.py:68
  2.2 0.0 copy-start.1
  2.2 7.4 %all-to-all-start = ((bf16[8,2,8320]{2,1,0:T(2,128)(2,1)}), bf16[8,2,8320]{2,1,0:T(2,128)(2,1)S(1)}, u32[]{:S(2)}, u32[]{:S(2)}) async-start(bf16[8,2,8320]{2,1,0:T(2,128)(2,1)} %shard_map.76), calls=%async_computation | async-start | bytes 532480 | tf_op jit(solution)/shard_map/all_to_all | solution.py:27
  9.6 9.0 %all-to-all-done = bf16[8,2,8320]{2,1,0:T(2,128)(2,1)S(1)} async-done(((bf16[8,2,8320]{2,1,0:T(2,128)(2,1)}), bf16[8,2,8320]{2,1,0:T(2,128)(2,1)S(1)}, u32[]{:S(2)}, u32[]{:S(2)}) %all-to-all-start) | async-done | bytes 266272 | tf_op jit(solution)/shard_map/all_to_all | solution.py:27
  18.6 0.1 reshape.25
  18.7 0.1 copy.9
  18.9 0.0 copy-done
  18.9 0.4 fusion.20
  19.3 0.0 copy-done.1
  19.3 0.3 fusion.21
  19.6 0.2 select_reduce_fusion.1
  19.9 1.5 %collective-permute-start = (f32[1,8,128]{2,1,0:T(8,128)S(1)}, f32[1,8,128]{2,1,0:T(8,128)S(1)}, u32[]{:S(2)}, u32[]{:S(2)}) collective-permute-start(f32[1,8,128]{2,1,0:T(8,128)S(1)} %pad_bitcast_fusion), channel_id=1, source_target_pairs={{0,2},{2,0},{4,6},{6,4},{8,10},{10,8},{12,14},{14,12},{1,3},{3,1},... | collective-permute-start | bytes 12296 | tf_op jit(solution)/shard_map/ppermute | solution.py:56
  21.4 2.2 %collective-permute-done = f32[1,8,128]{2,1,0:T(8,128)S(1)} collective-permute-done((f32[1,8,128]{2,1,0:T(8,128)S(1)}, f32[1,8,128]{2,1,0:T(8,128)S(1)}, u32[]{:S(2)}, u32[]{:S(2)}) %collective-permute-start) | collective-permute-done | bytes 4128 | tf_op jit(solution)/shard_map/ppermute | solution.py:56
  23.6 1.1 %collective-permute-start.1 = (f32[2,8,128]{2,1,0:T(8,128)S(1)}, f32[2,8,128]{2,1,0:T(8,128)S(1)}, u32[]{:S(2)}, u32[]{:S(2)}) collective-permute-start(f32[2,8,128]{2,1,0:T(8,128)S(1)} %pad_maximum_fusion.1), channel_id=1, source_target_pairs={{0,4},{2,6},{4,0},{6,2},{8,12},{10,14},{12,8},{14,10},{1,5},{3,7},... | collective-permute-start | bytes 24584 | tf_op jit(solution)/shard_map/ppermute | solution.py:56
  24.6 2.6 %collective-permute-done.1 = f32[2,8,128]{2,1,0:T(8,128)S(1)} collective-permute-done((f32[2,8,128]{2,1,0:T(8,128)S(1)}, f32[2,8,128]{2,1,0:T(8,128)S(1)}, u32[]{:S(2)}, u32[]{:S(2)}) %collective-permute-start.1) | collective-permute-done | bytes 8224 | tf_op jit(solution)/shard_map/ppermute | solution.py:56
  27.2 1.1 %collective-permute-start.2 = (f32[4,8,128]{2,1,0:T(8,128)S(1)}, f32[4,8,128]{2,1,0:T(8,128)S(1)}, u32[]{:S(2)}, u32[]{:S(2)}) collective-permute-start(f32[4,8,128]{2,1,0:T(8,128)S(1)} %pad_maximum_fusion), channel_id=1, source_target_pairs={{0,8},{2,10},{4,12},{6,14},{8,0},{10,2},{12,4},{14,6},{1,9},{3,11}... | collective-permute-start | bytes 49160 | tf_op jit(solution)/shard_map/ppermute | solution.py:56
  28.3 0.1 collective-permute-start.3
  28.4 3.5 %collective-permute-done.2 = f32[4,8,128]{2,1,0:T(8,128)S(1)} collective-permute-done((f32[4,8,128]{2,1,0:T(8,128)S(1)}, f32[4,8,128]{2,1,0:T(8,128)S(1)}, u32[]{:S(2)}, u32[]{:S(2)}) %collective-permute-start.2) | collective-permute-done | bytes 16416 | tf_op jit(solution)/shard_map/ppermute | solution.py:56
  32.0 0.1 subtract_convert_fusion
  32.1 0.1 collective-permute-start.4
  32.1 0.3 convolution_convert_fusion
  32.5 0.7 %reshape.26 = bf16[8,2,3584]{2,1,0:T(2,128)(2,1)} reshape(bf16[16,3584]{1,0:T(8,128)(2,1)S(1)} %convolution_convert_fusion) | data formatting | bytes 229376 | tf_op jit(solution)/shard_map/reshape | solution.py:119
  33.2 3.6 %all-to-all-start.1 = ((bf16[8,2,3584]{2,1,0:T(2,128)(2,1)}), bf16[8,2,3584]{2,1,0:T(2,128)(2,1)S(1)}, u32[]{:S(2)}, u32[]{:S(2)}) async-start(bf16[8,2,3584]{2,1,0:T(2,128)(2,1)} %reshape.26), calls=%async_computation.1 | async-start | bytes 229376 | tf_op jit(solution)/shard_map/all_to_all | solution.py:27
  36.8 0.6 %dynamic_slice.6 = f32[2]{0:T(128)} dynamic-slice(f32[16]{0:T(128)S(1)} %add_subtract_fusion, s32[]{:T(128)S(6)} %select_n.13), dynamic_slice_sizes={2} | dynamic-slice | bytes 20 | tf_op jit(solution)/shard_map/dynamic_slice | solution.py:112
  37.4 0.0 collective-permute-done.4
  37.4 0.0 collective-permute-done.3
  37.4 1.7 %fusion = f32[3584,128]{1,0:T(8,128)} fusion(bf16[16,3584]{1,0:T(8,128)(2,1)S(1)} %collective-permute-done.3, bf16[16,3584]{1,0:T(8,128)(2,1)S(1)} %slice.54, bf16[16,128]{1,0:T(8,128)(2,1)S(1)} %collective-permute-done.4, bf16[16,128]{1,0:T(8,128)(2,1)S(1)} %subtract_convert_fusion), kind=kOutput, calls=%fused_computation.2 | convolution fusion | flops 29835264 | bytes 2072576 | tf_op jit(solution)/shard_map/dot_general | solution.py:124
  39.1 5.1 %all-to-all-done.1 = bf16[8,2,3584]{2,1,0:T(2,128)(2,1)S(1)} async-done(((bf16[8,2,3584]{2,1,0:T(2,128)(2,1)}), bf16[8,2,3584]{2,1,0:T(2,128)(2,1)S(1)}, u32[]{:S(2)}, u32[]{:S(2)}) %all-to-all-start.1) | async-done | bytes 114720 | tf_op jit(solution)/shard_map/all_to_all | solution.py:27
  44.2 0.2 select_reduce_fusion
  44.4 1.0 %convolution_add_fusion = f32[2,3584]{1,0:T(2,128)} fusion(f32[2,3584]{1,0:T(2,128)S(1)} %select_reduce_fusion, bf16[3584,128]{1,0:T(8,128)(2,1)S(1)} %copy-done.1, bf16[16,128]{1,0:T(8,128)(2,1)S(1)} %subtract_convert_fusion, s32[]{:T(128)S(6)} %select_n.13), kind=kOutput, calls=%fused_computation.1 | convolution fusion | flops 1842176 | bytes 975364 | tf_op jit(solution)/shard_map/dot_general | solution.py:121
  (14 shorter events, 0.2 us)
Async XLA Ops:
  0.6 18.2 %copy-start = (bf16[4608,128]{1,0:T(8,128)(2,1)S(1)}, bf16[4608,128]{1,0:T(8,128)(2,1)}, u32[]{:S(2)}) copy-start(bf16[4608,128]{1,0:T(8,128)(2,1)} %param.7) | copy-start | bytes 3538948
  2.2 17.0 %copy-start.1 = (bf16[3584,128]{1,0:T(8,128)(2,1)S(1)}, bf16[3584,128]{1,0:T(8,128)(2,1)}, u32[]{:S(2)}) copy-start(bf16[3584,128]{1,0:T(8,128)(2,1)} %param.8) | copy-start | bytes 2752516
  2.2 16.4 %all-to-all-start = ((bf16[8,2,8320]{2,1,0:T(2,128)(2,1)}), bf16[8,2,8320]{2,1,0:T(2,128)(2,1)S(1)}, u32[]{:S(2)}, u32[]{:S(2)}) async-start(bf16[8,2,8320]{2,1,0:T(2,128)(2,1)} %shard_map.76), calls=%async_computation | async-start | bytes 532480 | tf_op jit(solution)/shard_map/all_to_all | solution.py:27
  19.9 3.7 %collective-permute-start = (f32[1,8,128]{2,1,0:T(8,128)S(1)}, f32[1,8,128]{2,1,0:T(8,128)S(1)}, u32[]{:S(2)}, u32[]{:S(2)}) collective-permute-start(f32[1,8,128]{2,1,0:T(8,128)S(1)} %pad_bitcast_fusion), channel_id=1, source_target_pairs={{0,2},{2,0},{4,6},{6,4},{8,10},{10,8},{12,14},{14,12},{1,3},{3,1},... | collective-permute-start | bytes 12296 | tf_op jit(solution)/shard_map/ppermute | solution.py:56
  23.6 3.7 %collective-permute-start.1 = (f32[2,8,128]{2,1,0:T(8,128)S(1)}, f32[2,8,128]{2,1,0:T(8,128)S(1)}, u32[]{:S(2)}, u32[]{:S(2)}) collective-permute-start(f32[2,8,128]{2,1,0:T(8,128)S(1)} %pad_maximum_fusion.1), channel_id=1, source_target_pairs={{0,4},{2,6},{4,0},{6,2},{8,12},{10,14},{12,8},{14,10},{1,5},{3,7},... | collective-permute-start | bytes 24584 | tf_op jit(solution)/shard_map/ppermute | solution.py:56
  27.2 4.6 %collective-permute-start.2 = (f32[4,8,128]{2,1,0:T(8,128)S(1)}, f32[4,8,128]{2,1,0:T(8,128)S(1)}, u32[]{:S(2)}, u32[]{:S(2)}) collective-permute-start(f32[4,8,128]{2,1,0:T(8,128)S(1)} %pad_maximum_fusion), channel_id=1, source_target_pairs={{0,8},{2,10},{4,12},{6,14},{8,0},{10,2},{12,4},{14,6},{1,9},{3,11}... | collective-permute-start | bytes 49160 | tf_op jit(solution)/shard_map/ppermute | solution.py:56
  28.3 9.1 %collective-permute-start.3 = (bf16[16,3584]{1,0:T(8,128)(2,1)S(1)}, bf16[16,3584]{1,0:T(8,128)(2,1)S(1)}, u32[]{:S(2)}, u32[]{:S(2)}) collective-permute-start(bf16[16,3584]{1,0:T(8,128)(2,1)S(1)} %slice.54), channel_id=1, source_target_pairs={{0,1},{1,0},{2,3},{3,2},{4,5},{5,4},{6,7},{7,6},{8,9},{9,8},{10,11... | collective-permute-start | bytes 344072 | tf_op jit(solution)/shard_map/ppermute | solution.py:80
  32.1 5.3 %collective-permute-start.4 = (bf16[16,128]{1,0:T(8,128)(2,1)S(1)}, bf16[16,128]{1,0:T(8,128)(2,1)S(1)}, u32[]{:S(2)}, u32[]{:S(2)}) collective-permute-start(bf16[16,128]{1,0:T(8,128)(2,1)S(1)} %subtract_convert_fusion), channel_id=1, source_target_pairs={{0,1},{1,0},{2,3},{3,2},{4,5},{5,4},{6,7},{7,6},{8,9},{9,8},{10,11... | collective-permute-start | bytes 12296 | tf_op jit(solution)/shard_map/ppermute | solution.py:117
  33.2 11.0 %all-to-all-start.1 = ((bf16[8,2,3584]{2,1,0:T(2,128)(2,1)}), bf16[8,2,3584]{2,1,0:T(2,128)(2,1)S(1)}, u32[]{:S(2)}, u32[]{:S(2)}) async-start(bf16[8,2,3584]{2,1,0:T(2,128)(2,1)} %reshape.26), calls=%async_computation.1 | async-start | bytes 229376 | tf_op jit(solution)/shard_map/all_to_all | solution.py:27

commit v6 on v5

--- a/solution.py
+++ b/solution.py
@@ -49,16 +49,6 @@
     over_shards(shards, write)
 
 
-def gather_stats(block, shards):
-    held = block[None]
-    bit = 1
-    while bit < shards:
-        arrived = lax.ppermute(held, "vocab", [(i, i ^ bit) for i in range(shards)])
-        held = jnp.concatenate([held, arrived], axis=0)
-        bit *= 2
-    return held
-
-
 def on_device(teacher_hidden, student_hidden, teacher_head, student_head, labels, *, shards):
     own, teacher_width = teacher_hidden.shape
     student_width = student_hidden.shape[1]
@@ -87,27 +77,26 @@
     exp_t = jnp.exp(teacher_logits - top_t)
     top_s = jnp.max(student_logits, axis=1, keepdims=True)
     exp_s = jnp.exp(student_logits - top_s)
-    stats = jnp.stack(
+    stats = jnp.concatenate(
         [
-            top_t[:, 0],
-            jnp.sum(exp_t, axis=1),
-            jnp.sum(exp_t * (teacher_logits - student_logits), axis=1),
-            top_s[:, 0],
-            jnp.sum(exp_s, axis=1),
-            jnp.sum(jnp.where(target, student_logits, 0.0), axis=1),
-        ]
+            top_t,
+            jnp.sum(exp_t, axis=1, keepdims=True),
+            jnp.sum(exp_t * (teacher_logits - student_logits), axis=1, keepdims=True),
+            top_s,
+            jnp.sum(exp_s, axis=1, keepdims=True),
+            jnp.sum(jnp.where(target, student_logits, 0.0), axis=1, keepdims=True),
+        ],
+        axis=1,
     )
-    lanes = -(-shards * own // 128) * 128
-    stats = jnp.pad(stats, ((0, 2), (0, lanes - shards * own)))
-    every = gather_stats(stats, shards)[:, :, : shards * own]
-    all_top_t = jnp.max(every[:, 0], axis=0)
-    factor_t = jnp.exp(every[:, 0] - all_top_t[None])
-    all_top_s = jnp.max(every[:, 3], axis=0)
-    factor_s = jnp.exp(every[:, 3] - all_top_s[None])
-    mass_t = jnp.sum(every[:, 1] * factor_t, axis=0)
-    cross = jnp.sum(every[:, 2] * factor_t, axis=0)
-    mass_s = jnp.sum(every[:, 4] * factor_s, axis=0)
-    picked = jnp.sum(every[:, 5], axis=0)
+    every = swap(jnp.broadcast_to(stats[None], (shards,) + stats.shape))
+    all_top_t = jnp.max(every[:, :, 0], axis=0)
+    factor_t = jnp.exp(every[:, :, 0] - all_top_t[None])
+    all_top_s = jnp.max(every[:, :, 3], axis=0)
+    factor_s = jnp.exp(every[:, :, 3] - all_top_s[None])
+    mass_t = jnp.sum(every[:, :, 1] * factor_t, axis=0)
+    cross = jnp.sum(every[:, :, 2] * factor_t, axis=0)
+    mass_s = jnp.sum(every[:, :, 4] * factor_s, axis=0)
+    picked = jnp.sum(every[:, :, 5], axis=0)
     loss = cross / mass_t - all_top_t - jnp.log(mass_t) + 2.0 * (all_top_s + jnp.log(mass_s)) - picked
     token_loss = lax.dynamic_slice_in_dim(loss, lax.axis_index("vocab") * own, own, 0)
 
@@ -116,11 +105,8 @@
     grad_rows = (2.0 * student_prob - teacher_prob - target.astype(F32)).astype(BF16)
     grad_other = lax.ppermute(grad_rows, "rows", other)
     partial = lax.dot_general(grad_rows, student_head, (((1,), (1,)), ((), ())), preferred_element_type=F32)
-    arrived = swap(partial.astype(BF16).reshape(shards, own, student_width)).astype(F32)
-    own_grad = lax.dynamic_slice_in_dim(grad_rows, here[0] * own, own, 0)
-    own_partial = lax.dot_general(own_grad, student_head, (((1,), (1,)), ((), ())), preferred_element_type=F32)
-    others = lax.broadcasted_iota(jnp.int32, (shards, 1, 1), 0) != here[0]
-    hidden_grad = own_partial + jnp.sum(jnp.where(others, arrived, 0.0), axis=0)
+    arrived = swap(partial.astype(BF16).reshape(shards, own, student_width))
+    hidden_grad = jnp.sum(arrived.astype(F32), axis=0)
     head_grad = lax.dot_general(
         jnp.concatenate([student_rows, student_other], axis=0),
         jnp.concatenate([grad_rows, grad_other], axis=0),

time: 45.7 us -> 44.3 us (0.969)
  waiting for transfers between devices: 22.4 us -> 20.9 us
  matrix products: 3.7 us -> 2.73 us
  local copies, waits for them, and re-layouts: 1.58 us -> 2.19 us
  other arithmetic: 0.66 us -> 1.18 us
    ppermute x3 -> x0, waiting for transfers between devices: 8.27 us -> none  [gather_stats(): arrived = lax.ppermute(held, 'vocab', [(i, i ^ bit) for i in range(shards)])]
    all_to_all x2 -> x3, waiting for transfers between devices: 14.1 us -> 20.9 us  [swap(): lax.all_to_all(blocks, 'vocab', split_axis=0, concat_axis=0, tiled=True)]
    ppermute x3 -> x0, starting transfers between devices: 3.6 us -> none  [gather_stats(): arrived = lax.ppermute(held, 'vocab', [(i, i ^ bit) for i in range(shards)])]
    all_to_all x2 -> x3, starting transfers between devices: 11 us -> 14.3 us  [swap(): lax.all_to_all(blocks, 'vocab', split_axis=0, concat_axis=0, tiled=True)]
    dot_general x1 -> x0, matrix products: 0.96 us -> none  [on_device(): lax.dot_general(own_grad, student_head, (((1,), (1,)), ((), ())), preferr...]
    broadcast_in_dim x1, local copies, waits for them, and re-layouts: 0.01 us -> 0.63 us  [on_device(): every = swap(jnp.broadcast_to(stats[None], (shards,) + stats.shape))]
    reduce_sum x4, other arithmetic: 0.47 us -> 0.99 us  [the longest x1 0.71 us: on_device(): hidden_grad = jnp.sum(arrived.astype(F32), axis=0)]
  transfers between devices with their start and end apart: 7 -> 5, of which waited for: 5 -> 3; matrix products, arithmetic and copies ran while one was open for 8% -> 8% of each run, Pallas kernels for 0% -> 0%
where the time goes in v6:
time: 44.3 us; the launch traced here: 43.8 us
  waiting for transfers between devices  20.9 us (47%)
  starting transfers between devices  14.5 us (33%)
  matrix products  2.73 us (6%)
  local copies, waits for them, and re-layouts  2.19 us (5%)
  Pallas kernels  1.57 us (4%)
  other arithmetic  1.18 us (3%)
  between operations  0.74 us (2%)
    all_to_all x3, waiting for transfers between devices, swap(): lax.all_to_all(blocks, 'vocab', split_axis=0, concat_axis=0, tiled=True)  20.9 us
    all_to_all x3, starting transfers between devices, swap(): lax.all_to_all(blocks, 'vocab', split_axis=0, concat_axis=0, tiled=True)  14.3 us
    dot_general x1, matrix products, on_device(): lax.dot_general(jnp.concatenate([student_rows, student_other], axis=0), j...  1.69 us
    pallas_call x1, Pallas kernels, on_device(): pl.pallas_call(payload_kernel, out_shape=jax.ShapeDtypeStruct((shards, ow...  1.57 us
  transfers between devices with their start and end apart: 5, of which 3 were waited for; matrix products, arithmetic and copies ran while one was open for 8% of the time, Pallas kernels for 0%

profile of v6, /device:TPU:0, one launch (start us, length us, event | category | flops | bytes accessed | tf_op | source)
XLA Modules:
  0.0 43.8 jit_solution(15233386383238690830)
XLA Ops:
  0.6 0.0 copy-start
  0.6 1.6 %shard_map.76 = bf16[8,2,8320]{2,1,0:T(2,128)(2,1)} custom-call(s32[2]{0:T(128)} %labels_ref.1, bf16[2,4608]{1,0:T(2,128)(2,1)} %teacher_ref.1, bf16[2,3584]{1,0:T(2,128)(2,1)} %student_ref.1), custom_call_target="tpu_custom_call" | custom-call | tf_op jit(solution)/shard_map/pallas_call | solution.py:58
  2.2 0.0 copy-start.1
  2.2 7.4 %all-to-all-start = ((bf16[8,2,8320]{2,1,0:T(2,128)(2,1)}), bf16[8,2,8320]{2,1,0:T(2,128)(2,1)S(1)}, u32[]{:S(2)}, u32[]{:S(2)}) async-start(bf16[8,2,8320]{2,1,0:T(2,128)(2,1)} %shard_map.76), calls=%async_computation | async-start | bytes 532480 | tf_op jit(solution)/shard_map/all_to_all | solution.py:27
  9.6 9.0 %all-to-all-done = bf16[8,2,8320]{2,1,0:T(2,128)(2,1)S(1)} async-done(((bf16[8,2,8320]{2,1,0:T(2,128)(2,1)}), bf16[8,2,8320]{2,1,0:T(2,128)(2,1)S(1)}, u32[]{:S(2)}, u32[]{:S(2)}) %all-to-all-start) | async-done | bytes 266272 | tf_op jit(solution)/shard_map/all_to_all | solution.py:27
  18.6 0.1 reshape.21
  18.7 0.1 copy.15
  18.9 0.0 copy-done
  18.9 0.4 fusion.16
  19.3 0.0 copy-done.1
  19.3 0.3 fusion.17
  19.6 0.2 select_reduce_fusion
  19.9 0.6 %broadcast_in_dim.42 = f32[8,16,6]{1,2,0:T(8,128)} broadcast(f32[16,6]{0,1:T(8,128)S(1)} %concatenate.9), dimensions={1,2} | broadcast | bytes 3456 | tf_op jit(solution)/shard_map/broadcast_in_dim | solution.py:91
  20.5 3.6 %all-to-all-start.1 = ((f32[8,16,6]{1,2,0:T(8,128)}), f32[8,16,6]{1,2,0:T(8,128)S(1)}, u32[]{:S(2)}, u32[]{:S(2)}) async-start(f32[8,16,6]{1,2,0:T(8,128)} %broadcast_in_dim.42), calls=%async_computation.1 | async-start | bytes 65536 | tf_op jit(solution)/shard_map/all_to_all | solution.py:27
  24.1 0.1 collective-permute-start
  24.2 6.6 %all-to-all-done.1 = f32[8,16,6]{1,2,0:T(8,128)S(1)} async-done(((f32[8,16,6]{1,2,0:T(8,128)}), f32[8,16,6]{1,2,0:T(8,128)S(1)}, u32[]{:S(2)}, u32[]{:S(2)}) %all-to-all-start.1) | async-done | bytes 3104 | tf_op jit(solution)/shard_map/all_to_all | solution.py:27
  30.9 0.1 subtract_convert_fusion
  31.0 0.1 collective-permute-start.1
  31.1 0.3 convolution_convert_fusion
  31.4 0.7 %reshape.22 = bf16[8,2,3584]{2,1,0:T(2,128)(2,1)} reshape(bf16[16,3584]{1,0:T(8,128)(2,1)S(1)} %convolution_convert_fusion) | data formatting | bytes 229376 | tf_op jit(solution)/shard_map/reshape | solution.py:108
  32.1 3.4 %all-to-all-start.2 = ((bf16[8,2,3584]{2,1,0:T(2,128)(2,1)}), bf16[8,2,3584]{2,1,0:T(2,128)(2,1)S(1)}, u32[]{:S(2)}, u32[]{:S(2)}) async-start(bf16[8,2,3584]{2,1,0:T(2,128)(2,1)} %reshape.22), calls=%async_computation.2 | async-start | bytes 229376 | tf_op jit(solution)/shard_map/all_to_all | solution.py:27
  35.5 0.6 %dynamic_slice.3 = f32[2]{0:T(128)} dynamic-slice(f32[16]{0:T(128)S(1)} %add_subtract_fusion, s32[]{:T(128)S(6)} %select_n.8), dynamic_slice_sizes={2} | dynamic-slice | bytes 20 | tf_op jit(solution)/shard_map/dynamic_slice | solution.py:101
  36.1 0.0 collective-permute-done.1
  36.1 0.0 collective-permute-done
  36.1 1.7 %fusion = f32[3584,128]{1,0:T(8,128)} fusion(bf16[16,3584]{1,0:T(8,128)(2,1)S(1)} %collective-permute-done, bf16[16,3584]{1,0:T(8,128)(2,1)S(1)} %slice.47, bf16[16,128]{1,0:T(8,128)(2,1)S(1)} %collective-permute-done.1, bf16[16,128]{1,0:T(8,128)(2,1)S(1)} %subtract_convert_fusion), kind=kOutput, calls=%fused_computation.1 | convolution fusion | flops 29835264 | bytes 2072576 | tf_op jit(solution)/shard_map/dot_general | solution.py:110
  37.8 5.3 %all-to-all-done.2 = bf16[8,2,3584]{2,1,0:T(2,128)(2,1)S(1)} async-done(((bf16[8,2,3584]{2,1,0:T(2,128)(2,1)}), bf16[8,2,3584]{2,1,0:T(2,128)(2,1)S(1)}, u32[]{:S(2)}, u32[]{:S(2)}) %all-to-all-start.2) | async-done | bytes 114720 | tf_op jit(solution)/shard_map/all_to_all | solution.py:27
  43.1 0.7 %convert_reduce_fusion = f32[2,3584]{1,0:T(2,128)} fusion(bf16[8,2,3584]{2,1,0:T(2,128)(2,1)S(1)} %all-to-all-done.2), kind=kLoop, calls=%fused_computation.5 | loop fusion | flops 107520 | bytes 143360 | tf_op jit(solution)/shard_map/reduce_sum | solution.py:109
  (11 shorter events, 0.2 us)
Async XLA Ops:
  0.6 18.2 %copy-start = (bf16[4608,128]{1,0:T(8,128)(2,1)S(1)}, bf16[4608,128]{1,0:T(8,128)(2,1)}, u32[]{:S(2)}) copy-start(bf16[4608,128]{1,0:T(8,128)(2,1)} %param.7) | copy-start | bytes 3538948
  2.2 17.0 %copy-start.1 = (bf16[3584,128]{1,0:T(8,128)(2,1)S(1)}, bf16[3584,128]{1,0:T(8,128)(2,1)}, u32[]{:S(2)}) copy-start(bf16[3584,128]{1,0:T(8,128)(2,1)} %param.8) | copy-start | bytes 2752516
  2.2 16.4 %all-to-all-start = ((bf16[8,2,8320]{2,1,0:T(2,128)(2,1)}), bf16[8,2,8320]{2,1,0:T(2,128)(2,1)S(1)}, u32[]{:S(2)}, u32[]{:S(2)}) async-start(bf16[8,2,8320]{2,1,0:T(2,128)(2,1)} %shard_map.76), calls=%async_computation | async-start | bytes 532480 | tf_op jit(solution)/shard_map/all_to_all | solution.py:27
  20.5 10.3 %all-to-all-start.1 = ((f32[8,16,6]{1,2,0:T(8,128)}), f32[8,16,6]{1,2,0:T(8,128)S(1)}, u32[]{:S(2)}, u32[]{:S(2)}) async-start(f32[8,16,6]{1,2,0:T(8,128)} %broadcast_in_dim.42), calls=%async_computation.1 | async-start | bytes 65536 | tf_op jit(solution)/shard_map/all_to_all | solution.py:27
  24.1 12.0 %collective-permute-start = (bf16[16,3584]{1,0:T(8,128)(2,1)S(1)}, bf16[16,3584]{1,0:T(8,128)(2,1)S(1)}, u32[]{:S(2)}, u32[]{:S(2)}) collective-permute-start(bf16[16,3584]{1,0:T(8,128)(2,1)S(1)} %slice.47), channel_id=1, source_target_pairs={{0,1},{1,0},{2,3},{3,2},{4,5},{5,4},{6,7},{7,6},{8,9},{9,8},{10,11... | collective-permute-start | bytes 344072 | tf_op jit(solution)/shard_map/ppermute | solution.py:70
  31.0 5.1 %collective-permute-start.1 = (bf16[16,128]{1,0:T(8,128)(2,1)S(1)}, bf16[16,128]{1,0:T(8,128)(2,1)S(1)}, u32[]{:S(2)}, u32[]{:S(2)}) collective-permute-start(bf16[16,128]{1,0:T(8,128)(2,1)S(1)} %subtract_convert_fusion), channel_id=1, source_target_pairs={{0,1},{1,0},{2,3},{3,2},{4,5},{5,4},{6,7},{7,6},{8,9},{9,8},{10,11... | collective-permute-start | bytes 12296 | tf_op jit(solution)/shard_map/ppermute | solution.py:106
  32.1 11.0 %all-to-all-start.2 = ((bf16[8,2,3584]{2,1,0:T(2,128)(2,1)}), bf16[8,2,3584]{2,1,0:T(2,128)(2,1)S(1)}, u32[]{:S(2)}, u32[]{:S(2)}) async-start(bf16[8,2,3584]{2,1,0:T(2,128)(2,1)} %reshape.22), calls=%async_computation.2 | async-start | bytes 229376 | tf_op jit(solution)/shard_map/all_to_all | solution.py:27

commit v7 on v6

--- a/solution.py
+++ b/solution.py
@@ -49,12 +49,9 @@
     over_shards(shards, write)
 
 
-def on_device(teacher_hidden, student_hidden, teacher_head, student_head, labels, *, shards):
+def gather_tokens(teacher_hidden, student_hidden, labels, shards):
     own, teacher_width = teacher_hidden.shape
     student_width = student_hidden.shape[1]
-    columns_here = student_head.shape[1]
-    first_column = lax.axis_index("vocab") * columns_here
-    here = lax.axis_index("vocab").astype(jnp.int32)[None]
     payload = pl.pallas_call(
         payload_kernel,
         out_shape=jax.ShapeDtypeStruct((shards, own, teacher_width + student_width + CODE), BF16),
@@ -62,9 +59,168 @@
         out_specs=VMEM,
     )(labels, teacher_hidden, student_hidden)
     rows = swap(payload).reshape(shards * own, -1)
-    teacher_rows = rows[:, :teacher_width]
-    student_rows = rows[:, teacher_width : teacher_width + student_width]
-    code = rows[:, teacher_width + student_width :].astype(jnp.int32)
+    return (
+        rows[:, :teacher_width],
+        rows[:, teacher_width : teacher_width + student_width],
+        rows[:, teacher_width + student_width :],
+    )
+
+
+def round_bf16(array):
+    return lax.reduce_precision(array, exponent_bits=8, mantissa_bits=7)
+
+
+def three_parts(array):
+    high = round_bf16(array)
+    middle = round_bf16(array - high)
+    return [part.astype(BF16) for part in (high, middle, array - high - middle)]
+
+
+def raw_partial_kernel(first_ref, teacher_ref, student_ref, code_ref, stats_ref, head_ref, out_ref):
+    shards, _, _ = out_ref.shape
+    tokens, columns = student_ref.shape
+    width = head_ref.shape[0]
+    rows = 4 * tokens
+
+    def iota(shape, dim):
+        return lax.broadcasted_iota(jnp.int32, shape, dim)
+
+    def dot(left, right, dims):
+        return lax.dot_general(left, right, (dims, ((), ())), preferred_element_type=F32)
+
+    teacher = teacher_ref[...]
+    student = student_ref[...]
+    exp_t = jnp.exp(teacher - jnp.max(teacher, axis=1, keepdims=True))
+    exp_s = jnp.exp(student - jnp.max(student, axis=1, keepdims=True))
+    code = code_ref[...].astype(F32)
+    lane = iota(code.shape, 1)
+    label = jnp.sum(jnp.where(lane == 0, code * 128.0, jnp.where(lane == 1, code, 0.0)), axis=1, keepdims=True)
+    target = (label.astype(jnp.int32) - first_ref[0] == iota((tokens, columns), 1)).astype(F32)
+    high_t = exp_t.astype(BF16).astype(F32)
+    high_s = exp_s.astype(BF16).astype(F32)
+    members = 3 * tokens
+    spread_shape = (rows, members)
+    row, column = iota(spread_shape, 0), iota(spread_shape, 1)
+    pick = jnp.zeros(spread_shape, F32)
+    for j in range(3):
+        pick += ((row % 4 == j) & (column == row // 4 + j * tokens)).astype(F32)
+    pick = pick.astype(BF16)
+    high = jnp.concatenate([high_s, high_t, target], axis=0).astype(BF16)
+    low = jnp.concatenate([exp_s - high_s, exp_t - high_t, jnp.zeros_like(target)], axis=0).astype(BF16)
+    left_high = dot(pick, high, ((1,), (0,))).astype(BF16)
+    left_low = dot(pick, low, ((1,), (0,))).astype(BF16)
+    mix_shape = (tokens, rows)
+    token, place = iota(mix_shape, 0), iota(mix_shape, 1)
+    scale_s = 2.0 / jnp.sum(exp_s, axis=1, keepdims=True)
+    scale_t = 1.0 / jnp.sum(exp_t, axis=1, keepdims=True)
+    mix = jnp.where(place == 4 * token, scale_s, jnp.where(place == 4 * token + 1, -scale_t, 0.0))
+    put = (iota((rows, tokens), 0) == 4 * iota((rows, tokens), 1) + 3).astype(F32).astype(BF16)
+    mix = dot(put, mix.astype(BF16), ((1,), (0,))).astype(BF16)
+    step = 512
+    for start in range(0, width, step):
+        head = head_ref[pl.ds(start, step), :]
+        exact = dot(left_high, head, ((1,), (1,))) + dot(left_low, head, ((1,), (1,)))
+        sent = exact.astype(BF16).astype(F32)
+        residue = (exact - sent).astype(BF16)
+        sent += dot(mix, residue, ((1,), (0,)))
+        for shard in range(shards):
+            out_ref[shard, :, pl.ds(start, step)] = sent[8 * shard : 8 * shard + 8].astype(BF16)
+    stats = stats_ref[...]
+    for shard in range(shards):
+        out_ref[shard, :, width:] = stats
+
+
+def two_exchanges(teacher_hidden, student_hidden, teacher_head, student_head, labels, *, shards):
+    own = labels.shape[0]
+    width = student_hidden.shape[1]
+    columns_here = student_head.shape[1]
+    tokens = shards * own
+    here = lax.axis_index("vocab").astype(jnp.int32)
+    first_column = here * columns_here
+    teacher_rows, student_rows, code = gather_tokens(teacher_hidden, student_hidden, labels, shards)
+    other = [(0, 1), (1, 0)]
+    student_other = lax.ppermute(student_rows, "rows", other)
+
+    teacher_logits = jnp.dot(teacher_rows, teacher_head, preferred_element_type=F32)
+    student_logits = jnp.dot(student_rows, student_head, preferred_element_type=F32)
+    label_rows = code[:, 0].astype(jnp.int32) * 128 + code[:, 1].astype(jnp.int32)
+    columns = lax.broadcasted_iota(jnp.int32, student_logits.shape, 1)
+    target = (label_rows - first_column)[:, None] == columns
+    top_t = jnp.max(teacher_logits, axis=1)
+    exp_t = jnp.exp(teacher_logits - top_t[:, None])
+    top_s = jnp.max(student_logits, axis=1)
+    exp_s = jnp.exp(student_logits - top_s[:, None])
+    stats = jnp.stack(
+        [
+            top_t,
+            jnp.sum(exp_t, axis=1),
+            jnp.sum(exp_t * (teacher_logits - student_logits), axis=1),
+            top_s,
+            jnp.sum(exp_s, axis=1),
+            jnp.sum(jnp.where(target, student_logits, 0.0), axis=1),
+            jnp.sum(jnp.where(target, teacher_logits, 0.0), axis=1),
+            jnp.zeros_like(top_t),
+        ]
+    )
+    stats = jnp.pad(stats, ((0, 0), (0, 128 - tokens)))
+    payload = pl.pallas_call(
+        raw_partial_kernel,
+        out_shape=jax.ShapeDtypeStruct((shards, 8, width + 3 * 128), BF16),
+        in_specs=[SMEM, VMEM, VMEM, VMEM, VMEM, VMEM],
+        out_specs=VMEM,
+    )(first_column[None], teacher_logits, student_logits, code, jnp.concatenate(three_parts(stats), axis=1), student_head)
+    arrived = swap(payload)
+
+    tail = arrived[:, :, width:].astype(F32)
+    every = tail[:, :, :128] + tail[:, :, 128:256] + tail[:, :, 256:]
+
+    def fold(part):
+        top_t = jnp.max(part[:, 0], axis=0)
+        factor_t = jnp.exp(part[:, 0] - top_t)
+        top_s = jnp.max(part[:, 3], axis=0)
+        factor_s = jnp.exp(part[:, 3] - top_s)
+        mass_t = jnp.sum(part[:, 1] * factor_t, axis=0)
+        mass_s = jnp.sum(part[:, 4] * factor_s, axis=0)
+        return top_t, factor_t, mass_t, top_s, factor_s, mass_s
+
+    top_t, _, mass_t, top_s, _, mass_s = fold(every[:, :, :tokens])
+    teacher_prob = jnp.exp(teacher_logits - top_t[:, None]) / mass_t[:, None]
+    student_prob = jnp.exp(student_logits - top_s[:, None]) / mass_s[:, None]
+    grad_rows = (2.0 * student_prob - teacher_prob - target.astype(F32)).astype(BF16)
+    grad_other = lax.ppermute(grad_rows, "rows", other)
+
+    mine = lax.dynamic_slice_in_dim(every, here * own, own, 2)
+    top_t, factor_t, mass_t, top_s, factor_s, mass_s = fold(mine)
+    cross = jnp.sum(mine[:, 2] * factor_t, axis=0)
+    picked = jnp.sum(mine[:, 5], axis=0)
+    picked_t = jnp.sum(mine[:, 6], axis=0)
+    token_loss = cross / mass_t - top_t - jnp.log(mass_t) + 2.0 * (top_s + jnp.log(mass_s)) - picked
+    label_grad = 2.0 * jnp.exp(picked - top_s) / mass_s - jnp.exp(picked_t - top_t) / mass_t - 1.0
+    label_weight = round_bf16(label_grad) - label_grad - 1.0
+    weight_s = factor_s / mass_s
+    weight_t = factor_t / mass_t
+    share = 0.8 * weight_s * mine[:, 4] + 0.2 * weight_t * mine[:, 1]
+    weights = jnp.stack(
+        [2.0 * weight_s, -weight_t, jnp.broadcast_to(label_weight, weight_s.shape), share], axis=2
+    ).reshape(shards, 4 * own, 1)
+    by_row = jnp.sum(weights * arrived[:, :, :width].astype(F32), axis=0)
+    hidden_grad = jnp.sum(by_row.reshape(own, 4, width), axis=1)
+    head_grad = lax.dot_general(
+        jnp.concatenate([student_rows, student_other], axis=0),
+        jnp.concatenate([grad_rows, grad_other], axis=0),
+        (((0,), (0,)), ((), ())),
+        preferred_element_type=F32,
+    )
+    return (token_loss, hidden_grad, head_grad)
+
+
+def three_exchanges(teacher_hidden, student_hidden, teacher_head, student_head, labels, *, shards):
+    own = labels.shape[0]
+    student_width = student_hidden.shape[1]
+    columns_here = student_head.shape[1]
+    first_column = lax.axis_index("vocab") * columns_here
+    teacher_rows, student_rows, code = gather_tokens(teacher_hidden, student_hidden, labels, shards)
+    code = code.astype(jnp.int32)
     label_rows = code[:, 0] * 128 + code[:, 1]
     other = [(0, 1), (1, 0)]
     student_other = lax.ppermute(student_rows, "rows", other)
@@ -122,6 +278,9 @@
     out_specs = (P(tokens), P(tokens, None), P("groups", "vocab"))
 
     def body(*arrays):
-        return on_device(*arrays, shards=mesh.shape["vocab"])
+        shards = mesh.shape["vocab"]
+        tokens_here = shards * arrays[4].shape[0]
+        small = shards <= UNROLL and tokens_here <= 128 and arrays[4].shape[0] == 2
+        return (two_exchanges if small else three_exchanges)(*arrays, shards=shards)
 
     return jax.shard_map(body, mesh=mesh, in_specs=in_specs, out_specs=out_specs, check_vma=False)

time: 44.3 us -> 47.7 us (1.077)
  Pallas kernels: 1.57 us -> 5.54 us
  starting transfers between devices: 14.5 us -> 11.1 us
  waiting for transfers between devices: 20.9 us -> 23 us
  other arithmetic: 1.18 us -> 3.12 us
  local copies, waits for them, and re-layouts: 2.19 us -> 1.35 us
    pallas_call x1 -> x2, Pallas kernels: 1.57 us -> 5.54 us  [the longest x1 3.92 us: two_exchanges(): pl.pallas_call(raw_partial_kernel, out_shape=jax.ShapeDtypeStruct((shards...]
    all_to_all x3 -> x2, starting transfers between devices: 14.3 us -> 11 us  [swap(): lax.all_to_all(blocks, 'vocab', split_axis=0, concat_axis=0, tiled=True)]
    all_to_all x3 -> x2, waiting for transfers between devices: 20.9 us -> 22.7 us  [swap(): lax.all_to_all(blocks, 'vocab', split_axis=0, concat_axis=0, tiled=True)]
    slice x2 -> x7, local copies, waits for them, and re-layouts: 0.01 us -> 1 us  [the longest x1 0.59 us: gather_tokens(): rows[:, teacher_width + student_width:]]
    sub x1 -> x2, other arithmetic: 0.01 us -> 0.72 us  [the longest x1 0.53 us: two_exchanges(): label_weight = round_bf16(label_grad) - label_grad - 1.0]
    reshape x2, local copies, waits for them, and re-layouts: 0.81 us -> 0.13 us  [the longest x1 0.1 us: gather_tokens(): rows = swap(payload).reshape(shards * own, -1)]
    broadcast_in_dim x1 -> x0, local copies, waits for them, and re-layouts: 0.63 us -> none  [on_device(): every = swap(jnp.broadcast_to(stats[None], (shards,) + stats.shape))]
    concatenate x0 -> x1, other arithmetic: none -> 0.59 us  [two_exchanges(): jnp.concatenate(three_parts(stats), axis=1)]
  transfers between devices with their start and end apart: 5 -> 4, of which waited for: 3 -> 3; matrix products, arithmetic and copies ran while one was open for 8% -> 6% of each run, Pallas kernels for 0% -> 0%
where the time goes in v7:
time: 47.7 us; the launch traced here: 47.3 us
  waiting for transfers between devices  23 us (48%)
  starting transfers between devices  11.1 us (23%)
  Pallas kernels  5.54 us (12%)
  other arithmetic  3.12 us (7%)
  matrix products  2.41 us (5%)
  local copies, waits for them, and re-layouts  1.35 us (3%)
  between operations  0.78 us (2%)
    all_to_all x2, waiting for transfers between devices, swap(): lax.all_to_all(blocks, 'vocab', split_axis=0, concat_axis=0, tiled=True)  22.7 us
    all_to_all x2, starting transfers between devices, swap(): lax.all_to_all(blocks, 'vocab', split_axis=0, concat_axis=0, tiled=True)  11 us
    pallas_call x1, Pallas kernels, two_exchanges(): pl.pallas_call(raw_partial_kernel, out_shape=jax.ShapeDtypeStruct((shards...  3.92 us
    dot_general x1, matrix products, two_exchanges(): lax.dot_general(jnp.concatenate([student_rows, student_other], axis=0), j...  1.69 us
    pallas_call x1, Pallas kernels, gather_tokens(): pl.pallas_call(payload_kernel, out_shape=jax.ShapeDtypeStruct((shards, ow...  1.62 us
  transfers between devices with their start and end apart: 4, of which 3 were waited for; matrix products, arithmetic and copies ran while one was open for 6% of the time, Pallas kernels for 0%

profile of v7, /device:TPU:0, one launch (start us, length us, event | category | flops | bytes accessed | tf_op | source)
XLA Modules:
  0.0 47.3 jit_solution(9704579830046898987)
XLA Ops:
  0.6 0.0 copy-start
  0.6 0.0 copy-start.1
  0.7 1.6 %shard_map.76 = bf16[8,2,8320]{2,1,0:T(2,128)(2,1)} custom-call(s32[2]{0:T(128)} %labels_ref.1, bf16[2,4608]{1,0:T(2,128)(2,1)} %teacher_ref.1, bf16[2,3584]{1,0:T(2,128)(2,1)} %student_ref.1), custom_call_target="tpu_custom_call" | custom-call | tf_op jit(solution)/shard_map/pallas_call | solution.py:55
  2.3 7.3 %all-to-all-start = ((bf16[8,2,8320]{2,1,0:T(2,128)(2,1)}), bf16[8,2,8320]{2,1,0:T(2,128)(2,1)S(1)}, u32[]{:S(2)}, u32[]{:S(2)}) async-start(bf16[8,2,8320]{2,1,0:T(2,128)(2,1)} %shard_map.76), calls=%async_computation | async-start | bytes 532480 | tf_op jit(solution)/shard_map/all_to_all | solution.py:27
  9.5 9.0 %all-to-all-done = bf16[8,2,8320]{2,1,0:T(2,128)(2,1)S(1)} async-done(((bf16[8,2,8320]{2,1,0:T(2,128)(2,1)}), bf16[8,2,8320]{2,1,0:T(2,128)(2,1)S(1)}, u32[]{:S(2)}, u32[]{:S(2)}) %all-to-all-start) | async-done | bytes 266272 | tf_op jit(solution)/shard_map/all_to_all | solution.py:27
  18.5 0.1 reshape.231
  18.6 0.6 %slice.99.code_ref = bf16[16,128]{1,0:T(8,128)(2,1)} slice(bf16[16,8320]{1,0:T(8,128)(2,1)S(1)} %reshape.231), slice={[0:16], [8192:8320]} | slice | bytes 8192 | tf_op jit(solution)/shard_map/slice | solution.py:65
  19.2 0.2 subtract_reduce_fusion
  19.4 0.0 copy-done.1
  19.4 0.3 fusion.32
  19.8 0.0 copy-done
  19.8 0.0 copy-start.4
  19.8 0.4 fusion.31
  20.2 0.0 copy-start.2
  20.2 0.3 multiply_reduce_fusion.1
  20.5 0.6 %pad_maximum_fusion.stats_ref = bf16[8,384]{1,0:T(8,128)(2,1)} fusion(bf16[8,128]{1,0:T(8,128)(2,1)S(1)} %get-tuple-element.36, bf16[8,128]{1,0:T(8,128)(2,1)S(1)} %get-tuple-element.37, bf16[8,128]{1,0:T(8,128)(2,1)S(1)} %get-tuple-element.35), kind=kLoop, calls=%fused_computation.22 | loop fusion | flops 18432 | bytes 12288 | tf_op jit(solution)/shard_map/concatenate | solution.py:171
  21.1 0.0 copy-done.4
  21.1 0.0 copy-done.2
  21.1 3.9 %shard_map.77 = bf16[8,8,3968]{2,1,0:T(8,128)(2,1)} custom-call(s32[1]{0:T(128)} %bitcast.first_ref, f32[16,128]{1,0:T(8,128)} %copy-done.2, f32[16,128]{1,0:T(8,128)} %copy-done.4, bf16[16,128]{1,0:T(8,128)(2,1)} %slice.99.code_ref, bf16[8,384]{1,0:T(8,128)(2,1)} %pad_maximum_fusion.stats_ref, bf16[3584,128]{1,0:T(8,128)(2,1)} %head_ref.1), custom_call_target="tpu_custom_call" | custom-call | tf_op jit(solution)/shard_map/pallas_call | solution.py:166
  25.0 0.0 copy-start.3
  25.0 0.0 copy-start.5
  25.0 3.7 %all-to-all-start.1 = ((bf16[8,8,3968]{2,1,0:T(8,128)(2,1)}), bf16[8,8,3968]{2,1,0:T(8,128)(2,1)S(1)}, u32[]{:S(2)}, u32[]{:S(2)}) async-start(bf16[8,8,3968]{2,1,0:T(8,128)(2,1)} %shard_map.77), calls=%async_computation.1 | async-start | bytes 1015808 | tf_op jit(solution)/shard_map/all_to_all | solution.py:27
  28.7 0.1 collective-permute-start
  28.8 13.7 %all-to-all-done.1 = bf16[8,8,3968]{2,1,0:T(8,128)(2,1)S(1)} async-done(((bf16[8,8,3968]{2,1,0:T(8,128)(2,1)}), bf16[8,8,3968]{2,1,0:T(8,128)(2,1)S(1)}, u32[]{:S(2)}, u32[]{:S(2)}) %all-to-all-start.1) | async-done | bytes 507936 | tf_op jit(solution)/shard_map/all_to_all | solution.py:27
  42.6 0.1 constant_dynamic-slice_fusion.2
  42.8 0.1 copy.32
  42.8 0.1 copy.33
  42.9 0.1 copy.34
  43.0 0.1 copy.31
  43.1 0.1 copy.30
  43.2 0.2 fusion.21
  43.4 0.1 broadcast_multiply_fusion
  43.5 0.1 fusion.27
  43.6 0.5 %fusion.22 = (f32[2]{0:T(128)S(1)}, f32[2]{0:T(128)}) fusion(f32[2]{0:T(128)S(1)} %get-tuple-element.13, f32[2]{0:T(128)S(1)} %get-tuple-element.34, f32[2]{0:T(128)S(1)} %get-tuple-element.30, f32[2]{0:T(128)S(1)} %get-tuple-element.44, f32[2]{0:T(128)S(1)} %get-tuple-element.33, f32[2]{0:T(128)S(1)} %get-tuple-element.28, f32[2]{0:T(128)S(1)} %get-tuple-element.12), kind=kLoop, calls=%fused_computation.58 | loop fusion | flops 34 | bytes 72 | tf_op jit(solution)/shard_map/sub | solution.py:199
  44.1 0.1 stack_broadcast_in_dim.3
  44.2 0.1 copy.40
  44.3 0.0 copy-done.3
  44.3 0.0 copy-done.5
  44.3 0.1 subtract_convert_fusion
  44.4 0.1 collective-permute-start.1
  44.5 0.2 multiply_reduce_fusion
  44.7 0.7 %reduce_sum.137 = f32[2,3584]{1,0:T(2,128)} reduce(f32[2,4,3584]{2,1,0:T(4,128)S(1)} %reshape.232, f32[]{:T(128)} %constant.5.clone.1), dimensions={1}, to_apply=%region_15.16 | reduce | flops 21504 | bytes 143364 | tf_op jit(solution)/shard_map/reduce_sum | solution.py:207
  45.4 0.0 collective-permute-done
  45.4 0.3 collective-permute-done.1
  45.6 1.7 %fusion = f32[3584,128]{1,0:T(8,128)} fusion(bf16[16,3584]{1,0:T(8,128)(2,1)S(1)} %collective-permute-done, bf16[16,3584]{1,0:T(8,128)(2,1)S(1)} %slice.98, bf16[16,128]{1,0:T(8,128)(2,1)S(1)} %collective-permute-done.1, bf16[16,128]{1,0:T(8,128)(2,1)S(1)} %subtract_convert_fusion), kind=kOutput, calls=%fused_computation.1 | convolution fusion | flops 29835264 | bytes 2072576 | tf_op jit(solution)/shard_map/dot_general | solution.py:208
  (12 shorter events, 0.2 us)
Async XLA Ops:
  0.6 19.1 %copy-start = (bf16[4608,128]{1,0:T(8,128)(2,1)S(1)}, bf16[4608,128]{1,0:T(8,128)(2,1)}, u32[]{:S(2)}) copy-start(bf16[4608,128]{1,0:T(8,128)(2,1)} %param.7) | copy-start | bytes 3538948
  0.6 18.8 %copy-start.1 = (bf16[3584,128]{1,0:T(8,128)(2,1)S(1)}, bf16[3584,128]{1,0:T(8,128)(2,1)}, u32[]{:S(2)}) copy-start(bf16[3584,128]{1,0:T(8,128)(2,1)} %head_ref.1) | copy-start | bytes 2752516
  2.3 16.3 %all-to-all-start = ((bf16[8,2,8320]{2,1,0:T(2,128)(2,1)}), bf16[8,2,8320]{2,1,0:T(2,128)(2,1)S(1)}, u32[]{:S(2)}, u32[]{:S(2)}) async-start(bf16[8,2,8320]{2,1,0:T(2,128)(2,1)} %shard_map.76), calls=%async_computation | async-start | bytes 532480 | tf_op jit(solution)/shard_map/all_to_all | solution.py:27
  19.8 1.3 %copy-start.4 = (f32[16,128]{1,0:T(8,128)}, f32[16,128]{1,0:T(8,128)S(1)}, u32[]{:S(2)}) copy-start(f32[16,128]{1,0:T(8,128)S(1)} %get-tuple-element.43.student_ref) | copy-start | bytes 24580
  20.2 0.9 %copy-start.2 = (f32[16,128]{1,0:T(8,128)}, f32[16,128]{1,0:T(8,128)S(1)}, u32[]{:S(2)}) copy-start(f32[16,128]{1,0:T(8,128)S(1)} %get-tuple-element.41.teacher_ref) | copy-start | bytes 24580
  25.0 19.3 %copy-start.3 = (f32[16,128]{1,0:T(8,128)S(1)}, f32[16,128]{1,0:T(8,128)}, u32[]{:S(2)}) copy-start(f32[16,128]{1,0:T(8,128)} %copy-done.2) | copy-start | bytes 24580
  25.0 19.3 %copy-start.5 = (f32[16,128]{1,0:T(8,128)S(1)}, f32[16,128]{1,0:T(8,128)}, u32[]{:S(2)}) copy-start(f32[16,128]{1,0:T(8,128)} %copy-done.4) | copy-start | bytes 24580
  25.0 17.5 %all-to-all-start.1 = ((bf16[8,8,3968]{2,1,0:T(8,128)(2,1)}), bf16[8,8,3968]{2,1,0:T(8,128)(2,1)S(1)}, u32[]{:S(2)}, u32[]{:S(2)}) async-start(bf16[8,8,3968]{2,1,0:T(8,128)(2,1)} %shard_map.77), calls=%async_computation.1 | async-start | bytes 1015808 | tf_op jit(solution)/shard_map/all_to_all | solution.py:27
  28.7 16.6 %collective-permute-start = (bf16[16,3584]{1,0:T(8,128)(2,1)S(1)}, bf16[16,3584]{1,0:T(8,128)(2,1)S(1)}, u32[]{:S(2)}, u32[]{:S(2)}) collective-permute-start(bf16[16,3584]{1,0:T(8,128)(2,1)S(1)} %slice.98), channel_id=1, source_target_pairs={{0,1},{1,0},{2,3},{3,2},{4,5},{5,4},{6,7},{7,6},{8,9},{9,8},{10,11... | collective-permute-start | bytes 344072 | tf_op jit(solution)/shard_map/ppermute | solution.py:142
  44.4 1.2 %collective-permute-start.1 = (bf16[16,128]{1,0:T(8,128)(2,1)S(1)}, bf16[16,128]{1,0:T(8,128)(2,1)S(1)}, u32[]{:S(2)}, u32[]{:S(2)}) collective-permute-start(bf16[16,128]{1,0:T(8,128)(2,1)S(1)} %subtract_convert_fusion), channel_id=1, source_target_pairs={{0,1},{1,0},{2,3},{3,2},{4,5},{5,4},{6,7},{7,6},{8,9},{9,8},{10,11... | collective-permute-start | bytes 12296 | tf_op jit(solution)/shard_map/ppermute | solution.py:190

commit v8 on v6

--- a/solution.py
+++ b/solution.py
@@ -49,19 +49,221 @@
     over_shards(shards, write)
 
 
-def on_device(teacher_hidden, student_hidden, teacher_head, student_head, labels, *, shards):
+def gather_tokens(teacher_hidden, student_hidden, labels, shards):
     own, teacher_width = teacher_hidden.shape
     student_width = student_hidden.shape[1]
-    columns_here = student_head.shape[1]
-    first_column = lax.axis_index("vocab") * columns_here
-    here = lax.axis_index("vocab").astype(jnp.int32)[None]
     payload = pl.pallas_call(
         payload_kernel,
         out_shape=jax.ShapeDtypeStruct((shards, own, teacher_width + student_width + CODE), BF16),
         in_specs=[SMEM, VMEM, VMEM],
         out_specs=VMEM,
     )(labels, teacher_hidden, student_hidden)
-    rows = swap(payload).reshape(shards * own, -1)
+    return swap(payload)
+
+
+def round_bf16(array):
+    return lax.reduce_precision(array, exponent_bits=8, mantissa_bits=7)
+
+
+def raw_partial_kernel(first_ref, rows_ref, teacher_head_ref, head_ref, out_ref, teacher_ref, student_ref, target_ref):
+    shards, own, _ = rows_ref.shape
+    tokens = shards * own
+    wide = 8 * shards
+    columns = head_ref.shape[1]
+    teacher_width, width = teacher_head_ref.shape[0], head_ref.shape[0]
+    quarter = width // 4
+
+    def iota(shape, dim):
+        return lax.broadcasted_iota(jnp.int32, shape, dim)
+
+    def dot(left, right, dims):
+        return lax.dot_general(left, right, (dims, ((), ())), preferred_element_type=F32)
+
+    def rows_of(start, size):
+        return jnp.concatenate([rows_ref[shard, :, start : start + size] for shard in range(shards)], axis=0)
+
+    student = dot(rows_of(teacher_width, width), head_ref[...], ((1,), (0,)))
+    teacher = dot(rows_of(0, teacher_width), teacher_head_ref[...], ((1,), (0,)))
+    code = rows_of(teacher_width + width, CODE).astype(F32)
+    lane = iota(code.shape, 1)
+    label = jnp.sum(jnp.where(lane == 0, code * 128.0, jnp.where(lane == 1, code, 0.0)), axis=1, keepdims=True)
+    target = (label.astype(jnp.int32) - first_ref[0] == iota((tokens, columns), 1)).astype(F32)
+    teacher_ref[...] = teacher
+    student_ref[...] = student
+    target_ref[...] = target
+
+    def total(array):
+        return jnp.sum(array, axis=1, keepdims=True)
+
+    top_t = jnp.max(teacher, axis=1, keepdims=True)
+    top_s = jnp.max(student, axis=1, keepdims=True)
+    exp_t = jnp.exp(teacher - top_t)
+    exp_s = jnp.exp(student - top_s)
+    mass_t, mass_s = total(exp_t), total(exp_s)
+    combined = exp_s * (2.0 / mass_s) - exp_t / mass_t
+    kappa = (total(target * combined) > 0.5).astype(F32)
+    stats = [
+        top_t,
+        mass_t,
+        total(exp_t * (teacher - student)),
+        top_s,
+        mass_s,
+        total(target * student),
+        total(target * teacher),
+        2.0 * kappa + total(target),
+    ]
+    lane = iota((tokens, 128), 1)
+    table = jnp.zeros((tokens, 128), F32)
+    for k, stat in enumerate(stats):
+        table = jnp.where(lane % 8 == k, stat, table)
+    first = table.astype(BF16).astype(F32)
+    second = (table - first).astype(BF16).astype(F32)
+    part = (lane % 32) // 8
+    parts = jnp.where(
+        part == 0, first, jnp.where(part == 1, second, jnp.where(part == 2, table - first - second, 0.0))
+    ).astype(BF16)
+
+    row, column = iota((wide, tokens), 0), iota((wide, tokens), 1)
+    of_token = (column == (row // 8) * 2 + row % 2).astype(F32).astype(BF16)
+    by_row = dot(of_token, parts, ((1,), (0,)))
+
+    def stat_by_row(k):
+        picked = by_row[:, k : k + 1] + by_row[:, 8 + k : 9 + k] + by_row[:, 16 + k : 17 + k]
+        return picked
+
+    members = jnp.concatenate([exp_s, exp_t, kappa * combined * total(target) - target], axis=0)
+    member_high = members.astype(BF16)
+    member_low = (members - member_high.astype(F32)).astype(BF16)
+    row, column = iota((wide, 3 * tokens), 0), iota((wide, 3 * tokens), 1)
+    place = row % 8
+    token = (row // 8) * 2 + row % 2
+    picks = [((place < 6) & (column == (place // 2) * tokens + token)).astype(F32)]
+    for j in range(3):
+        picks.append(((place >= 6) & (column == j * tokens + token)).astype(F32))
+    pick = jnp.concatenate(picks, axis=0).astype(BF16)
+    left_high = dot(pick, member_high, ((1,), (0,))).astype(BF16)
+    left_low = dot(pick, member_low, ((1,), (0,))).astype(BF16)
+    left = jnp.concatenate([left_high[:wide], left_low[:wide]], axis=0)
+    left_last = jnp.concatenate([left_high[wide:], left_low[wide:]], axis=0)
+
+    place = iota((wide, 1), 0) % 8
+    has_label = stat_by_row(7) > 0.5
+    scale_s = jnp.where(has_label, 0.0, 2.0 / stat_by_row(4))
+    scale_t = jnp.where(has_label, 0.0, -1.0 / stat_by_row(1))
+    scale = jnp.where(place < 2, scale_s, jnp.where(place < 4, scale_t, 0.0))
+    in_third = ((place == 4) | (place == 5)).astype(F32)
+    scale_s = jnp.where(place >= 6, scale_s, 0.0)
+    scale_t = jnp.where(place >= 6, scale_t, 0.0)
+    last = dot(left_last, head_ref[3 * quarter :, :], ((1,), (1,)))
+    correction = jnp.zeros((wide, quarter), F32)
+    for j in range(3):
+        both = dot(left, head_ref[j * quarter : (j + 1) * quarter, :], ((1,), (1,)))
+        exact = both[:wide] + both[wide:] + last[j * wide : (j + 1) * wide] + last[(3 + j) * wide : (4 + j) * wide]
+        sent = exact.astype(BF16).astype(F32)
+        residue = exact - sent
+        if j < 2:
+            correction += residue * (scale_s, scale_t)[j]
+        else:
+            sent += correction
+        scaled = residue * scale
+        sent += in_third * (pltpu.roll(scaled, 4, 0) + pltpu.roll(scaled, 2, 0))
+        for shard in range(shards):
+            out_ref[shard, :, j * quarter : (j + 1) * quarter] = sent[8 * shard : 8 * shard + 8].astype(BF16)
+    lane = iota((8, 128), 1)
+    shared = jnp.zeros((8, 128), F32)
+    wide_parts = parts.astype(F32)
+    for group in range(tokens // 8):
+        shared = jnp.where(lane // 32 == group + 1, wide_parts[8 * group : 8 * group + 8], shared)
+    for shard in range(shards):
+        block = jnp.where(lane < 32, by_row[8 * shard : 8 * shard + 8], shared)
+        out_ref[shard, :, 3 * quarter :] = block.astype(BF16)
+
+
+def two_exchanges(teacher_hidden, student_hidden, teacher_head, student_head, labels, *, shards):
+    own = labels.shape[0]
+    teacher_width, width = teacher_hidden.shape[1], student_hidden.shape[1]
+    columns_here = student_head.shape[1]
+    tokens = shards * own
+    quarter = width // 4
+    here = lax.axis_index("vocab").astype(jnp.int32)
+    rows = gather_tokens(teacher_hidden, student_hidden, labels, shards)
+    student_rows = rows[:, :, teacher_width : teacher_width + width].reshape(tokens, width)
+    other = [(0, 1), (1, 0)]
+    student_other = lax.ppermute(student_rows, "rows", other)
+
+    square = jax.ShapeDtypeStruct((tokens, columns_here), F32)
+    payload, teacher_logits, student_logits, target = pl.pallas_call(
+        raw_partial_kernel,
+        out_shape=(jax.ShapeDtypeStruct((shards, 8, 3 * quarter + 128), BF16), square, square, square),
+        in_specs=[SMEM, VMEM, VMEM, VMEM],
+        out_specs=(VMEM, VMEM, VMEM, VMEM),
+        compiler_params=pltpu.CompilerParams(vmem_limit_bytes=24 * 1024 * 1024),
+    )((here * columns_here)[None], rows, teacher_head, student_head)
+    arrived = swap(payload)
+    tail = arrived[:, :, 3 * quarter :].astype(F32)
+
+    def statistics(lane):
+        return tail[:, :, lane : lane + 8] + tail[:, :, lane + 8 : lane + 16] + tail[:, :, lane + 16 : lane + 24]
+
+    def fold(stats):
+        top_t = jnp.max(stats[:, :, 0:1], axis=0)
+        factor_t = jnp.exp(stats[:, :, 0:1] - top_t)
+        top_s = jnp.max(stats[:, :, 3:4], axis=0)
+        factor_s = jnp.exp(stats[:, :, 3:4] - top_s)
+        mass_t = jnp.sum(stats[:, :, 1:2] * factor_t, axis=0)
+        mass_s = jnp.sum(stats[:, :, 4:5] * factor_s, axis=0)
+        return top_t, factor_t, mass_t, top_s, factor_s, mass_s
+
+    folded = [fold(statistics(32 * group + 32)) for group in range(tokens // 8)]
+    top_t, _, mass_t, top_s, _, mass_s = [jnp.concatenate([f[i] for f in folded], axis=-2) for i in range(6)]
+    grad_rows = (
+        2.0 * (jnp.exp(student_logits - top_s) / mass_s) - jnp.exp(teacher_logits - top_t) / mass_t - target
+    ).astype(BF16)
+    grad_other = lax.ppermute(grad_rows, "rows", other)
+
+    mine = statistics(0)
+    top_t, factor_t, mass_t, top_s, factor_s, mass_s = fold(mine)
+    cross = jnp.sum(mine[:, :, 2:3] * factor_t, axis=0)
+    picked = jnp.sum(mine[:, :, 5:6], axis=0)
+    picked_t = jnp.sum(mine[:, :, 6:7], axis=0)
+    loss = cross / mass_t - top_t - jnp.log(mass_t) + 2.0 * (top_s + jnp.log(mass_s)) - picked
+    token_loss = loss[:own, 0]
+    label_grad = 2.0 * (jnp.exp(picked - top_s) / mass_s) - jnp.exp(picked_t - top_t) / mass_t - 1.0
+    rounding = round_bf16(label_grad) - label_grad
+    weight_s = factor_s / mass_s
+    weight_t = factor_t / mass_t
+    share_s = weight_s * mine[:, :, 4:5]
+    share_t = weight_t * mine[:, :, 1:2]
+    kappa = (mine[:, :, 7:8] > 2.0).astype(F32)
+    weight_l = jnp.where(mine[:, :, 7:8] > 0.5, 1.0 - (1.0 - kappa) * rounding, 0.8 * share_s + 0.2 * share_t)
+    weight_s = 2.0 * (weight_s - kappa / mine[:, :, 4:5])
+    weight_t = kappa / mine[:, :, 1:2] - weight_t
+    place = lax.broadcasted_iota(jnp.int32, (1, 8, 1), 1)
+    pieces = []
+    for j, weight_last in enumerate((weight_s, weight_t, weight_l)):
+        weight = jnp.where(
+            place < 2, weight_s, jnp.where(place < 4, weight_t, jnp.where(place < 6, weight_l, weight_last))
+        )
+        pieces.append(jnp.sum(weight * arrived[:, :, j * quarter : (j + 1) * quarter].astype(F32), axis=0))
+    hidden_grad = jnp.concatenate(
+        [piece[0:2] + piece[2:4] + piece[4:6] for piece in pieces] + [sum(piece[6:8] for piece in pieces)], axis=1
+    )
+    head_grad = lax.dot_general(
+        jnp.concatenate([student_rows, student_other], axis=0),
+        jnp.concatenate([grad_rows, grad_other], axis=0),
+        (((0,), (0,)), ((), ())),
+        preferred_element_type=F32,
+    )
+    return (token_loss, hidden_grad, head_grad)
+
+
+def three_exchanges(teacher_hidden, student_hidden, teacher_head, student_head, labels, *, shards):
+    own = labels.shape[0]
+    student_width = student_hidden.shape[1]
+    columns_here = student_head.shape[1]
+    first_column = lax.axis_index("vocab") * columns_here
+    rows = gather_tokens(teacher_hidden, student_hidden, labels, shards).reshape(shards * own, -1)
+    teacher_width = teacher_hidden.shape[1]
     teacher_rows = rows[:, :teacher_width]
     student_rows = rows[:, teacher_width : teacher_width + student_width]
     code = rows[:, teacher_width + student_width :].astype(jnp.int32)
@@ -122,6 +324,9 @@
     out_specs = (P(tokens), P(tokens, None), P("groups", "vocab"))
 
     def body(*arrays):
-        return on_device(*arrays, shards=mesh.shape["vocab"])
+        shards = mesh.shape["vocab"]
+        own = arrays[4].shape[0]
+        small = own == 2 and shards % 4 == 0 and shards * own <= 24
+        return (two_exchanges if small else three_exchanges)(*arrays, shards=shards)
 
     return jax.shard_map(body, mesh=mesh, in_specs=in_specs, out_specs=out_specs, check_vma=False)

time: 44.3 us -> 43.2 us (0.975)
  starting transfers between devices: 14.5 us -> 11 us
  other arithmetic: 1.18 us -> 3.54 us
  Pallas kernels: 1.57 us -> 3.62 us
  waiting for transfers between devices: 20.9 us -> 19.6 us
  matrix products: 2.73 us -> 1.69 us
    all_to_all x3 -> x2, starting transfers between devices: 14.3 us -> 10.8 us  [swap(): lax.all_to_all(blocks, 'vocab', split_axis=0, concat_axis=0, tiled=True)]
    unnamed x5 -> x4, local copies, waits for them, and re-layouts: 0.14 us -> 2.45 us
    pallas_call x1 -> x2, Pallas kernels: 1.57 us -> 3.62 us  [the longest x1 2.15 us: two_exchanges(): pl.pallas_call(raw_partial_kernel, out_shape=(jax.ShapeDtypeStruct((shard...]
    all_to_all x3 -> x2, waiting for transfers between devices: 20.9 us -> 19.4 us  [swap(): lax.all_to_all(blocks, 'vocab', split_axis=0, concat_axis=0, tiled=True)]
    dot_general x4 -> x1, matrix products: 2.73 us -> 1.69 us  [two_exchanges(): lax.dot_general(jnp.concatenate([student_rows, student_other], axis=0), j...]
    sub x1 -> x3, other arithmetic: 0.01 us -> 0.86 us  [the longest x1 0.53 us: two_exchanges(): rounding = round_bf16(label_grad) - label_grad]
    reshape x2 -> x1, local copies, waits for them, and re-layouts: 0.81 us -> 0.05 us  [two_exchanges(): rows[:, :, teacher_width:teacher_width + width].reshape(tokens, width)]
    broadcast_in_dim x1 -> x0, local copies, waits for them, and re-layouts: 0.63 us -> none  [on_device(): every = swap(jnp.broadcast_to(stats[None], (shards,) + stats.shape))]
  transfers between devices with their start and end apart: 5 -> 4, of which waited for: 3 -> 3; matrix products, arithmetic and copies ran while one was open for 8% -> 9% of each run, Pallas kernels for 0% -> 0%
where the time goes in v8:
time: 43.2 us; the launch traced here: 42.8 us
  waiting for transfers between devices  19.6 us (45%)
  starting transfers between devices  11 us (25%)
  Pallas kernels  3.62 us (8%)
  other arithmetic  3.54 us (8%)
  local copies, waits for them, and re-layouts  2.58 us (6%)
  matrix products  1.69 us (4%)
  between operations  0.75 us (2%)
    all_to_all x2, waiting for transfers between devices, swap(): lax.all_to_all(blocks, 'vocab', split_axis=0, concat_axis=0, tiled=True)  19.4 us
    all_to_all x2, starting transfers between devices, swap(): lax.all_to_all(blocks, 'vocab', split_axis=0, concat_axis=0, tiled=True)  10.8 us
    unnamed x4, local copies, waits for them, and re-layouts  2.45 us
    pallas_call x1, Pallas kernels, two_exchanges(): pl.pallas_call(raw_partial_kernel, out_shape=(jax.ShapeDtypeStruct((shard...  2.15 us
    dot_general x1, matrix products, two_exchanges(): lax.dot_general(jnp.concatenate([student_rows, student_other], axis=0), j...  1.69 us
    pallas_call x1, Pallas kernels, gather_tokens(): pl.pallas_call(payload_kernel, out_shape=jax.ShapeDtypeStruct((shards, ow...  1.48 us
  transfers between devices with their start and end apart: 4, of which 3 were waited for; matrix products, arithmetic and copies ran while one was open for 9% of the time, Pallas kernels for 0%

profile of v8, /device:TPU:0, one launch (start us, length us, event | category | flops | bytes accessed | tf_op | source)
XLA Modules:
  0.0 42.8 jit_solution(1426251649445203272)
XLA Ops:
  0.6 1.5 %shard_map.76 = bf16[8,2,8320]{2,1,0:T(2,128)(2,1)} custom-call(s32[2]{0:T(128)} %labels_ref.1, bf16[2,4608]{1,0:T(2,128)(2,1)} %teacher_ref.1, bf16[2,3584]{1,0:T(2,128)(2,1)} %student_ref.1), custom_call_target="tpu_custom_call" | custom-call | tf_op jit(solution)/shard_map/pallas_call | solution.py:55
  2.1 7.3 %all-to-all-start = ((bf16[8,2,8320]{2,1,0:T(2,128)(2,1)}), bf16[8,2,8320]{2,1,0:T(2,128)(2,1)S(1)}, u32[]{:S(2)}, u32[]{:S(2)}) async-start(bf16[8,2,8320]{2,1,0:T(2,128)(2,1)} %shard_map.76), calls=%async_computation | async-start | bytes 532480 | tf_op jit(solution)/shard_map/all_to_all | solution.py:27
  9.4 9.0 %all-to-all-done.rows_ref = bf16[8,2,8320]{2,1,0:T(2,128)(2,1)S(1)} async-done(((bf16[8,2,8320]{2,1,0:T(2,128)(2,1)}), bf16[8,2,8320]{2,1,0:T(2,128)(2,1)S(1)}, u32[]{:S(2)}, u32[]{:S(2)}) %all-to-all-start) | async-done | bytes 266272 | tf_op jit(solution)/shard_map/all_to_all | solution.py:27
  18.4 0.0 copy-start
  18.4 1.3 %copy-done = bf16[4608,128]{1,0:T(8,128)(2,1)S(1)} copy-done((bf16[4608,128]{1,0:T(8,128)(2,1)S(1)}, bf16[4608,128]{1,0:T(8,128)(2,1)}, u32[]{:S(2)}) %copy-start) | copy-done | bytes 1179672
  19.6 0.0 copy-start.1
  19.6 1.2 %copy-done.1 = bf16[3584,128]{1,0:T(8,128)(2,1)S(1)} copy-done((bf16[3584,128]{1,0:T(8,128)(2,1)S(1)}, bf16[3584,128]{1,0:T(8,128)(2,1)}, u32[]{:S(2)}) %copy-start.1) | copy-done | bytes 917528
  20.8 2.1 %shard_map.77 = (bf16[8,8,2816]{2,1,0:T(8,128)(2,1)}, f32[16,128]{1,0:T(8,128)S(1)}, f32[16,128]{1,0:T(8,128)S(1)}, f32[16,128]{1,0:T(8,128)S(1)}) custom-call(s32[1]{0:T(128)} %bitcast.first_ref, bf16[8,2,8320]{2,1,0:T(2,128)(2,1)S(1)} %all-to-all-done.rows_ref, bf16[4608,128]{1,0:T(8,128)(2,1)S(1)} %copy-done, bf16[3584,128]{1,0:T(8,128)(2,1)S(1)} %copy-done.1), custom_call_target="tpu_custom_call" | custom-call | tf_op jit(solution)/shard_map/pallas_call | solution.py:195
  23.0 3.6 %all-to-all-start.1 = ((bf16[8,8,2816]{2,1,0:T(8,128)(2,1)}), bf16[8,8,2816]{2,1,0:T(8,128)(2,1)S(1)}, u32[]{:S(2)}, u32[]{:S(2)}) async-start(bf16[8,8,2816]{2,1,0:T(8,128)(2,1)} %get-tuple-element.7), calls=%async_computation.1 | async-start | bytes 720896 | tf_op jit(solution)/shard_map/all_to_all | solution.py:27
  26.6 0.1 slice.211
  26.7 0.1 collective-permute-start
  26.8 10.4 %all-to-all-done.1 = bf16[8,8,2816]{2,1,0:T(8,128)(2,1)S(1)} async-done(((bf16[8,8,2816]{2,1,0:T(8,128)(2,1)}), bf16[8,8,2816]{2,1,0:T(8,128)(2,1)S(1)}, u32[]{:S(2)}, u32[]{:S(2)}) %all-to-all-start.1) | async-done | bytes 360480 | tf_op jit(solution)/shard_map/all_to_all | solution.py:27
  37.2 0.1 slice_add_fusion.2
  37.4 0.2 slice_reduce_fusion.6
  37.6 0.2 slice_reduce_fusion.5
  37.8 0.2 slice_reduce_fusion.4
  37.9 0.3 slice_reduce_fusion
  38.2 0.2 fusion.16
  38.4 0.5 %reduce-precision_subtract_fusion = (f32[8]{0:T(128)S(1)}, f32[8]{0:T(128)}) fusion(f32[8]{0:T(128)S(1)} %get-tuple-element.18, f32[8]{0:T(128)S(1)} %get-tuple-element.27, f32[8]{0:T(128)S(1)} %get-tuple-element.30, f32[8]{0:T(128)S(1)} %get-tuple-element.29, f32[8]{0:T(128)S(1)} %get-tuple-element.28, f32[8]{0:T(128)S(1)} %slice_reduce_fusion.6, ...), kind=kLoop, calls=%fused_computation.66 | loop fusion | flops 128 | bytes 288 | tf_op jit(solution)/shard_map/sub | solution.py:232
  38.9 0.1 fusion.11
  39.1 0.2 fusion.15
  39.3 0.3 fusion.8
  39.5 0.1 maximum_bitcast_fusion.1
  39.6 0.1 maximum_bitcast_fusion.3
  39.7 0.1 maximum_bitcast_fusion
  39.8 0.1 subtract_convert_fusion
  39.9 0.1 collective-permute-start.1
  39.9 0.2 select_reduce_fusion.1
  40.1 0.1 multiply_reduce_fusion.2
  40.3 0.6 %pad_maximum_fusion = f32[2,3584]{1,0:T(2,128)} fusion(f32[2,896]{1,0:T(2,128)S(1)} %get-tuple-element.39, f32[2,896]{1,0:T(2,128)S(1)} %get-tuple-element.41, f32[2,896]{1,0:T(2,128)S(1)} %get-tuple-element.40, f32[2,896]{1,0:T(2,128)S(1)} %get-tuple-element.38), kind=kLoop, calls=%fused_computation.50 | loop fusion | flops 21504 | bytes 57344 | tf_op jit(solution)/shard_map/concatenate | solution.py:248
  40.9 0.0 collective-permute-done
  40.9 0.2 collective-permute-done.1
  41.1 1.7 %fusion = f32[3584,128]{1,0:T(8,128)} fusion(bf16[16,3584]{1,0:T(8,128)(2,1)S(1)} %collective-permute-done, bf16[16,3584]{1,0:T(8,128)(2,1)S(1)} %reshape.195, bf16[16,128]{1,0:T(8,128)(2,1)S(1)} %collective-permute-done.1, bf16[16,128]{1,0:T(8,128)(2,1)S(1)} %subtract_convert_fusion), kind=kOutput, calls=%fused_computation | convolution fusion | flops 29835264 | bytes 2072576 | tf_op jit(solution)/shard_map/dot_general | solution.py:251
  (5 shorter events, 0.1 us)
Async XLA Ops:
  2.1 16.3 %all-to-all-start = ((bf16[8,2,8320]{2,1,0:T(2,128)(2,1)}), bf16[8,2,8320]{2,1,0:T(2,128)(2,1)S(1)}, u32[]{:S(2)}, u32[]{:S(2)}) async-start(bf16[8,2,8320]{2,1,0:T(2,128)(2,1)} %shard_map.76), calls=%async_computation | async-start | bytes 532480 | tf_op jit(solution)/shard_map/all_to_all | solution.py:27
  18.4 1.3 %copy-start = (bf16[4608,128]{1,0:T(8,128)(2,1)S(1)}, bf16[4608,128]{1,0:T(8,128)(2,1)}, u32[]{:S(2)}) copy-start(bf16[4608,128]{1,0:T(8,128)(2,1)} %teacher_head_ref.1) | copy-start | bytes 3538948
  19.6 1.2 %copy-start.1 = (bf16[3584,128]{1,0:T(8,128)(2,1)S(1)}, bf16[3584,128]{1,0:T(8,128)(2,1)}, u32[]{:S(2)}) copy-start(bf16[3584,128]{1,0:T(8,128)(2,1)} %head_ref.1) | copy-start | bytes 2752516
  23.0 14.3 %all-to-all-start.1 = ((bf16[8,8,2816]{2,1,0:T(8,128)(2,1)}), bf16[8,8,2816]{2,1,0:T(8,128)(2,1)S(1)}, u32[]{:S(2)}, u32[]{:S(2)}) async-start(bf16[8,8,2816]{2,1,0:T(8,128)(2,1)} %get-tuple-element.7), calls=%async_computation.1 | async-start | bytes 720896 | tf_op jit(solution)/shard_map/all_to_all | solution.py:27
  26.7 14.2 %collective-permute-start = (bf16[16,3584]{1,0:T(8,128)(2,1)S(1)}, bf16[16,3584]{1,0:T(8,128)(2,1)S(1)}, u32[]{:S(2)}, u32[]{:S(2)}) collective-permute-start(bf16[16,3584]{1,0:T(8,128)(2,1)S(1)} %reshape.195), channel_id=1, source_target_pairs={{0,1},{1,0},{2,3},{3,2},{4,5},{5,4},{6,7},{7,6},{8,9},{9,8},{10,11... | collective-permute-start | bytes 344072 | tf_op jit(solution)/shard_map/ppermute | solution.py:192
  39.9 1.2 %collective-permute-start.1 = (bf16[16,128]{1,0:T(8,128)(2,1)S(1)}, bf16[16,128]{1,0:T(8,128)(2,1)S(1)}, u32[]{:S(2)}, u32[]{:S(2)}) collective-permute-start(bf16[16,128]{1,0:T(8,128)(2,1)S(1)} %subtract_convert_fusion), channel_id=1, source_target_pairs={{0,1},{1,0},{2,3},{3,2},{4,5},{5,4},{6,7},{7,6},{8,9},{9,8},{10,11... | collective-permute-start | bytes 12296 | tf_op jit(solution)/shard_map/ppermute | solution.py:222

commit v9 on v8

--- a/solution.py
+++ b/solution.py
@@ -13,6 +13,7 @@
 UNROLL = 16
 SMEM = pl.BlockSpec(memory_space=pltpu.SMEM)
 VMEM = pl.BlockSpec(memory_space=pltpu.VMEM)
+SMALL = pltpu.CompilerParams(vmem_limit_bytes=16 * 1024 * 1024)
 
 
 def over_shards(shards, body):
@@ -57,21 +58,19 @@
         out_shape=jax.ShapeDtypeStruct((shards, own, teacher_width + student_width + CODE), BF16),
         in_specs=[SMEM, VMEM, VMEM],
         out_specs=VMEM,
+        compiler_params=SMALL,
     )(labels, teacher_hidden, student_hidden)
     return swap(payload)
 
 
-def round_bf16(array):
-    return lax.reduce_precision(array, exponent_bits=8, mantissa_bits=7)
-
-
-def raw_partial_kernel(first_ref, rows_ref, teacher_head_ref, head_ref, out_ref, teacher_ref, student_ref, target_ref):
+def raw_partial_kernel(first_ref, rows_ref, heads_ref, out_ref, teacher_ref, student_ref, target_ref):
     shards, own, _ = rows_ref.shape
     tokens = shards * own
     wide = 8 * shards
-    columns = head_ref.shape[1]
-    teacher_width, width = teacher_head_ref.shape[0], head_ref.shape[0]
-    quarter = width // 4
+    columns = heads_ref.shape[1]
+    quarter = (out_ref.shape[2] - 128) // 3
+    width = 4 * quarter
+    teacher_width = heads_ref.shape[0] - width
 
     def iota(shape, dim):
         return lax.broadcasted_iota(jnp.int32, shape, dim)
@@ -82,8 +81,8 @@
     def rows_of(start, size):
         return jnp.concatenate([rows_ref[shard, :, start : start + size] for shard in range(shards)], axis=0)
 
-    student = dot(rows_of(teacher_width, width), head_ref[...], ((1,), (0,)))
-    teacher = dot(rows_of(0, teacher_width), teacher_head_ref[...], ((1,), (0,)))
+    student = dot(rows_of(teacher_width, width), heads_ref[teacher_width:, :], ((1,), (0,)))
+    teacher = dot(rows_of(0, teacher_width), heads_ref[:teacher_width, :], ((1,), (0,)))
     code = rows_of(teacher_width + width, CODE).astype(F32)
     lane = iota(code.shape, 1)
     label = jnp.sum(jnp.where(lane == 0, code * 128.0, jnp.where(lane == 1, code, 0.0)), axis=1, keepdims=True)
@@ -154,10 +153,10 @@
     in_third = ((place == 4) | (place == 5)).astype(F32)
     scale_s = jnp.where(place >= 6, scale_s, 0.0)
     scale_t = jnp.where(place >= 6, scale_t, 0.0)
-    last = dot(left_last, head_ref[3 * quarter :, :], ((1,), (1,)))
+    last = dot(left_last, heads_ref[teacher_width + 3 * quarter :, :], ((1,), (1,)))
     correction = jnp.zeros((wide, quarter), F32)
     for j in range(3):
-        both = dot(left, head_ref[j * quarter : (j + 1) * quarter, :], ((1,), (1,)))
+        both = dot(left, heads_ref[teacher_width + j * quarter : teacher_width + (j + 1) * quarter, :], ((1,), (1,)))
         exact = both[:wide] + both[wide:] + last[j * wide : (j + 1) * wide] + last[(3 + j) * wide : (4 + j) * wide]
         sent = exact.astype(BF16).astype(F32)
         residue = exact - sent
@@ -179,6 +178,67 @@
         out_ref[shard, :, 3 * quarter :] = block.astype(BF16)
 
 
+def sum_parts(tail):
+    shards = tail.shape[0]
+    flat = tail.astype(F32).reshape(shards * 8, 128)
+    return flat + pltpu.roll(flat, 120, 1) + pltpu.roll(flat, 112, 1)
+
+
+def fold(flat, lane):
+    shards = flat.shape[0] // 8
+    stats = [flat[:, lane + k : lane + k + 1].reshape(shards, 8, 1) for k in range(8)]
+    top_t = jnp.max(stats[0], axis=0)
+    factor_t = jnp.exp(stats[0] - top_t)
+    top_s = jnp.max(stats[3], axis=0)
+    factor_s = jnp.exp(stats[3] - top_s)
+    mass_t = jnp.sum(stats[1] * factor_t, axis=0)
+    mass_s = jnp.sum(stats[4] * factor_s, axis=0)
+    return stats, top_t, factor_t, mass_t, top_s, factor_s, mass_s
+
+
+def logit_grad_kernel(tail_ref, teacher_ref, student_ref, target_ref, out_ref):
+    flat = sum_parts(tail_ref[...])
+    folded = [fold(flat, 32 * group + 32) for group in range(out_ref.shape[0] // 8)]
+    top_t, mass_t, top_s, mass_s = [jnp.concatenate([f[i] for f in folded], axis=0) for i in (1, 3, 4, 6)]
+    teacher_prob = jnp.exp(teacher_ref[...] - top_t) / mass_t
+    student_prob = jnp.exp(student_ref[...] - top_s) / mass_s
+    out_ref[...] = (2.0 * student_prob - teacher_prob - target_ref[...]).astype(BF16)
+
+
+def owner_kernel(arrived_ref, out_ref, loss_ref):
+    shards, _, lanes = arrived_ref.shape
+    quarter = (lanes - 128) // 3
+    stats, top_t, factor_t, mass_t, top_s, factor_s, mass_s = fold(sum_parts(arrived_ref[:, :, 3 * quarter :]), 0)
+    cross = jnp.sum(stats[2] * factor_t, axis=0)
+    picked = jnp.sum(stats[5], axis=0)
+    picked_t = jnp.sum(stats[6], axis=0)
+    loss = cross / mass_t - top_t - jnp.log(mass_t) + 2.0 * (top_s + jnp.log(mass_s)) - picked
+    square = (8, 128)
+    same = lax.broadcasted_iota(jnp.int32, square, 0) == lax.broadcasted_iota(jnp.int32, square, 1)
+    loss_ref[...] = jnp.sum(jnp.where(same, loss, 0.0), axis=0, keepdims=True)
+    label_grad = 2.0 * (jnp.exp(picked - top_s) / mass_s) - jnp.exp(picked_t - top_t) / mass_t - 1.0
+    rounding = label_grad.astype(BF16).astype(F32) - label_grad
+    weight_s = factor_s / mass_s
+    weight_t = factor_t / mass_t
+    share = 0.8 * weight_s * stats[4] + 0.2 * weight_t * stats[1]
+    kappa = jnp.where(stats[7] > 2.0, 1.0, 0.0)
+    weight_l = jnp.where(stats[7] > 0.5, 1.0 - (1.0 - kappa) * rounding, share)
+    weight_s = 2.0 * (weight_s - kappa / stats[4])
+    weight_t = kappa / stats[1] - weight_t
+    place = lax.broadcasted_iota(jnp.int32, (shards, 8, 1), 1)
+    last = jnp.zeros((8, quarter), F32)
+    for j, weight_last in enumerate((weight_s, weight_t, weight_l)):
+        weight = jnp.where(
+            place < 2, weight_s, jnp.where(place < 4, weight_t, jnp.where(place < 6, weight_l, weight_last))
+        )
+        piece = jnp.zeros((8, quarter), F32)
+        for shard in range(shards):
+            piece += weight[shard] * arrived_ref[shard, :, j * quarter : (j + 1) * quarter].astype(F32)
+        last += piece
+        out_ref[:, j * quarter : (j + 1) * quarter] = piece[0:2] + piece[2:4] + piece[4:6]
+    out_ref[:, 3 * quarter :] = last[6:8]
+
+
 def two_exchanges(teacher_hidden, student_hidden, teacher_head, student_head, labels, *, shards):
     own = labels.shape[0]
     teacher_width, width = teacher_hidden.shape[1], student_hidden.shape[1]
@@ -195,59 +255,27 @@
     payload, teacher_logits, student_logits, target = pl.pallas_call(
         raw_partial_kernel,
         out_shape=(jax.ShapeDtypeStruct((shards, 8, 3 * quarter + 128), BF16), square, square, square),
-        in_specs=[SMEM, VMEM, VMEM, VMEM],
+        in_specs=[SMEM, VMEM, VMEM],
         out_specs=(VMEM, VMEM, VMEM, VMEM),
-        compiler_params=pltpu.CompilerParams(vmem_limit_bytes=24 * 1024 * 1024),
-    )((here * columns_here)[None], rows, teacher_head, student_head)
+        compiler_params=SMALL,
+    )((here * columns_here)[None], rows, jnp.concatenate([teacher_head, student_head], axis=0))
     arrived = swap(payload)
-    tail = arrived[:, :, 3 * quarter :].astype(F32)
-
-    def statistics(lane):
-        return tail[:, :, lane : lane + 8] + tail[:, :, lane + 8 : lane + 16] + tail[:, :, lane + 16 : lane + 24]
-
-    def fold(stats):
-        top_t = jnp.max(stats[:, :, 0:1], axis=0)
-        factor_t = jnp.exp(stats[:, :, 0:1] - top_t)
-        top_s = jnp.max(stats[:, :, 3:4], axis=0)
-        factor_s = jnp.exp(stats[:, :, 3:4] - top_s)
-        mass_t = jnp.sum(stats[:, :, 1:2] * factor_t, axis=0)
-        mass_s = jnp.sum(stats[:, :, 4:5] * factor_s, axis=0)
-        return top_t, factor_t, mass_t, top_s, factor_s, mass_s
-
-    folded = [fold(statistics(32 * group + 32)) for group in range(tokens // 8)]
-    top_t, _, mass_t, top_s, _, mass_s = [jnp.concatenate([f[i] for f in folded], axis=-2) for i in range(6)]
-    grad_rows = (
-        2.0 * (jnp.exp(student_logits - top_s) / mass_s) - jnp.exp(teacher_logits - top_t) / mass_t - target
-    ).astype(BF16)
+    grad_rows = pl.pallas_call(
+        logit_grad_kernel,
+        out_shape=jax.ShapeDtypeStruct((tokens, columns_here), BF16),
+        in_specs=[VMEM] * 4,
+        out_specs=VMEM,
+        compiler_params=SMALL,
+    )(arrived[:, :, 3 * quarter :], teacher_logits, student_logits, target)
     grad_other = lax.ppermute(grad_rows, "rows", other)
-
-    mine = statistics(0)
-    top_t, factor_t, mass_t, top_s, factor_s, mass_s = fold(mine)
-    cross = jnp.sum(mine[:, :, 2:3] * factor_t, axis=0)
-    picked = jnp.sum(mine[:, :, 5:6], axis=0)
-    picked_t = jnp.sum(mine[:, :, 6:7], axis=0)
-    loss = cross / mass_t - top_t - jnp.log(mass_t) + 2.0 * (top_s + jnp.log(mass_s)) - picked
-    token_loss = loss[:own, 0]
-    label_grad = 2.0 * (jnp.exp(picked - top_s) / mass_s) - jnp.exp(picked_t - top_t) / mass_t - 1.0
-    rounding = round_bf16(label_grad) - label_grad
-    weight_s = factor_s / mass_s
-    weight_t = factor_t / mass_t
-    share_s = weight_s * mine[:, :, 4:5]
-    share_t = weight_t * mine[:, :, 1:2]
-    kappa = (mine[:, :, 7:8] > 2.0).astype(F32)
-    weight_l = jnp.where(mine[:, :, 7:8] > 0.5, 1.0 - (1.0 - kappa) * rounding, 0.8 * share_s + 0.2 * share_t)
-    weight_s = 2.0 * (weight_s - kappa / mine[:, :, 4:5])
-    weight_t = kappa / mine[:, :, 1:2] - weight_t
-    place = lax.broadcasted_iota(jnp.int32, (1, 8, 1), 1)
-    pieces = []
-    for j, weight_last in enumerate((weight_s, weight_t, weight_l)):
-        weight = jnp.where(
-            place < 2, weight_s, jnp.where(place < 4, weight_t, jnp.where(place < 6, weight_l, weight_last))
-        )
-        pieces.append(jnp.sum(weight * arrived[:, :, j * quarter : (j + 1) * quarter].astype(F32), axis=0))
-    hidden_grad = jnp.concatenate(
-        [piece[0:2] + piece[2:4] + piece[4:6] for piece in pieces] + [sum(piece[6:8] for piece in pieces)], axis=1
-    )
+    hidden_grad, loss = pl.pallas_call(
+        owner_kernel,
+        out_shape=(jax.ShapeDtypeStruct((own, width), F32), jax.ShapeDtypeStruct((1, 128), F32)),
+        in_specs=[VMEM],
+        out_specs=(VMEM, VMEM),
+        compiler_params=SMALL,
+    )(arrived)
+    token_loss = loss[0, :own]
     head_grad = lax.dot_general(
         jnp.concatenate([student_rows, student_other], axis=0),
         jnp.concatenate([grad_rows, grad_other], axis=0),

time: 43.2 us -> 41 us (0.949)
  other arithmetic: 3.54 us -> 1.69 us
  waiting for transfers between devices: 19.6 us -> 17.8 us
  Pallas kernels: 3.62 us -> 4.97 us
    all_to_all x2, waiting for transfers between devices: 19.4 us -> 17.8 us  [swap(): lax.all_to_all(blocks, 'vocab', split_axis=0, concat_axis=0, tiled=True)]
    pallas_call x0 -> x2, Pallas kernels: none -> 1.56 us  [the longest x1 1.24 us: two_exchanges(): pl.pallas_call(owner_kernel, out_shape=(jax.ShapeDtypeStruct((own, width)...]
    concatenate x1, other arithmetic: 0.62 us -> 1.69 us  [two_exchanges(): jnp.concatenate([teacher_head, student_head], axis=0)]
    sub x3 -> x0, other arithmetic: 0.86 us -> none  [the longest x1 0.53 us: two_exchanges(): rounding = round_bf16(label_grad) - label_grad]
    reduce_sum x4 -> x0, other arithmetic: 0.8 us -> none  [the longest x1 0.26 us: two_exchanges(): picked_t = jnp.sum(mine[:, :, 6:7], axis=0)]
    reduce_max x3 -> x0, other arithmetic: 0.57 us -> none  [fold(): top_s = jnp.max(stats[:, :, 3:4], axis=0)]
    squeeze x0 -> x1, local copies, waits for them, and re-layouts: none -> 0.51 us  [two_exchanges(): token_loss = loss[0, :own]]
    unnamed x4 -> x6, local copies, waits for them, and re-layouts: 2.45 us -> 2.08 us
  transfers between devices with their start and end apart: 4 -> 4, of which waited for: 3 -> 2; matrix products, arithmetic and copies ran while one was open for 9% -> 6% of each run, Pallas kernels for 0% -> 4%
where the time goes in v9:
time: 41 us; the launch traced here: 40.5 us
  waiting for transfers between devices  17.8 us (43%)
  starting transfers between devices  11 us (27%)
  Pallas kernels  4.97 us (12%)
  local copies, waits for them, and re-layouts  2.72 us (7%)
  other arithmetic  1.69 us (4%)
  matrix products  1.69 us (4%)
  between operations  0.68 us (2%)
    all_to_all x2, waiting for transfers between devices, swap(): lax.all_to_all(blocks, 'vocab', split_axis=0, concat_axis=0, tiled=True)  17.8 us
    all_to_all x2, starting transfers between devices, swap(): lax.all_to_all(blocks, 'vocab', split_axis=0, concat_axis=0, tiled=True)  10.8 us
    pallas_call x1, Pallas kernels, two_exchanges(): pl.pallas_call(raw_partial_kernel, out_shape=(jax.ShapeDtypeStruct((shard...  2.14 us
    unnamed x6, local copies, waits for them, and re-layouts  2.08 us
    dot_general x1, matrix products, two_exchanges(): lax.dot_general(jnp.concatenate([student_rows, student_other], axis=0), j...  1.69 us
    concatenate x1, other arithmetic, two_exchanges(): jnp.concatenate([teacher_head, student_head], axis=0)  1.69 us
    pallas_call x1, Pallas kernels, gather_tokens(): pl.pallas_call(payload_kernel, out_shape=jax.ShapeDtypeStruct((shards, ow...  1.28 us
    pallas_call x1, Pallas kernels, two_exchanges(): pl.pallas_call(owner_kernel, out_shape=(jax.ShapeDtypeStruct((own, width)...  1.24 us
  transfers between devices with their start and end apart: 4, of which 2 were waited for; matrix products, arithmetic and copies ran while one was open for 6% of the time, Pallas kernels for 4%

profile of v9, /device:TPU:0, one launch (start us, length us, event | category | flops | bytes accessed | tf_op | source)
XLA Modules:
  0.0 40.5 jit_solution(15373558081293838631)
XLA Ops:
  0.6 0.0 copy-start
  0.6 0.7 %copy-done = bf16[2,4608]{1,0:T(2,128)(2,1)S(1)} copy-done((bf16[2,4608]{1,0:T(2,128)(2,1)S(1)}, bf16[2,4608]{1,0:T(2,128)(2,1)}, u32[]{:S(2)}) %copy-start) | copy-done | bytes 18456
  1.4 0.0 copy-start.1
  1.4 0.7 %copy-done.1 = bf16[2,3584]{1,0:T(2,128)(2,1)S(1)} copy-done((bf16[2,3584]{1,0:T(2,128)(2,1)S(1)}, bf16[2,3584]{1,0:T(2,128)(2,1)}, u32[]{:S(2)}) %copy-start.1) | copy-done | bytes 14360
  2.1 0.0 copy-start.2
  2.1 0.7 %copy-done.2 = s32[2]{0:T(128)S(1)} copy-done((s32[2]{0:T(128)S(1)}, s32[2]{0:T(128)}, u32[]{:S(2)}) %copy-start.2) | copy-done | bytes 32
  2.7 1.3 %shard_map.76 = bf16[8,2,8320]{2,1,0:T(2,128)(2,1)} custom-call(s32[2]{0:T(128)S(1)} %copy-done.2, bf16[2,4608]{1,0:T(2,128)(2,1)S(1)} %copy-done, bf16[2,3584]{1,0:T(2,128)(2,1)S(1)} %copy-done.1), custom_call_target="tpu_custom_call" | custom-call | tf_op jit(solution)/shard_map/pallas_call | solution.py:56
  4.0 7.3 %all-to-all-start = ((bf16[8,2,8320]{2,1,0:T(2,128)(2,1)}), bf16[8,2,8320]{2,1,0:T(2,128)(2,1)S(1)}, u32[]{:S(2)}, u32[]{:S(2)}) async-start(bf16[8,2,8320]{2,1,0:T(2,128)(2,1)} %shard_map.76), calls=%async_computation | async-start | bytes 532480 | tf_op jit(solution)/shard_map/all_to_all | solution.py:28
  11.3 1.7 %pad_maximum_fusion.heads_ref = bf16[8192,128]{1,0:T(8,128)(2,1)S(1)} fusion(bf16[3584,128]{1,0:T(8,128)(2,1)} %param.8, bf16[4608,128]{1,0:T(8,128)(2,1)} %param.7), kind=kLoop, calls=%fused_computation | loop fusion | flops 4194304 | bytes 4194304 | tf_op jit(solution)/shard_map/concatenate | solution.py:261
  12.9 7.3 %all-to-all-done.rows_ref = bf16[8,2,8320]{2,1,0:T(2,128)(2,1)S(1)} async-done(((bf16[8,2,8320]{2,1,0:T(2,128)(2,1)}), bf16[8,2,8320]{2,1,0:T(2,128)(2,1)S(1)}, u32[]{:S(2)}, u32[]{:S(2)}) %all-to-all-start) | async-done | bytes 266272 | tf_op jit(solution)/shard_map/all_to_all | solution.py:28
  20.3 2.1 %shard_map.77 = (bf16[8,8,2816]{2,1,0:T(8,128)(2,1)}, f32[16,128]{1,0:T(8,128)S(1)}, f32[16,128]{1,0:T(8,128)S(1)}, f32[16,128]{1,0:T(8,128)S(1)}) custom-call(s32[1]{0:T(128)} %bitcast.first_ref, bf16[8,2,8320]{2,1,0:T(2,128)(2,1)S(1)} %all-to-all-done.rows_ref, bf16[8192,128]{1,0:T(8,128)(2,1)S(1)} %pad_maximum_fusion.heads_ref), custom_call_target="tpu_custom_call" | custom-call | tf_op jit(solution)/shard_map/pallas_call | solution.py:255
  22.4 3.6 %all-to-all-start.1 = ((bf16[8,8,2816]{2,1,0:T(8,128)(2,1)}), bf16[8,8,2816]{2,1,0:T(8,128)(2,1)S(1)}, u32[]{:S(2)}, u32[]{:S(2)}) async-start(bf16[8,8,2816]{2,1,0:T(8,128)(2,1)} %get-tuple-element.9), calls=%async_computation.1 | async-start | bytes 720896 | tf_op jit(solution)/shard_map/all_to_all | solution.py:28
  26.0 0.1 slice.12
  26.1 0.1 collective-permute-start
  26.2 10.5 %all-to-all-done.1.arrived_ref = bf16[8,8,2816]{2,1,0:T(8,128)(2,1)S(1)} async-done(((bf16[8,8,2816]{2,1,0:T(8,128)(2,1)}), bf16[8,8,2816]{2,1,0:T(8,128)(2,1)S(1)}, u32[]{:S(2)}, u32[]{:S(2)}) %all-to-all-start.1) | async-done | bytes 360480 | tf_op jit(solution)/shard_map/all_to_all | solution.py:28
  36.7 0.3 shard_map.79
  37.0 0.1 collective-permute-start.1
  37.1 1.2 %shard_map.78 = (f32[2,3584]{1,0:T(2,128)}, f32[1,128]{1,0:T(1,128)S(1)}) custom-call(bf16[8,8,2816]{2,1,0:T(8,128)(2,1)S(1)} %all-to-all-done.1.arrived_ref), custom_call_target="tpu_custom_call" | custom-call | tf_op jit(solution)/shard_map/pallas_call | solution.py:271
  38.3 0.5 %slice_bitcast_fusion = f32[2]{0:T(128)} fusion(f32[1,128]{1,0:T(1,128)S(1)} %get-tuple-element.10), kind=kLoop, calls=%fused_computation.8 | loop fusion | bytes 16 | tf_op jit(solution)/shard_map/squeeze | solution.py:278
  38.8 0.0 collective-permute-done
  38.8 0.0 collective-permute-done.1
  38.8 1.7 %fusion = f32[3584,128]{1,0:T(8,128)} fusion(bf16[16,3584]{1,0:T(8,128)(2,1)S(1)} %collective-permute-done, bf16[16,3584]{1,0:T(8,128)(2,1)S(1)} %reshape.9, bf16[16,128]{1,0:T(8,128)(2,1)S(1)} %collective-permute-done.1, bf16[16,128]{1,0:T(8,128)(2,1)S(1)} %shard_map.79), kind=kOutput, calls=%fused_computation.1 | convolution fusion | flops 29835264 | bytes 2072576 | tf_op jit(solution)/shard_map/dot_general | solution.py:279
  (2 shorter events, 0.0 us)
Async XLA Ops:
  0.6 0.7 %copy-start = (bf16[2,4608]{1,0:T(2,128)(2,1)S(1)}, bf16[2,4608]{1,0:T(2,128)(2,1)}, u32[]{:S(2)}) copy-start(bf16[2,4608]{1,0:T(2,128)(2,1)} %teacher_ref.1) | copy-start | bytes 55300
  1.4 0.7 %copy-start.1 = (bf16[2,3584]{1,0:T(2,128)(2,1)S(1)}, bf16[2,3584]{1,0:T(2,128)(2,1)}, u32[]{:S(2)}) copy-start(bf16[2,3584]{1,0:T(2,128)(2,1)} %student_ref.1) | copy-start | bytes 43012
  2.1 0.7 %copy-start.2 = (s32[2]{0:T(128)S(1)}, s32[2]{0:T(128)}, u32[]{:S(2)}) copy-start(s32[2]{0:T(128)} %labels_ref.1) | copy-start | bytes 28
  4.0 16.3 %all-to-all-start = ((bf16[8,2,8320]{2,1,0:T(2,128)(2,1)}), bf16[8,2,8320]{2,1,0:T(2,128)(2,1)S(1)}, u32[]{:S(2)}, u32[]{:S(2)}) async-start(bf16[8,2,8320]{2,1,0:T(2,128)(2,1)} %shard_map.76), calls=%async_computation | async-start | bytes 532480 | tf_op jit(solution)/shard_map/all_to_all | solution.py:28
  22.4 14.3 %all-to-all-start.1 = ((bf16[8,8,2816]{2,1,0:T(8,128)(2,1)}), bf16[8,8,2816]{2,1,0:T(8,128)(2,1)S(1)}, u32[]{:S(2)}, u32[]{:S(2)}) async-start(bf16[8,8,2816]{2,1,0:T(8,128)(2,1)} %get-tuple-element.9), calls=%async_computation.1 | async-start | bytes 720896 | tf_op jit(solution)/shard_map/all_to_all | solution.py:28
  26.1 12.7 %collective-permute-start = (bf16[16,3584]{1,0:T(8,128)(2,1)S(1)}, bf16[16,3584]{1,0:T(8,128)(2,1)S(1)}, u32[]{:S(2)}, u32[]{:S(2)}) collective-permute-start(bf16[16,3584]{1,0:T(8,128)(2,1)S(1)} %reshape.9), channel_id=1, source_target_pairs={{0,1},{1,0},{2,3},{3,2},{4,5},{5,4},{6,7},{7,6},{8,9},{9,8},{10,11... | collective-permute-start | bytes 344072 | tf_op jit(solution)/shard_map/ppermute | solution.py:252
  37.0 1.8 %collective-permute-start.1 = (bf16[16,128]{1,0:T(8,128)(2,1)S(1)}, bf16[16,128]{1,0:T(8,128)(2,1)S(1)}, u32[]{:S(2)}, u32[]{:S(2)}) collective-permute-start(bf16[16,128]{1,0:T(8,128)(2,1)S(1)} %shard_map.79), channel_id=1, source_target_pairs={{0,1},{1,0},{2,3},{3,2},{4,5},{5,4},{6,7},{7,6},{8,9},{9,8},{10,11... | collective-permute-start | bytes 12296 | tf_op jit(solution)/shard_map/ppermute | solution.py:270

commit v10 on v9

--- a/solution.py
+++ b/solution.py
@@ -11,6 +11,7 @@
 
 
 UNROLL = 16
+PIECES = 4
 SMEM = pl.BlockSpec(memory_space=pltpu.SMEM)
 VMEM = pl.BlockSpec(memory_space=pltpu.VMEM)
 SMALL = pltpu.CompilerParams(vmem_limit_bytes=16 * 1024 * 1024)
@@ -58,7 +59,6 @@
         out_shape=jax.ShapeDtypeStruct((shards, own, teacher_width + student_width + CODE), BF16),
         in_specs=[SMEM, VMEM, VMEM],
         out_specs=VMEM,
-        compiler_params=SMALL,
     )(labels, teacher_hidden, student_hidden)
     return swap(payload)
 
@@ -213,9 +213,9 @@
     picked = jnp.sum(stats[5], axis=0)
     picked_t = jnp.sum(stats[6], axis=0)
     loss = cross / mass_t - top_t - jnp.log(mass_t) + 2.0 * (top_s + jnp.log(mass_s)) - picked
-    square = (8, 128)
-    same = lax.broadcasted_iota(jnp.int32, square, 0) == lax.broadcasted_iota(jnp.int32, square, 1)
-    loss_ref[...] = jnp.sum(jnp.where(same, loss, 0.0), axis=0, keepdims=True)
+    token = lax.broadcasted_iota(jnp.int32, (8, 1), 0)
+    for t in range(out_ref.shape[0]):
+        loss_ref[t] = jnp.sum(jnp.where(token == t, loss, 0.0))
     label_grad = 2.0 * (jnp.exp(picked - top_s) / mass_s) - jnp.exp(picked_t - top_t) / mass_t - 1.0
     rounding = label_grad.astype(BF16).astype(F32) - label_grad
     weight_s = factor_s / mass_s
@@ -239,6 +239,19 @@
     out_ref[:, 3 * quarter :] = last[6:8]
 
 
+def head_grad_kernel(hidden_ref, grad_ref, other_ref, out_ref, total_ref, sems):
+    grads = jnp.concatenate([grad_ref[...], other_ref[...]], axis=0)
+    size = hidden_ref.shape[0] // PIECES
+    copies = []
+    for piece in range(PIECES):
+        rows = pl.ds(piece * size, size)
+        total_ref[rows, :] = jnp.dot(hidden_ref[rows, :], grads, preferred_element_type=F32)
+        copies.append(pltpu.make_async_copy(total_ref.at[rows, :], out_ref.at[rows, :], sems.at[piece]))
+        copies[-1].start()
+    for copy in copies:
+        copy.wait()
+
+
 def two_exchanges(teacher_hidden, student_hidden, teacher_head, student_head, labels, *, shards):
     own = labels.shape[0]
     teacher_width, width = teacher_hidden.shape[1], student_hidden.shape[1]
@@ -268,20 +281,21 @@
         compiler_params=SMALL,
     )(arrived[:, :, 3 * quarter :], teacher_logits, student_logits, target)
     grad_other = lax.ppermute(grad_rows, "rows", other)
-    hidden_grad, loss = pl.pallas_call(
+    hidden_grad, token_loss = pl.pallas_call(
         owner_kernel,
-        out_shape=(jax.ShapeDtypeStruct((own, width), F32), jax.ShapeDtypeStruct((1, 128), F32)),
+        out_shape=(jax.ShapeDtypeStruct((own, width), F32), jax.ShapeDtypeStruct((own,), F32)),
         in_specs=[VMEM],
-        out_specs=(VMEM, VMEM),
+        out_specs=(VMEM, SMEM),
         compiler_params=SMALL,
     )(arrived)
-    token_loss = loss[0, :own]
-    head_grad = lax.dot_general(
-        jnp.concatenate([student_rows, student_other], axis=0),
-        jnp.concatenate([grad_rows, grad_other], axis=0),
-        (((0,), (0,)), ((), ())),
-        preferred_element_type=F32,
-    )
+    head_grad = pl.pallas_call(
+        head_grad_kernel,
+        out_shape=jax.ShapeDtypeStruct((width, columns_here), F32),
+        in_specs=[VMEM] * 3,
+        out_specs=pl.BlockSpec(memory_space=pl.ANY),
+        scratch_shapes=[pltpu.VMEM((width, columns_here), F32), pltpu.SemaphoreType.DMA((PIECES,))],
+        compiler_params=SMALL,
+    )(jnp.concatenate([student_rows, student_other], axis=0).T, grad_rows, grad_other)
     return (token_loss, hidden_grad, head_grad)
 
 

time: 41 us -> 38.9 us (0.949)
  local copies, waits for them, and re-layouts: 2.72 us -> 0.55 us
  Pallas kernels: 4.97 us -> 6.7 us
  matrix products: 1.69 us -> 0 us
    unnamed x6 -> x0, local copies, waits for them, and re-layouts: 2.08 us -> none
    dot_general x1 -> x0, matrix products: 1.69 us -> none  [two_exchanges(): lax.dot_general(jnp.concatenate([student_rows, student_other], axis=0), j...]
    pallas_call x0 -> x1, Pallas kernels: none -> 1.5 us  [two_exchanges(): pl.pallas_call(head_grad_kernel, out_shape=jax.ShapeDtypeStruct((width, c...]
    squeeze x1 -> x0, local copies, waits for them, and re-layouts: 0.51 us -> none  [two_exchanges(): token_loss = loss[0, :own]]
    concatenate x0 -> x1, local copies, waits for them, and re-layouts: none -> 0.42 us  [two_exchanges(): jnp.concatenate([student_rows, student_other], axis=0)]
where the time goes in v10:
time: 38.9 us; the launch traced here: 38.4 us
  waiting for transfers between devices  17.8 us (46%)
  starting transfers between devices  11 us (28%)
  Pallas kernels  6.7 us (17%)
  other arithmetic  1.7 us (4%)
  between operations  0.71 us (2%)
  local copies, waits for them, and re-layouts  0.55 us (1%)
    all_to_all x2, waiting for transfers between devices, swap(): lax.all_to_all(blocks, 'vocab', split_axis=0, concat_axis=0, tiled=True)  17.8 us
    all_to_all x2, starting transfers between devices, swap(): lax.all_to_all(blocks, 'vocab', split_axis=0, concat_axis=0, tiled=True)  10.8 us
    pallas_call x1, Pallas kernels, two_exchanges(): pl.pallas_call(raw_partial_kernel, out_shape=(jax.ShapeDtypeStruct((shard...  2.15 us
    concatenate x1, other arithmetic, two_exchanges(): jnp.concatenate([teacher_head, student_head], axis=0)  1.69 us
    pallas_call x1, Pallas kernels, two_exchanges(): pl.pallas_call(head_grad_kernel, out_shape=jax.ShapeDtypeStruct((width, c...  1.5 us
    pallas_call x1, Pallas kernels, gather_tokens(): pl.pallas_call(payload_kernel, out_shape=jax.ShapeDtypeStruct((shards, ow...  1.48 us
    pallas_call x1, Pallas kernels, two_exchanges(): pl.pallas_call(owner_kernel, out_shape=(jax.ShapeDtypeStruct((own, width)...  1.26 us
  transfers between devices with their start and end apart: 4, of which 2 were waited for; matrix products, arithmetic and copies ran while one was open for 6% of the time, Pallas kernels for 4%

profile of v10, /device:TPU:0, one launch (start us, length us, event | category | flops | bytes accessed | tf_op | source)
XLA Modules:
  0.0 38.4 jit_solution(9737443342054538569)
XLA Ops:
  0.6 1.5 %shard_map.76 = bf16[8,2,8320]{2,1,0:T(2,128)(2,1)} custom-call(s32[2]{0:T(128)} %labels_ref.1, bf16[2,4608]{1,0:T(2,128)(2,1)} %teacher_ref.1, bf16[2,3584]{1,0:T(2,128)(2,1)} %student_ref.1), custom_call_target="tpu_custom_call" | custom-call | tf_op jit(solution)/shard_map/pallas_call | solution.py:57
  2.1 7.3 %all-to-all-start = ((bf16[8,2,8320]{2,1,0:T(2,128)(2,1)}), bf16[8,2,8320]{2,1,0:T(2,128)(2,1)S(1)}, u32[]{:S(2)}, u32[]{:S(2)}) async-start(bf16[8,2,8320]{2,1,0:T(2,128)(2,1)} %shard_map.76), calls=%async_computation | async-start | bytes 532480 | tf_op jit(solution)/shard_map/all_to_all | solution.py:29
  9.4 1.7 %pad_maximum_fusion.heads_ref = bf16[8192,128]{1,0:T(8,128)(2,1)S(1)} fusion(bf16[3584,128]{1,0:T(8,128)(2,1)} %param.8, bf16[4608,128]{1,0:T(8,128)(2,1)} %param.7), kind=kLoop, calls=%fused_computation | loop fusion | flops 4194304 | bytes 4194304 | tf_op jit(solution)/shard_map/concatenate | solution.py:274
  11.1 7.3 %all-to-all-done.rows_ref = bf16[8,2,8320]{2,1,0:T(2,128)(2,1)S(1)} async-done(((bf16[8,2,8320]{2,1,0:T(2,128)(2,1)}), bf16[8,2,8320]{2,1,0:T(2,128)(2,1)S(1)}, u32[]{:S(2)}, u32[]{:S(2)}) %all-to-all-start) | async-done | bytes 266272 | tf_op jit(solution)/shard_map/all_to_all | solution.py:29
  18.4 2.1 %shard_map.77 = (bf16[8,8,2816]{2,1,0:T(8,128)(2,1)}, f32[16,128]{1,0:T(8,128)S(1)}, f32[16,128]{1,0:T(8,128)S(1)}, f32[16,128]{1,0:T(8,128)S(1)}) custom-call(s32[1]{0:T(128)} %bitcast.first_ref, bf16[8,2,8320]{2,1,0:T(2,128)(2,1)S(1)} %all-to-all-done.rows_ref, bf16[8192,128]{1,0:T(8,128)(2,1)S(1)} %pad_maximum_fusion.heads_ref), custom_call_target="tpu_custom_call" | custom-call | tf_op jit(solution)/shard_map/pallas_call | solution.py:268
  20.5 3.6 %all-to-all-start.1 = ((bf16[8,8,2816]{2,1,0:T(8,128)(2,1)}), bf16[8,8,2816]{2,1,0:T(8,128)(2,1)S(1)}, u32[]{:S(2)}, u32[]{:S(2)}) async-start(bf16[8,8,2816]{2,1,0:T(8,128)(2,1)} %get-tuple-element.9), calls=%async_computation.1 | async-start | bytes 720896 | tf_op jit(solution)/shard_map/all_to_all | solution.py:29
  24.1 0.1 slice.8
  24.2 0.1 collective-permute-start
  24.3 10.5 %all-to-all-done.1.arrived_ref = bf16[8,8,2816]{2,1,0:T(8,128)(2,1)S(1)} async-done(((bf16[8,8,2816]{2,1,0:T(8,128)(2,1)}), bf16[8,8,2816]{2,1,0:T(8,128)(2,1)S(1)}, u32[]{:S(2)}, u32[]{:S(2)}) %all-to-all-start.1) | async-done | bytes 360480 | tf_op jit(solution)/shard_map/all_to_all | solution.py:29
  34.8 0.3 shard_map.79.grad_ref
  35.1 0.1 collective-permute-start.1
  35.2 0.0 collective-permute-done
  35.2 0.4 %copy.11 = bf16[32,3584]{0,1:T(8,128)(2,1)S(1)} copy(bf16[32,3584]{1,0:T(8,128)(2,1)S(1)} %pad_maximum_fusion.1) | data formatting | bytes 458752 | tf_op jit(solution)/shard_map/concatenate | solution.py:298
  35.6 1.3 %shard_map.78 = (f32[2,3584]{1,0:T(2,128)}, f32[2]{0:T(128)}) custom-call(bf16[8,8,2816]{2,1,0:T(8,128)(2,1)S(1)} %all-to-all-done.1.arrived_ref), custom_call_target="tpu_custom_call" | custom-call | tf_op jit(solution)/shard_map/pallas_call | solution.py:284
  36.9 0.0 collective-permute-done.1.other_ref
  36.9 1.5 %shard_map.80 = f32[3584,128]{1,0:T(8,128)} custom-call(bf16[3584,32]{1,0:T(8,128)(2,1)S(1)} %bitcast.2, bf16[16,128]{1,0:T(8,128)(2,1)S(1)} %shard_map.79.grad_ref, bf16[16,128]{1,0:T(8,128)(2,1)S(1)} %collective-permute-done.1.other_ref), custom_call_target="tpu_custom_call" | custom-call | tf_op jit(solution)/shard_map/pallas_call | solution.py:291
  (3 shorter events, 0.1 us)
Async XLA Ops:
  2.1 16.3 %all-to-all-start = ((bf16[8,2,8320]{2,1,0:T(2,128)(2,1)}), bf16[8,2,8320]{2,1,0:T(2,128)(2,1)S(1)}, u32[]{:S(2)}, u32[]{:S(2)}) async-start(bf16[8,2,8320]{2,1,0:T(2,128)(2,1)} %shard_map.76), calls=%async_computation | async-start | bytes 532480 | tf_op jit(solution)/shard_map/all_to_all | solution.py:29
  20.5 14.3 %all-to-all-start.1 = ((bf16[8,8,2816]{2,1,0:T(8,128)(2,1)}), bf16[8,8,2816]{2,1,0:T(8,128)(2,1)S(1)}, u32[]{:S(2)}, u32[]{:S(2)}) async-start(bf16[8,8,2816]{2,1,0:T(8,128)(2,1)} %get-tuple-element.9), calls=%async_computation.1 | async-start | bytes 720896 | tf_op jit(solution)/shard_map/all_to_all | solution.py:29
  24.2 10.9 %collective-permute-start = (bf16[16,3584]{1,0:T(8,128)(2,1)S(1)}, bf16[16,3584]{1,0:T(8,128)(2,1)S(1)}, u32[]{:S(2)}, u32[]{:S(2)}) collective-permute-start(bf16[16,3584]{1,0:T(8,128)(2,1)S(1)} %reshape.9), channel_id=1, source_target_pairs={{0,1},{1,0},{2,3},{3,2},{4,5},{5,4},{6,7},{7,6},{8,9},{9,8},{10,11... | collective-permute-start | bytes 344072 | tf_op jit(solution)/shard_map/ppermute | solution.py:265
  35.1 1.8 %collective-permute-start.1 = (bf16[16,128]{1,0:T(8,128)(2,1)S(1)}, bf16[16,128]{1,0:T(8,128)(2,1)S(1)}, u32[]{:S(2)}, u32[]{:S(2)}) collective-permute-start(bf16[16,128]{1,0:T(8,128)(2,1)S(1)} %shard_map.79.grad_ref), channel_id=1, source_target_pairs={{0,1},{1,0},{2,3},{3,2},{4,5},{5,4},{6,7},{7,6},{8,9},{9,8},{10,11... | collective-permute-start | bytes 12296 | tf_op jit(solution)/shard_map/ppermute | solution.py:283

commit v11 on v10

--- a/solution.py
+++ b/solution.py
@@ -14,6 +14,7 @@
 PIECES = 4
 SMEM = pl.BlockSpec(memory_space=pltpu.SMEM)
 VMEM = pl.BlockSpec(memory_space=pltpu.VMEM)
+ANY = pl.BlockSpec(memory_space=pl.ANY)
 SMALL = pltpu.CompilerParams(vmem_limit_bytes=16 * 1024 * 1024)
 
 
@@ -32,6 +33,19 @@
 def payload_kernel(labels_ref, teacher_ref, student_ref, out_ref):
     shards, own, _ = out_ref.shape
     teacher_width, student_width = teacher_ref.shape[1], student_ref.shape[1]
+    teacher = teacher_ref[...]
+    student = student_ref[...]
+    code = label_digits(labels_ref, own)
+
+    def write(shard):
+        out_ref[shard, :, :teacher_width] = teacher
+        out_ref[shard, :, teacher_width : teacher_width + student_width] = student
+        out_ref[shard, :, teacher_width + student_width :] = code
+
+    over_shards(shards, write)
+
+
+def label_digits(labels_ref, own):
     row = lax.broadcasted_iota(jnp.int32, (own, CODE), 0)
     lane = lax.broadcasted_iota(jnp.int32, (own, CODE), 1)
     digits = jnp.zeros((own, CODE), jnp.int32)
@@ -39,31 +53,61 @@
         label = labels_ref[token]
         pair = jnp.where(lane == 0, label >> 7, label & 127)
         digits = jnp.where(row == token, pair, digits)
-    teacher = teacher_ref[...]
-    student = student_ref[...]
-    code = digits.astype(F32).astype(BF16)
-
-    def write(shard):
-        out_ref[shard, :, :teacher_width] = teacher
-        out_ref[shard, :, teacher_width : teacher_width + student_width] = student
-        out_ref[shard, :, teacher_width + student_width :] = code
-
-    over_shards(shards, write)
+    return digits.astype(F32).astype(BF16)
+
+
+def payload_copy_kernel(labels_hbm, teacher_hbm, student_hbm, out_hbm, labels_ref, code_ref, label_sem, sems):
+    shards, own, _ = out_hbm.shape
+    teacher_width, width = teacher_hbm.shape[1], student_hbm.shape[1]
+    labels_in = pltpu.make_async_copy(labels_hbm, labels_ref, label_sem)
+    labels_in.start()
+    copies = []
+
+    def copy_out(source, start, size):
+        for shard in range(shards):
+            target = out_hbm.at[shard, :, pl.ds(start, size)]
+            copies.append(pltpu.make_async_copy(source, target, sems.at[len(copies)]))
+            copies[-1].start()
+
+    copy_out(teacher_hbm, 0, teacher_width)
+    copy_out(student_hbm, teacher_width, width)
+    labels_in.wait()
+    code_ref[...] = label_digits(labels_ref, own)
+    copy_out(code_ref, teacher_width + width, CODE)
+    for copy in copies:
+        copy.wait()
 
 
 def gather_tokens(teacher_hidden, student_hidden, labels, shards):
     own, teacher_width = teacher_hidden.shape
     student_width = student_hidden.shape[1]
-    payload = pl.pallas_call(
-        payload_kernel,
-        out_shape=jax.ShapeDtypeStruct((shards, own, teacher_width + student_width + CODE), BF16),
-        in_specs=[SMEM, VMEM, VMEM],
-        out_specs=VMEM,
-    )(labels, teacher_hidden, student_hidden)
+    out_shape = jax.ShapeDtypeStruct((shards, own, teacher_width + student_width + CODE), BF16)
+    if shards <= UNROLL:
+        payload = pl.pallas_call(
+            payload_copy_kernel,
+            out_shape=out_shape,
+            in_specs=[ANY] * 3,
+            out_specs=ANY,
+            scratch_shapes=[
+                pltpu.SMEM((own,), jnp.int32),
+                pltpu.VMEM((own, CODE), BF16),
+                pltpu.SemaphoreType.DMA,
+                pltpu.SemaphoreType.DMA((3 * shards,)),
+            ],
+        )(labels, teacher_hidden, student_hidden)
+    else:
+        payload = pl.pallas_call(
+            payload_kernel,
+            out_shape=out_shape,
+            in_specs=[SMEM, VMEM, VMEM],
+            out_specs=VMEM,
+        )(labels, teacher_hidden, student_hidden)
     return swap(payload)
 
 
-def raw_partial_kernel(first_ref, rows_ref, heads_ref, out_ref, teacher_ref, student_ref, target_ref):
+def raw_partial_kernel(
+    first_ref, rows_ref, heads_ref, out_hbm, teacher_ref, student_ref, target_ref, out_ref, sems
+):
     shards, own, _ = rows_ref.shape
     tokens = shards * own
     wide = 8 * shards
@@ -77,6 +121,13 @@
 
     def dot(left, right, dims):
         return lax.dot_general(left, right, (dims, ((), ())), preferred_element_type=F32)
+
+    copies = []
+
+    def send_out(piece, start, size):
+        lanes = pl.ds(start, size)
+        copies.append(pltpu.make_async_copy(out_ref.at[:, :, lanes], out_hbm.at[:, :, lanes], sems.at[piece]))
+        copies[-1].start()
 
     def rows_of(start, size):
         return jnp.concatenate([rows_ref[shard, :, start : start + size] for shard in range(shards)], axis=0)
@@ -130,6 +181,16 @@
         picked = by_row[:, k : k + 1] + by_row[:, 8 + k : 9 + k] + by_row[:, 16 + k : 17 + k]
         return picked
 
+    lane = iota((8, 128), 1)
+    shared = jnp.zeros((8, 128), F32)
+    wide_parts = parts.astype(F32)
+    for group in range(tokens // 8):
+        shared = jnp.where(lane // 32 == group + 1, wide_parts[8 * group : 8 * group + 8], shared)
+    for shard in range(shards):
+        block = jnp.where(lane < 32, by_row[8 * shard : 8 * shard + 8], shared)
+        out_ref[shard, :, 3 * quarter :] = block.astype(BF16)
+    send_out(3, 3 * quarter, 128)
+
     members = jnp.concatenate([exp_s, exp_t, kappa * combined * total(target) - target], axis=0)
     member_high = members.astype(BF16)
     member_low = (members - member_high.astype(F32)).astype(BF16)
@@ -168,14 +229,9 @@
         sent += in_third * (pltpu.roll(scaled, 4, 0) + pltpu.roll(scaled, 2, 0))
         for shard in range(shards):
             out_ref[shard, :, j * quarter : (j + 1) * quarter] = sent[8 * shard : 8 * shard + 8].astype(BF16)
-    lane = iota((8, 128), 1)
-    shared = jnp.zeros((8, 128), F32)
-    wide_parts = parts.astype(F32)
-    for group in range(tokens // 8):
-        shared = jnp.where(lane // 32 == group + 1, wide_parts[8 * group : 8 * group + 8], shared)
-    for shard in range(shards):
-        block = jnp.where(lane < 32, by_row[8 * shard : 8 * shard + 8], shared)
-        out_ref[shard, :, 3 * quarter :] = block.astype(BF16)
+        send_out(j, j * quarter, quarter)
+    for copy in copies:
+        copy.wait()
 
 
 def sum_parts(tail):
@@ -239,13 +295,14 @@
     out_ref[:, 3 * quarter :] = last[6:8]
 
 
-def head_grad_kernel(hidden_ref, grad_ref, other_ref, out_ref, total_ref, sems):
+def head_grad_kernel(hidden_ref, hidden_other_ref, grad_ref, other_ref, out_ref, total_ref, sems):
     grads = jnp.concatenate([grad_ref[...], other_ref[...]], axis=0)
-    size = hidden_ref.shape[0] // PIECES
+    size = hidden_ref.shape[1] // PIECES
     copies = []
     for piece in range(PIECES):
         rows = pl.ds(piece * size, size)
-        total_ref[rows, :] = jnp.dot(hidden_ref[rows, :], grads, preferred_element_type=F32)
+        hidden = jnp.concatenate([hidden_ref[:, rows], hidden_other_ref[:, rows]], axis=0)
+        total_ref[rows, :] = lax.dot_general(hidden, grads, (((0,), (0,)), ((), ())), preferred_element_type=F32)
         copies.append(pltpu.make_async_copy(total_ref.at[rows, :], out_ref.at[rows, :], sems.at[piece]))
         copies[-1].start()
     for copy in copies:
@@ -269,7 +326,8 @@
         raw_partial_kernel,
         out_shape=(jax.ShapeDtypeStruct((shards, 8, 3 * quarter + 128), BF16), square, square, square),
         in_specs=[SMEM, VMEM, VMEM],
-        out_specs=(VMEM, VMEM, VMEM, VMEM),
+        out_specs=(ANY, VMEM, VMEM, VMEM),
+        scratch_shapes=[pltpu.VMEM((shards, 8, 3 * quarter + 128), BF16), pltpu.SemaphoreType.DMA((4,))],
         compiler_params=SMALL,
     )((here * columns_here)[None], rows, jnp.concatenate([teacher_head, student_head], axis=0))
     arrived = swap(payload)
@@ -291,11 +349,11 @@
     head_grad = pl.pallas_call(
         head_grad_kernel,
         out_shape=jax.ShapeDtypeStruct((width, columns_here), F32),
-        in_specs=[VMEM] * 3,
-        out_specs=pl.BlockSpec(memory_space=pl.ANY),
+        in_specs=[VMEM] * 4,
+        out_specs=ANY,
         scratch_shapes=[pltpu.VMEM((width, columns_here), F32), pltpu.SemaphoreType.DMA((PIECES,))],
         compiler_params=SMALL,
-    )(jnp.concatenate([student_rows, student_other], axis=0).T, grad_rows, grad_other)
+    )(student_rows, student_other, grad_rows, grad_other)
     return (token_loss, hidden_grad, head_grad)
 
 

time: 38.9 us -> 46.2 us (1.19)
  Pallas kernels: 6.7 us -> 14.5 us
    pallas_call x1, Pallas kernels: 1.48 us -> 9.28 us  [gather_tokens(): pl.pallas_call(payload_copy_kernel, out_shape=out_shape, in_specs=[ANY] *...]
  transfers between devices with their start and end apart: 4 -> 4, of which waited for: 2 -> 2; matrix products, arithmetic and copies ran while one was open for 6% -> 4% of each run, Pallas kernels for 4% -> 3%
where the time goes in v11:
time: 46.2 us; the launch traced here: 45.8 us
  waiting for transfers between devices  17.8 us (39%)
  Pallas kernels  14.5 us (31%)
  starting transfers between devices  11 us (24%)
  other arithmetic  1.69 us (4%)
  between operations  0.71 us (2%)
    all_to_all x2, waiting for transfers between devices, swap(): lax.all_to_all(blocks, 'vocab', split_axis=0, concat_axis=0, tiled=True)  17.7 us
    all_to_all x2, starting transfers between devices, swap(): lax.all_to_all(blocks, 'vocab', split_axis=0, concat_axis=0, tiled=True)  10.9 us
    pallas_call x1, Pallas kernels, gather_tokens(): pl.pallas_call(payload_copy_kernel, out_shape=out_shape, in_specs=[ANY] *...  9.28 us
    pallas_call x1, Pallas kernels, two_exchanges(): pl.pallas_call(raw_partial_kernel, out_shape=(jax.ShapeDtypeStruct((shard...  2.1 us
    concatenate x1, other arithmetic, two_exchanges(): jnp.concatenate([teacher_head, student_head], axis=0)  1.69 us
    pallas_call x1, Pallas kernels, two_exchanges(): pl.pallas_call(head_grad_kernel, out_shape=jax.ShapeDtypeStruct((width, c...  1.6 us
    pallas_call x1, Pallas kernels, two_exchanges(): pl.pallas_call(owner_kernel, out_shape=(jax.ShapeDtypeStruct((own, width)...  1.26 us
  transfers between devices with their start and end apart: 4, of which 2 were waited for; matrix products, arithmetic and copies ran while one was open for 4% of the time, Pallas kernels for 3%

profile of v11, /device:TPU:0, one launch (start us, length us, event | category | flops | bytes accessed | tf_op | source)
XLA Modules:
  0.0 45.8 jit_solution(13519583080668615776)
XLA Ops:
  0.6 9.3 %shard_map.76 = bf16[8,2,8320]{2,1,0:T(2,128)(2,1)} custom-call(s32[2]{0:T(128)} %labels_hbm.1, bf16[2,4608]{1,0:T(2,128)(2,1)} %teacher_hbm.1, bf16[2,3584]{1,0:T(2,128)(2,1)} %student_hbm.1), custom_call_target="tpu_custom_call" | custom-call | tf_op jit(solution)/shard_map/pallas_call | solution.py:86
  9.9 7.3 %all-to-all-start = ((bf16[8,2,8320]{2,1,0:T(2,128)(2,1)}), bf16[8,2,8320]{2,1,0:T(2,128)(2,1)S(1)}, u32[]{:S(2)}, u32[]{:S(2)}) async-start(bf16[8,2,8320]{2,1,0:T(2,128)(2,1)} %shard_map.76), calls=%async_computation | async-start | bytes 532480 | tf_op jit(solution)/shard_map/all_to_all | solution.py:30
  17.2 1.7 %pad_maximum_fusion.heads_ref = bf16[8192,128]{1,0:T(8,128)(2,1)S(1)} fusion(bf16[3584,128]{1,0:T(8,128)(2,1)} %param.8, bf16[4608,128]{1,0:T(8,128)(2,1)} %param.7), kind=kLoop, calls=%fused_computation | loop fusion | flops 4194304 | bytes 4194304 | tf_op jit(solution)/shard_map/concatenate | solution.py:332
  18.9 7.3 %all-to-all-done.rows_ref = bf16[8,2,8320]{2,1,0:T(2,128)(2,1)S(1)} async-done(((bf16[8,2,8320]{2,1,0:T(2,128)(2,1)}), bf16[8,2,8320]{2,1,0:T(2,128)(2,1)S(1)}, u32[]{:S(2)}, u32[]{:S(2)}) %all-to-all-start) | async-done | bytes 266272 | tf_op jit(solution)/shard_map/all_to_all | solution.py:30
  26.2 2.1 %shard_map.77 = (bf16[8,8,2816]{2,1,0:T(8,128)(2,1)}, f32[16,128]{1,0:T(8,128)S(1)}, f32[16,128]{1,0:T(8,128)S(1)}, f32[16,128]{1,0:T(8,128)S(1)}) custom-call(s32[1]{0:T(128)} %bitcast.first_ref, bf16[8,2,8320]{2,1,0:T(2,128)(2,1)S(1)} %all-to-all-done.rows_ref, bf16[8192,128]{1,0:T(8,128)(2,1)S(1)} %pad_maximum_fusion.heads_ref), custom_call_target="tpu_custom_call" | custom-call | tf_op jit(solution)/shard_map/pallas_call | solution.py:325
  28.3 3.6 %all-to-all-start.1 = ((bf16[8,8,2816]{2,1,0:T(8,128)(2,1)}), bf16[8,8,2816]{2,1,0:T(8,128)(2,1)S(1)}, u32[]{:S(2)}, u32[]{:S(2)}) async-start(bf16[8,8,2816]{2,1,0:T(8,128)(2,1)} %get-tuple-element.9), calls=%async_computation.1 | async-start | bytes 720896 | tf_op jit(solution)/shard_map/all_to_all | solution.py:30
  31.9 0.1 slice.8
  32.0 0.1 collective-permute-start
  32.1 10.4 %all-to-all-done.1.arrived_ref = bf16[8,8,2816]{2,1,0:T(8,128)(2,1)S(1)} async-done(((bf16[8,8,2816]{2,1,0:T(8,128)(2,1)}), bf16[8,8,2816]{2,1,0:T(8,128)(2,1)S(1)}, u32[]{:S(2)}, u32[]{:S(2)}) %all-to-all-start.1) | async-done | bytes 360480 | tf_op jit(solution)/shard_map/all_to_all | solution.py:30
  42.6 0.3 shard_map.79.grad_ref
  42.9 0.1 collective-permute-start.1
  43.0 1.3 %shard_map.78 = (f32[2,3584]{1,0:T(2,128)}, f32[2]{0:T(128)}) custom-call(bf16[8,8,2816]{2,1,0:T(8,128)(2,1)S(1)} %all-to-all-done.1.arrived_ref), custom_call_target="tpu_custom_call" | custom-call | tf_op jit(solution)/shard_map/pallas_call | solution.py:342
  44.2 0.0 collective-permute-done.hidden_other_ref
  44.2 0.0 collective-permute-done.1.other_ref
  44.2 1.6 %shard_map.80 = f32[3584,128]{1,0:T(8,128)} custom-call(bf16[16,3584]{1,0:T(8,128)(2,1)S(1)} %reshape.9.hidden_ref, bf16[16,3584]{1,0:T(8,128)(2,1)S(1)} %collective-permute-done.hidden_other_ref, bf16[16,128]{1,0:T(8,128)(2,1)S(1)} %shard_map.79.grad_ref, bf16[16,128]{1,0:T(8,128)(2,1)S(1)} %collective-permute-done.1.other_ref), custom_call_target="tpu_custom_call" | custom-call | tf_op jit(solution)/shard_map/pallas_call | solution.py:349
  (2 shorter events, 0.0 us)
Async XLA Ops:
  9.9 16.3 %all-to-all-start = ((bf16[8,2,8320]{2,1,0:T(2,128)(2,1)}), bf16[8,2,8320]{2,1,0:T(2,128)(2,1)S(1)}, u32[]{:S(2)}, u32[]{:S(2)}) async-start(bf16[8,2,8320]{2,1,0:T(2,128)(2,1)} %shard_map.76), calls=%async_computation | async-start | bytes 532480 | tf_op jit(solution)/shard_map/all_to_all | solution.py:30
  28.3 14.3 %all-to-all-start.1 = ((bf16[8,8,2816]{2,1,0:T(8,128)(2,1)}), bf16[8,8,2816]{2,1,0:T(8,128)(2,1)S(1)}, u32[]{:S(2)}, u32[]{:S(2)}) async-start(bf16[8,8,2816]{2,1,0:T(8,128)(2,1)} %get-tuple-element.9), calls=%async_computation.1 | async-start | bytes 720896 | tf_op jit(solution)/shard_map/all_to_all | solution.py:30
  32.0 12.2 %collective-permute-start = (bf16[16,3584]{1,0:T(8,128)(2,1)S(1)}, bf16[16,3584]{1,0:T(8,128)(2,1)S(1)}, u32[]{:S(2)}, u32[]{:S(2)}) collective-permute-start(bf16[16,3584]{1,0:T(8,128)(2,1)S(1)} %reshape.9.hidden_ref), channel_id=1, source_target_pairs={{0,1},{1,0},{2,3},{3,2},{4,5},{5,4},{6,7},{7,6},{8,9},{9,8},{10,11... | collective-permute-start | bytes 344072 | tf_op jit(solution)/shard_map/ppermute | solution.py:322
  42.9 1.4 %collective-permute-start.1 = (bf16[16,128]{1,0:T(8,128)(2,1)S(1)}, bf16[16,128]{1,0:T(8,128)(2,1)S(1)}, u32[]{:S(2)}, u32[]{:S(2)}) collective-permute-start(bf16[16,128]{1,0:T(8,128)(2,1)S(1)} %shard_map.79.grad_ref), channel_id=1, source_target_pairs={{0,1},{1,0},{2,3},{3,2},{4,5},{5,4},{6,7},{7,6},{8,9},{9,8},{10,11... | collective-permute-start | bytes 12296 | tf_op jit(solution)/shard_map/ppermute | solution.py:341

commit v12 on v11

--- a/solution.py
+++ b/solution.py
@@ -11,7 +11,7 @@
 
 
 UNROLL = 16
-PIECES = 4
+PIECES = 7
 SMEM = pl.BlockSpec(memory_space=pltpu.SMEM)
 VMEM = pl.BlockSpec(memory_space=pltpu.VMEM)
 ANY = pl.BlockSpec(memory_space=pl.ANY)
@@ -56,52 +56,15 @@
     return digits.astype(F32).astype(BF16)
 
 
-def payload_copy_kernel(labels_hbm, teacher_hbm, student_hbm, out_hbm, labels_ref, code_ref, label_sem, sems):
-    shards, own, _ = out_hbm.shape
-    teacher_width, width = teacher_hbm.shape[1], student_hbm.shape[1]
-    labels_in = pltpu.make_async_copy(labels_hbm, labels_ref, label_sem)
-    labels_in.start()
-    copies = []
-
-    def copy_out(source, start, size):
-        for shard in range(shards):
-            target = out_hbm.at[shard, :, pl.ds(start, size)]
-            copies.append(pltpu.make_async_copy(source, target, sems.at[len(copies)]))
-            copies[-1].start()
-
-    copy_out(teacher_hbm, 0, teacher_width)
-    copy_out(student_hbm, teacher_width, width)
-    labels_in.wait()
-    code_ref[...] = label_digits(labels_ref, own)
-    copy_out(code_ref, teacher_width + width, CODE)
-    for copy in copies:
-        copy.wait()
-
-
 def gather_tokens(teacher_hidden, student_hidden, labels, shards):
     own, teacher_width = teacher_hidden.shape
     student_width = student_hidden.shape[1]
-    out_shape = jax.ShapeDtypeStruct((shards, own, teacher_width + student_width + CODE), BF16)
-    if shards <= UNROLL:
-        payload = pl.pallas_call(
-            payload_copy_kernel,
-            out_shape=out_shape,
-            in_specs=[ANY] * 3,
-            out_specs=ANY,
-            scratch_shapes=[
-                pltpu.SMEM((own,), jnp.int32),
-                pltpu.VMEM((own, CODE), BF16),
-                pltpu.SemaphoreType.DMA,
-                pltpu.SemaphoreType.DMA((3 * shards,)),
-            ],
-        )(labels, teacher_hidden, student_hidden)
-    else:
-        payload = pl.pallas_call(
-            payload_kernel,
-            out_shape=out_shape,
-            in_specs=[SMEM, VMEM, VMEM],
-            out_specs=VMEM,
-        )(labels, teacher_hidden, student_hidden)
+    payload = pl.pallas_call(
+        payload_kernel,
+        out_shape=jax.ShapeDtypeStruct((shards, own, teacher_width + student_width + CODE), BF16),
+        in_specs=[SMEM, VMEM, VMEM],
+        out_specs=VMEM,
+    )(labels, teacher_hidden, student_hidden)
     return swap(payload)
 
 

time: 46.2 us -> 38.4 us (0.83)
  Pallas kernels: 14.5 us -> 6.69 us
    pallas_call x1, Pallas kernels: 9.28 us -> 1.48 us  [gather_tokens(): pl.pallas_call(payload_kernel, out_shape=jax.ShapeDtypeStruct((shards, ow...]
  transfers between devices with their start and end apart: 4 -> 4, of which waited for: 2 -> 2; matrix products, arithmetic and copies ran while one was open for 4% -> 5% of each run, Pallas kernels for 3% -> 4%
where the time goes in v12:
time: 38.4 us; the launch traced here: 38 us
  waiting for transfers between devices  17.8 us (46%)
  starting transfers between devices  11 us (29%)
  Pallas kernels  6.69 us (17%)
  other arithmetic  1.69 us (4%)
  between operations  0.7 us (2%)
    all_to_all x2, waiting for transfers between devices, swap(): lax.all_to_all(blocks, 'vocab', split_axis=0, concat_axis=0, tiled=True)  17.8 us
    all_to_all x2, starting transfers between devices, swap(): lax.all_to_all(blocks, 'vocab', split_axis=0, concat_axis=0, tiled=True)  10.8 us
    pallas_call x1, Pallas kernels, two_exchanges(): pl.pallas_call(raw_partial_kernel, out_shape=(jax.ShapeDtypeStruct((shard...  2.11 us
    concatenate x1, other arithmetic, two_exchanges(): jnp.concatenate([teacher_head, student_head], axis=0)  1.69 us
    pallas_call x1, Pallas kernels, two_exchanges(): pl.pallas_call(head_grad_kernel, out_shape=jax.ShapeDtypeStruct((width, c...  1.54 us
    pallas_call x1, Pallas kernels, gather_tokens(): pl.pallas_call(payload_kernel, out_shape=jax.ShapeDtypeStruct((shards, ow...  1.48 us
    pallas_call x1, Pallas kernels, two_exchanges(): pl.pallas_call(owner_kernel, out_shape=(jax.ShapeDtypeStruct((own, width)...  1.26 us
  transfers between devices with their start and end apart: 4, of which 2 were waited for; matrix products, arithmetic and copies ran while one was open for 5% of the time, Pallas kernels for 4%

profile of v12, /device:TPU:0, one launch (start us, length us, event | category | flops | bytes accessed | tf_op | source)
XLA Modules:
  0.0 38.0 jit_solution(12925644158582821729)
XLA Ops:
  0.6 1.5 %shard_map.76 = bf16[8,2,8320]{2,1,0:T(2,128)(2,1)} custom-call(s32[2]{0:T(128)} %labels_ref.1, bf16[2,4608]{1,0:T(2,128)(2,1)} %teacher_ref.1, bf16[2,3584]{1,0:T(2,128)(2,1)} %student_ref.1), custom_call_target="tpu_custom_call" | custom-call | tf_op jit(solution)/shard_map/pallas_call | solution.py:62
  2.1 7.3 %all-to-all-start = ((bf16[8,2,8320]{2,1,0:T(2,128)(2,1)}), bf16[8,2,8320]{2,1,0:T(2,128)(2,1)S(1)}, u32[]{:S(2)}, u32[]{:S(2)}) async-start(bf16[8,2,8320]{2,1,0:T(2,128)(2,1)} %shard_map.76), calls=%async_computation | async-start | bytes 532480 | tf_op jit(solution)/shard_map/all_to_all | solution.py:30
  9.4 1.7 %pad_maximum_fusion.heads_ref = bf16[8192,128]{1,0:T(8,128)(2,1)S(1)} fusion(bf16[3584,128]{1,0:T(8,128)(2,1)} %param.8, bf16[4608,128]{1,0:T(8,128)(2,1)} %param.7), kind=kLoop, calls=%fused_computation | loop fusion | flops 4194304 | bytes 4194304 | tf_op jit(solution)/shard_map/concatenate | solution.py:295
  11.1 7.3 %all-to-all-done.rows_ref = bf16[8,2,8320]{2,1,0:T(2,128)(2,1)S(1)} async-done(((bf16[8,2,8320]{2,1,0:T(2,128)(2,1)}), bf16[8,2,8320]{2,1,0:T(2,128)(2,1)S(1)}, u32[]{:S(2)}, u32[]{:S(2)}) %all-to-all-start) | async-done | bytes 266272 | tf_op jit(solution)/shard_map/all_to_all | solution.py:30
  18.4 2.1 %shard_map.77 = (bf16[8,8,2816]{2,1,0:T(8,128)(2,1)}, f32[16,128]{1,0:T(8,128)S(1)}, f32[16,128]{1,0:T(8,128)S(1)}, f32[16,128]{1,0:T(8,128)S(1)}) custom-call(s32[1]{0:T(128)} %bitcast.first_ref, bf16[8,2,8320]{2,1,0:T(2,128)(2,1)S(1)} %all-to-all-done.rows_ref, bf16[8192,128]{1,0:T(8,128)(2,1)S(1)} %pad_maximum_fusion.heads_ref), custom_call_target="tpu_custom_call" | custom-call | tf_op jit(solution)/shard_map/pallas_call | solution.py:288
  20.5 3.6 %all-to-all-start.1 = ((bf16[8,8,2816]{2,1,0:T(8,128)(2,1)}), bf16[8,8,2816]{2,1,0:T(8,128)(2,1)S(1)}, u32[]{:S(2)}, u32[]{:S(2)}) async-start(bf16[8,8,2816]{2,1,0:T(8,128)(2,1)} %get-tuple-element.9), calls=%async_computation.1 | async-start | bytes 720896 | tf_op jit(solution)/shard_map/all_to_all | solution.py:30
  24.1 0.1 slice.8
  24.2 0.1 collective-permute-start
  24.3 10.4 %all-to-all-done.1.arrived_ref = bf16[8,8,2816]{2,1,0:T(8,128)(2,1)S(1)} async-done(((bf16[8,8,2816]{2,1,0:T(8,128)(2,1)}), bf16[8,8,2816]{2,1,0:T(8,128)(2,1)S(1)}, u32[]{:S(2)}, u32[]{:S(2)}) %all-to-all-start.1) | async-done | bytes 360480 | tf_op jit(solution)/shard_map/all_to_all | solution.py:30
  34.7 0.3 shard_map.79.grad_ref
  35.1 0.1 collective-permute-start.1
  35.1 1.3 %shard_map.78 = (f32[2,3584]{1,0:T(2,128)}, f32[2]{0:T(128)}) custom-call(bf16[8,8,2816]{2,1,0:T(8,128)(2,1)S(1)} %all-to-all-done.1.arrived_ref), custom_call_target="tpu_custom_call" | custom-call | tf_op jit(solution)/shard_map/pallas_call | solution.py:305
  36.4 0.0 collective-permute-done.hidden_other_ref
  36.4 0.0 collective-permute-done.1.other_ref
  36.4 1.5 %shard_map.80 = f32[3584,128]{1,0:T(8,128)} custom-call(bf16[16,3584]{1,0:T(8,128)(2,1)S(1)} %reshape.9.hidden_ref, bf16[16,3584]{1,0:T(8,128)(2,1)S(1)} %collective-permute-done.hidden_other_ref, bf16[16,128]{1,0:T(8,128)(2,1)S(1)} %shard_map.79.grad_ref, bf16[16,128]{1,0:T(8,128)(2,1)S(1)} %collective-permute-done.1.other_ref), custom_call_target="tpu_custom_call" | custom-call | tf_op jit(solution)/shard_map/pallas_call | solution.py:312
  (2 shorter events, 0.0 us)
Async XLA Ops:
  2.1 16.3 %all-to-all-start = ((bf16[8,2,8320]{2,1,0:T(2,128)(2,1)}), bf16[8,2,8320]{2,1,0:T(2,128)(2,1)S(1)}, u32[]{:S(2)}, u32[]{:S(2)}) async-start(bf16[8,2,8320]{2,1,0:T(2,128)(2,1)} %shard_map.76), calls=%async_computation | async-start | bytes 532480 | tf_op jit(solution)/shard_map/all_to_all | solution.py:30
  20.5 14.3 %all-to-all-start.1 = ((bf16[8,8,2816]{2,1,0:T(8,128)(2,1)}), bf16[8,8,2816]{2,1,0:T(8,128)(2,1)S(1)}, u32[]{:S(2)}, u32[]{:S(2)}) async-start(bf16[8,8,2816]{2,1,0:T(8,128)(2,1)} %get-tuple-element.9), calls=%async_computation.1 | async-start | bytes 720896 | tf_op jit(solution)/shard_map/all_to_all | solution.py:30
  24.2 12.2 %collective-permute-start = (bf16[16,3584]{1,0:T(8,128)(2,1)S(1)}, bf16[16,3584]{1,0:T(8,128)(2,1)S(1)}, u32[]{:S(2)}, u32[]{:S(2)}) collective-permute-start(bf16[16,3584]{1,0:T(8,128)(2,1)S(1)} %reshape.9.hidden_ref), channel_id=1, source_target_pairs={{0,1},{1,0},{2,3},{3,2},{4,5},{5,4},{6,7},{7,6},{8,9},{9,8},{10,11... | collective-permute-start | bytes 344072 | tf_op jit(solution)/shard_map/ppermute | solution.py:285
  35.1 1.4 %collective-permute-start.1 = (bf16[16,128]{1,0:T(8,128)(2,1)S(1)}, bf16[16,128]{1,0:T(8,128)(2,1)S(1)}, u32[]{:S(2)}, u32[]{:S(2)}) collective-permute-start(bf16[16,128]{1,0:T(8,128)(2,1)S(1)} %shard_map.79.grad_ref), channel_id=1, source_target_pairs={{0,1},{1,0},{2,3},{3,2},{4,5},{5,4},{6,7},{7,6},{8,9},{9,8},{10,11... | collective-permute-start | bytes 12296 | tf_op jit(solution)/shard_map/ppermute | solution.py:304

commit v13 on v12

--- a/solution.py
+++ b/solution.py
@@ -71,8 +71,8 @@
 def raw_partial_kernel(
     first_ref, rows_ref, heads_ref, out_hbm, teacher_ref, student_ref, target_ref, out_ref, sems
 ):
-    shards, own, _ = rows_ref.shape
-    tokens = shards * own
+    tokens = rows_ref.shape[0]
+    shards = out_ref.shape[0]
     wide = 8 * shards
     columns = heads_ref.shape[1]
     quarter = (out_ref.shape[2] - 128) // 3
@@ -92,12 +92,9 @@
         copies.append(pltpu.make_async_copy(out_ref.at[:, :, lanes], out_hbm.at[:, :, lanes], sems.at[piece]))
         copies[-1].start()
 
-    def rows_of(start, size):
-        return jnp.concatenate([rows_ref[shard, :, start : start + size] for shard in range(shards)], axis=0)
-
-    student = dot(rows_of(teacher_width, width), heads_ref[teacher_width:, :], ((1,), (0,)))
-    teacher = dot(rows_of(0, teacher_width), heads_ref[:teacher_width, :], ((1,), (0,)))
-    code = rows_of(teacher_width + width, CODE).astype(F32)
+    student = dot(rows_ref[:, teacher_width : teacher_width + width], heads_ref[teacher_width:, :], ((1,), (0,)))
+    teacher = dot(rows_ref[:, :teacher_width], heads_ref[:teacher_width, :], ((1,), (0,)))
+    code = rows_ref[:, teacher_width + width :].astype(F32)
     lane = iota(code.shape, 1)
     label = jnp.sum(jnp.where(lane == 0, code * 128.0, jnp.where(lane == 1, code, 0.0)), axis=1, keepdims=True)
     target = (label.astype(jnp.int32) - first_ref[0] == iota((tokens, columns), 1)).astype(F32)
@@ -114,7 +111,8 @@
     exp_s = jnp.exp(student - top_s)
     mass_t, mass_s = total(exp_t), total(exp_s)
     combined = exp_s * (2.0 / mass_s) - exp_t / mass_t
-    kappa = (total(target * combined) > 0.5).astype(F32)
+    confidence = total(target * (exp_s * (2.0 / mass_s) + exp_t / mass_t))
+    kappa = (confidence > 0.75).astype(F32)
     stats = [
         top_t,
         mass_t,
@@ -160,14 +158,13 @@
     row, column = iota((wide, 3 * tokens), 0), iota((wide, 3 * tokens), 1)
     place = row % 8
     token = (row // 8) * 2 + row % 2
-    picks = [((place < 6) & (column == (place // 2) * tokens + token)).astype(F32)]
-    for j in range(3):
-        picks.append(((place >= 6) & (column == j * tokens + token)).astype(F32))
-    pick = jnp.concatenate(picks, axis=0).astype(BF16)
-    left_high = dot(pick, member_high, ((1,), (0,))).astype(BF16)
-    left_low = dot(pick, member_low, ((1,), (0,))).astype(BF16)
-    left = jnp.concatenate([left_high[:wide], left_low[:wide]], axis=0)
-    left_last = jnp.concatenate([left_high[wide:], left_low[wide:]], axis=0)
+    pick = ((place < 6) & (column == (place // 2) * tokens + token)).astype(F32).astype(BF16)
+    left = dot(pick, jnp.concatenate([member_high, member_low], axis=1), ((1,), (0,))).astype(BF16)
+    left = jnp.concatenate([left[:, :columns], left[:, columns:]], axis=0)
+
+    def partials(start):
+        both = dot(left, heads_ref[teacher_width + start : teacher_width + start + quarter, :], ((1,), (1,)))
+        return both[:wide] + both[wide:]
 
     place = iota((wide, 1), 0) % 8
     has_label = stat_by_row(7) > 0.5
@@ -177,11 +174,10 @@
     in_third = ((place == 4) | (place == 5)).astype(F32)
     scale_s = jnp.where(place >= 6, scale_s, 0.0)
     scale_t = jnp.where(place >= 6, scale_t, 0.0)
-    last = dot(left_last, heads_ref[teacher_width + 3 * quarter :, :], ((1,), (1,)))
+    last = partials(3 * quarter)
     correction = jnp.zeros((wide, quarter), F32)
     for j in range(3):
-        both = dot(left, heads_ref[teacher_width + j * quarter : teacher_width + (j + 1) * quarter, :], ((1,), (1,)))
-        exact = both[:wide] + both[wide:] + last[j * wide : (j + 1) * wide] + last[(3 + j) * wide : (4 + j) * wide]
+        exact = partials(j * quarter) + jnp.where(place >= 6, pltpu.roll(last, 6 - 2 * j, 0), 0.0)
         sent = exact.astype(BF16).astype(F32)
         residue = exact - sent
         if j < 2:
@@ -260,14 +256,22 @@
 
 def head_grad_kernel(hidden_ref, hidden_other_ref, grad_ref, other_ref, out_ref, total_ref, sems):
     grads = jnp.concatenate([grad_ref[...], other_ref[...]], axis=0)
-    size = hidden_ref.shape[1] // PIECES
+    zeros = jnp.zeros_like(grads)
+    grads = jnp.concatenate(
+        [jnp.concatenate([grads, zeros], axis=1), jnp.concatenate([zeros, grads], axis=1)], axis=0
+    )
+    half, columns = total_ref.shape[0] // 2, total_ref.shape[1]
+    size = half // PIECES
     copies = []
     for piece in range(PIECES):
-        rows = pl.ds(piece * size, size)
-        hidden = jnp.concatenate([hidden_ref[:, rows], hidden_other_ref[:, rows]], axis=0)
-        total_ref[rows, :] = lax.dot_general(hidden, grads, (((0,), (0,)), ((), ())), preferred_element_type=F32)
-        copies.append(pltpu.make_async_copy(total_ref.at[rows, :], out_ref.at[rows, :], sems.at[piece]))
-        copies[-1].start()
+        places = [pl.ds(side * half + piece * size, size) for side in range(2)]
+        hidden = jnp.concatenate([ref[:, rows] for rows in places for ref in (hidden_ref, hidden_other_ref)], axis=0)
+        both = lax.dot_general(hidden, grads, (((0,), (0,)), ((), ())), preferred_element_type=F32)
+        for side, rows in enumerate(places):
+            total_ref[rows, :] = both[:, side * columns : (side + 1) * columns]
+            sem = sems.at[2 * piece + side]
+            copies.append(pltpu.make_async_copy(total_ref.at[rows, :], out_ref.at[rows, :], sem))
+            copies[-1].start()
     for copy in copies:
         copy.wait()
 
@@ -279,8 +283,8 @@
     tokens = shards * own
     quarter = width // 4
     here = lax.axis_index("vocab").astype(jnp.int32)
-    rows = gather_tokens(teacher_hidden, student_hidden, labels, shards)
-    student_rows = rows[:, :, teacher_width : teacher_width + width].reshape(tokens, width)
+    rows = gather_tokens(teacher_hidden, student_hidden, labels, shards).reshape(tokens, -1)
+    student_rows = rows[:, teacher_width : teacher_width + width]
     other = [(0, 1), (1, 0)]
     student_other = lax.ppermute(student_rows, "rows", other)
 
@@ -314,7 +318,7 @@
         out_shape=jax.ShapeDtypeStruct((width, columns_here), F32),
         in_specs=[VMEM] * 4,
         out_specs=ANY,
-        scratch_shapes=[pltpu.VMEM((width, columns_here), F32), pltpu.SemaphoreType.DMA((PIECES,))],
+        scratch_shapes=[pltpu.VMEM((width, columns_here), F32), pltpu.SemaphoreType.DMA((2 * PIECES,))],
         compiler_params=SMALL,
     )(student_rows, student_other, grad_rows, grad_other)
     return (token_loss, hidden_grad, head_grad)

time: 38.4 us -> 38.6 us (level)
  transfers between devices with their start and end apart: 4 -> 4, of which waited for: 2 -> 2; matrix products, arithmetic and copies ran while one was open for 5% -> 4% of each run, Pallas kernels for 4% -> 4%
where the time goes in v13:
time: 38.6 us; the launch traced here: 38.1 us
  waiting for transfers between devices  17.9 us (46%)
  starting transfers between devices  11 us (28%)
  Pallas kernels  6.74 us (17%)
  other arithmetic  1.69 us (4%)
  between operations  0.7 us (2%)
    all_to_all x2, waiting for transfers between devices, swap(): lax.all_to_all(blocks, 'vocab', split_axis=0, concat_axis=0, tiled=True)  17.9 us
    all_to_all x2, starting transfers between devices, swap(): lax.all_to_all(blocks, 'vocab', split_axis=0, concat_axis=0, tiled=True)  10.9 us
    pallas_call x1, Pallas kernels, two_exchanges(): pl.pallas_call(raw_partial_kernel, out_shape=(jax.ShapeDtypeStruct((shard...  2.13 us
    concatenate x1, other arithmetic, two_exchanges(): jnp.concatenate([teacher_head, student_head], axis=0)  1.69 us
    pallas_call x1, Pallas kernels, two_exchanges(): pl.pallas_call(head_grad_kernel, out_shape=jax.ShapeDtypeStruct((width, c...  1.57 us
    pallas_call x1, Pallas kernels, gather_tokens(): pl.pallas_call(payload_kernel, out_shape=jax.ShapeDtypeStruct((shards, ow...  1.48 us
    pallas_call x1, Pallas kernels, two_exchanges(): pl.pallas_call(owner_kernel, out_shape=(jax.ShapeDtypeStruct((own, width)...  1.26 us
  transfers between devices with their start and end apart: 4, of which 2 were waited for; matrix products, arithmetic and copies ran while one was open for 4% of the time, Pallas kernels for 4%

profile of v13, /device:TPU:0, one launch (start us, length us, event | category | flops | bytes accessed | tf_op | source)
XLA Modules:
  0.0 38.1 jit_solution(724987389499710356)
XLA Ops:
  0.6 1.5 %shard_map.76 = bf16[8,2,8320]{2,1,0:T(2,128)(2,1)} custom-call(s32[2]{0:T(128)} %labels_ref.1, bf16[2,4608]{1,0:T(2,128)(2,1)} %teacher_ref.1, bf16[2,3584]{1,0:T(2,128)(2,1)} %student_ref.1), custom_call_target="tpu_custom_call" | custom-call | tf_op jit(solution)/shard_map/pallas_call | solution.py:62
  2.1 7.3 %all-to-all-start = ((bf16[8,2,8320]{2,1,0:T(2,128)(2,1)}), bf16[8,2,8320]{2,1,0:T(2,128)(2,1)S(1)}, u32[]{:S(2)}, u32[]{:S(2)}) async-start(bf16[8,2,8320]{2,1,0:T(2,128)(2,1)} %shard_map.76), calls=%async_computation | async-start | bytes 532480 | tf_op jit(solution)/shard_map/all_to_all | solution.py:30
  9.4 1.7 %pad_maximum_fusion.heads_ref = bf16[8192,128]{1,0:T(8,128)(2,1)S(1)} fusion(bf16[3584,128]{1,0:T(8,128)(2,1)} %param.8, bf16[4608,128]{1,0:T(8,128)(2,1)} %param.7), kind=kLoop, calls=%fused_computation | loop fusion | flops 4194304 | bytes 4194304 | tf_op jit(solution)/shard_map/concatenate | solution.py:299
  11.1 7.3 %all-to-all-done = bf16[8,2,8320]{2,1,0:T(2,128)(2,1)S(1)} async-done(((bf16[8,2,8320]{2,1,0:T(2,128)(2,1)}), bf16[8,2,8320]{2,1,0:T(2,128)(2,1)S(1)}, u32[]{:S(2)}, u32[]{:S(2)}) %all-to-all-start) | async-done | bytes 266272 | tf_op jit(solution)/shard_map/all_to_all | solution.py:30
  18.4 0.1 reshape.9.rows_ref
  18.5 2.1 %shard_map.77 = (bf16[8,8,2816]{2,1,0:T(8,128)(2,1)}, f32[16,128]{1,0:T(8,128)S(1)}, f32[16,128]{1,0:T(8,128)S(1)}, f32[16,128]{1,0:T(8,128)S(1)}) custom-call(s32[1]{0:T(128)} %bitcast.first_ref, bf16[16,8320]{1,0:T(8,128)(2,1)S(1)} %reshape.9.rows_ref, bf16[8192,128]{1,0:T(8,128)(2,1)S(1)} %pad_maximum_fusion.heads_ref), custom_call_target="tpu_custom_call" | custom-call | tf_op jit(solution)/shard_map/pallas_call | solution.py:292
  20.6 3.6 %all-to-all-start.1 = ((bf16[8,8,2816]{2,1,0:T(8,128)(2,1)}), bf16[8,8,2816]{2,1,0:T(8,128)(2,1)S(1)}, u32[]{:S(2)}, u32[]{:S(2)}) async-start(bf16[8,8,2816]{2,1,0:T(8,128)(2,1)} %get-tuple-element.9), calls=%async_computation.1 | async-start | bytes 720896 | tf_op jit(solution)/shard_map/all_to_all | solution.py:30
  24.2 0.1 collective-permute-start
  24.3 10.6 %all-to-all-done.1.arrived_ref = bf16[8,8,2816]{2,1,0:T(8,128)(2,1)S(1)} async-done(((bf16[8,8,2816]{2,1,0:T(8,128)(2,1)}), bf16[8,8,2816]{2,1,0:T(8,128)(2,1)S(1)}, u32[]{:S(2)}, u32[]{:S(2)}) %all-to-all-start.1) | async-done | bytes 360480 | tf_op jit(solution)/shard_map/all_to_all | solution.py:30
  34.9 0.3 shard_map.79.grad_ref
  35.2 0.1 collective-permute-start.1
  35.3 1.3 %shard_map.78 = (f32[2,3584]{1,0:T(2,128)}, f32[2]{0:T(128)}) custom-call(bf16[8,8,2816]{2,1,0:T(8,128)(2,1)S(1)} %all-to-all-done.1.arrived_ref), custom_call_target="tpu_custom_call" | custom-call | tf_op jit(solution)/shard_map/pallas_call | solution.py:309
  36.5 0.0 collective-permute-done.hidden_other_ref
  36.5 0.0 collective-permute-done.1.other_ref
  36.6 1.6 %shard_map.80 = f32[3584,128]{1,0:T(8,128)} custom-call(bf16[16,3584]{1,0:T(8,128)(2,1)S(1)} %slice.8.hidden_ref, bf16[16,3584]{1,0:T(8,128)(2,1)S(1)} %collective-permute-done.hidden_other_ref, bf16[16,128]{1,0:T(8,128)(2,1)S(1)} %shard_map.79.grad_ref, bf16[16,128]{1,0:T(8,128)(2,1)S(1)} %collective-permute-done.1.other_ref), custom_call_target="tpu_custom_call" | custom-call | tf_op jit(solution)/shard_map/pallas_call | solution.py:316
  (2 shorter events, 0.0 us)
Async XLA Ops:
  2.1 16.3 %all-to-all-start = ((bf16[8,2,8320]{2,1,0:T(2,128)(2,1)}), bf16[8,2,8320]{2,1,0:T(2,128)(2,1)S(1)}, u32[]{:S(2)}, u32[]{:S(2)}) async-start(bf16[8,2,8320]{2,1,0:T(2,128)(2,1)} %shard_map.76), calls=%async_computation | async-start | bytes 532480 | tf_op jit(solution)/shard_map/all_to_all | solution.py:30
  20.6 14.3 %all-to-all-start.1 = ((bf16[8,8,2816]{2,1,0:T(8,128)(2,1)}), bf16[8,8,2816]{2,1,0:T(8,128)(2,1)S(1)}, u32[]{:S(2)}, u32[]{:S(2)}) async-start(bf16[8,8,2816]{2,1,0:T(8,128)(2,1)} %get-tuple-element.9), calls=%async_computation.1 | async-start | bytes 720896 | tf_op jit(solution)/shard_map/all_to_all | solution.py:30
  24.2 12.3 %collective-permute-start = (bf16[16,3584]{1,0:T(8,128)(2,1)S(1)}, bf16[16,3584]{1,0:T(8,128)(2,1)S(1)}, u32[]{:S(2)}, u32[]{:S(2)}) collective-permute-start(bf16[16,3584]{1,0:T(8,128)(2,1)S(1)} %slice.8.hidden_ref), channel_id=1, source_target_pairs={{0,1},{1,0},{2,3},{3,2},{4,5},{5,4},{6,7},{7,6},{8,9},{9,8},{10,11... | collective-permute-start | bytes 344072 | tf_op jit(solution)/shard_map/ppermute | solution.py:289
  35.2 1.4 %collective-permute-start.1 = (bf16[16,128]{1,0:T(8,128)(2,1)S(1)}, bf16[16,128]{1,0:T(8,128)(2,1)S(1)}, u32[]{:S(2)}, u32[]{:S(2)}) collective-permute-start(bf16[16,128]{1,0:T(8,128)(2,1)S(1)} %shard_map.79.grad_ref), channel_id=1, source_target_pairs={{0,1},{1,0},{2,3},{3,2},{4,5},{5,4},{6,7},{7,6},{8,9},{9,8},{10,11... | collective-permute-start | bytes 12296 | tf_op jit(solution)/shard_map/ppermute | solution.py:308

commit v14 on v13

--- a/solution.py
+++ b/solution.py
@@ -92,12 +92,20 @@
         copies.append(pltpu.make_async_copy(out_ref.at[:, :, lanes], out_hbm.at[:, :, lanes], sems.at[piece]))
         copies[-1].start()
 
-    student = dot(rows_ref[:, teacher_width : teacher_width + width], heads_ref[teacher_width:, :], ((1,), (0,)))
-    teacher = dot(rows_ref[:, :teacher_width], heads_ref[:teacher_width, :], ((1,), (0,)))
+    def logits(start, size):
+        half = size // 2
+        sides = [slice(start, start + half), slice(start + half, start + size)]
+        left = jnp.concatenate([rows_ref[:, side] for side in sides], axis=0)
+        right = jnp.concatenate([heads_ref[side, :] for side in sides], axis=1)
+        both = dot(left, right, ((1,), (0,)))
+        return both[:tokens, :columns] + both[tokens:, columns:]
+
+    student = logits(teacher_width, width)
+    teacher = logits(0, teacher_width)
     code = rows_ref[:, teacher_width + width :].astype(F32)
     lane = iota(code.shape, 1)
     label = jnp.sum(jnp.where(lane == 0, code * 128.0, jnp.where(lane == 1, code, 0.0)), axis=1, keepdims=True)
-    target = (label.astype(jnp.int32) - first_ref[0] == iota((tokens, columns), 1)).astype(F32)
+    target = (label.astype(jnp.int32) == iota((tokens, columns), 1) + first_ref[...]).astype(F32)
     teacher_ref[...] = teacher
     student_ref[...] = student
     target_ref[...] = target
@@ -256,22 +264,14 @@
 
 def head_grad_kernel(hidden_ref, hidden_other_ref, grad_ref, other_ref, out_ref, total_ref, sems):
     grads = jnp.concatenate([grad_ref[...], other_ref[...]], axis=0)
-    zeros = jnp.zeros_like(grads)
-    grads = jnp.concatenate(
-        [jnp.concatenate([grads, zeros], axis=1), jnp.concatenate([zeros, grads], axis=1)], axis=0
-    )
-    half, columns = total_ref.shape[0] // 2, total_ref.shape[1]
-    size = half // PIECES
+    size = hidden_ref.shape[1] // PIECES
     copies = []
     for piece in range(PIECES):
-        places = [pl.ds(side * half + piece * size, size) for side in range(2)]
-        hidden = jnp.concatenate([ref[:, rows] for rows in places for ref in (hidden_ref, hidden_other_ref)], axis=0)
-        both = lax.dot_general(hidden, grads, (((0,), (0,)), ((), ())), preferred_element_type=F32)
-        for side, rows in enumerate(places):
-            total_ref[rows, :] = both[:, side * columns : (side + 1) * columns]
-            sem = sems.at[2 * piece + side]
-            copies.append(pltpu.make_async_copy(total_ref.at[rows, :], out_ref.at[rows, :], sem))
-            copies[-1].start()
+        rows = pl.ds(piece * size, size)
+        hidden = jnp.concatenate([hidden_ref[:, rows], hidden_other_ref[:, rows]], axis=0)
+        total_ref[rows, :] = lax.dot_general(hidden, grads, (((0,), (0,)), ((), ())), preferred_element_type=F32)
+        copies.append(pltpu.make_async_copy(total_ref.at[rows, :], out_ref.at[rows, :], sems.at[piece]))
+        copies[-1].start()
     for copy in copies:
         copy.wait()
 
@@ -292,11 +292,11 @@
     payload, teacher_logits, student_logits, target = pl.pallas_call(
         raw_partial_kernel,
         out_shape=(jax.ShapeDtypeStruct((shards, 8, 3 * quarter + 128), BF16), square, square, square),
-        in_specs=[SMEM, VMEM, VMEM],
+        in_specs=[VMEM, VMEM, VMEM],
         out_specs=(ANY, VMEM, VMEM, VMEM),
         scratch_shapes=[pltpu.VMEM((shards, 8, 3 * quarter + 128), BF16), pltpu.SemaphoreType.DMA((4,))],
         compiler_params=SMALL,
-    )((here * columns_here)[None], rows, jnp.concatenate([teacher_head, student_head], axis=0))
+    )(jnp.full((1, columns_here), here * columns_here, jnp.int32), rows, jnp.concatenate([teacher_head, student_head], axis=0))
     arrived = swap(payload)
     grad_rows = pl.pallas_call(
         logit_grad_kernel,
@@ -318,7 +318,7 @@
         out_shape=jax.ShapeDtypeStruct((width, columns_here), F32),
         in_specs=[VMEM] * 4,
         out_specs=ANY,
-        scratch_shapes=[pltpu.VMEM((width, columns_here), F32), pltpu.SemaphoreType.DMA((2 * PIECES,))],
+        scratch_shapes=[pltpu.VMEM((width, columns_here), F32), pltpu.SemaphoreType.DMA((PIECES,))],
         compiler_params=SMALL,
     )(student_rows, student_other, grad_rows, grad_other)
     return (token_loss, hidden_grad, head_grad)

time: 38.6 us -> 38.6 us (level)
  no operation moved by 1% of the time
where the time goes in v14:
time: 38.6 us; the launch traced here: 38.2 us
  waiting for transfers between devices  17.9 us (46%)
  starting transfers between devices  11 us (28%)
  Pallas kernels  6.8 us (18%)
  other arithmetic  1.69 us (4%)
  between operations  0.71 us (2%)
    all_to_all x2, waiting for transfers between devices, swap(): lax.all_to_all(blocks, 'vocab', split_axis=0, concat_axis=0, tiled=True)  17.9 us
    all_to_all x2, starting transfers between devices, swap(): lax.all_to_all(blocks, 'vocab', split_axis=0, concat_axis=0, tiled=True)  10.9 us
    pallas_call x1, Pallas kernels, two_exchanges(): pl.pallas_call(raw_partial_kernel, out_shape=(jax.ShapeDtypeStruct((shard...  2.21 us
    concatenate x1, other arithmetic, two_exchanges(): jnp.concatenate([teacher_head, student_head], axis=0)  1.69 us
    pallas_call x1, Pallas kernels, two_exchanges(): pl.pallas_call(head_grad_kernel, out_shape=jax.ShapeDtypeStruct((width, c...  1.54 us
    pallas_call x1, Pallas kernels, gather_tokens(): pl.pallas_call(payload_kernel, out_shape=jax.ShapeDtypeStruct((shards, ow...  1.48 us
    pallas_call x1, Pallas kernels, two_exchanges(): pl.pallas_call(owner_kernel, out_shape=(jax.ShapeDtypeStruct((own, width)...  1.26 us
  transfers between devices with their start and end apart: 4, of which 2 were waited for; matrix products, arithmetic and copies ran while one was open for 4% of the time, Pallas kernels for 4%

profile of v14, /device:TPU:0, one launch (start us, length us, event | category | flops | bytes accessed | tf_op | source)
XLA Modules:
  0.0 38.2 jit_solution(14913346013774026311)
XLA Ops:
  0.6 1.5 %shard_map.76 = bf16[8,2,8320]{2,1,0:T(2,128)(2,1)} custom-call(s32[2]{0:T(128)} %labels_ref.1, bf16[2,4608]{1,0:T(2,128)(2,1)} %teacher_ref.1, bf16[2,3584]{1,0:T(2,128)(2,1)} %student_ref.1), custom_call_target="tpu_custom_call" | custom-call | tf_op jit(solution)/shard_map/pallas_call | solution.py:62
  2.1 7.3 %all-to-all-start = ((bf16[8,2,8320]{2,1,0:T(2,128)(2,1)}), bf16[8,2,8320]{2,1,0:T(2,128)(2,1)S(1)}, u32[]{:S(2)}, u32[]{:S(2)}) async-start(bf16[8,2,8320]{2,1,0:T(2,128)(2,1)} %shard_map.76), calls=%async_computation | async-start | bytes 532480 | tf_op jit(solution)/shard_map/all_to_all | solution.py:30
  9.4 1.7 %pad_maximum_fusion.heads_ref = bf16[8192,128]{1,0:T(8,128)(2,1)S(1)} fusion(bf16[3584,128]{1,0:T(8,128)(2,1)} %param.8, bf16[4608,128]{1,0:T(8,128)(2,1)} %param.7), kind=kLoop, calls=%fused_computation | loop fusion | flops 4194304 | bytes 4194304 | tf_op jit(solution)/shard_map/concatenate | solution.py:299
  11.1 7.3 %all-to-all-done = bf16[8,2,8320]{2,1,0:T(2,128)(2,1)S(1)} async-done(((bf16[8,2,8320]{2,1,0:T(2,128)(2,1)}), bf16[8,2,8320]{2,1,0:T(2,128)(2,1)S(1)}, u32[]{:S(2)}, u32[]{:S(2)}) %all-to-all-start) | async-done | bytes 266272 | tf_op jit(solution)/shard_map/all_to_all | solution.py:30
  18.4 0.1 reshape.9.rows_ref
  18.5 2.2 %shard_map.77 = (bf16[8,8,2816]{2,1,0:T(8,128)(2,1)}, f32[16,128]{1,0:T(8,128)S(1)}, f32[16,128]{1,0:T(8,128)S(1)}, f32[16,128]{1,0:T(8,128)S(1)}) custom-call(s32[1,128]{1,0:T(1,128)S(1)} %broadcast_in_dim.3.first_ref, bf16[16,8320]{1,0:T(8,128)(2,1)S(1)} %reshape.9.rows_ref, bf16[8192,128]{1,0:T(8,128)(2,1)S(1)} %pad_maximum_fusion.heads_ref), custom_call_target="tpu_custom_call" | custom-call | tf_op jit(solution)/shard_map/pallas_call | solution.py:292
  20.7 3.6 %all-to-all-start.1 = ((bf16[8,8,2816]{2,1,0:T(8,128)(2,1)}), bf16[8,8,2816]{2,1,0:T(8,128)(2,1)S(1)}, u32[]{:S(2)}, u32[]{:S(2)}) async-start(bf16[8,8,2816]{2,1,0:T(8,128)(2,1)} %get-tuple-element.9), calls=%async_computation.1 | async-start | bytes 720896 | tf_op jit(solution)/shard_map/all_to_all | solution.py:30
  24.3 0.1 collective-permute-start
  24.4 10.6 %all-to-all-done.1.arrived_ref = bf16[8,8,2816]{2,1,0:T(8,128)(2,1)S(1)} async-done(((bf16[8,8,2816]{2,1,0:T(8,128)(2,1)}), bf16[8,8,2816]{2,1,0:T(8,128)(2,1)S(1)}, u32[]{:S(2)}, u32[]{:S(2)}) %all-to-all-start.1) | async-done | bytes 360480 | tf_op jit(solution)/shard_map/all_to_all | solution.py:30
  35.0 0.3 shard_map.79.grad_ref
  35.3 0.1 collective-permute-start.1
  35.3 1.3 %shard_map.78 = (f32[2,3584]{1,0:T(2,128)}, f32[2]{0:T(128)}) custom-call(bf16[8,8,2816]{2,1,0:T(8,128)(2,1)S(1)} %all-to-all-done.1.arrived_ref), custom_call_target="tpu_custom_call" | custom-call | tf_op jit(solution)/shard_map/pallas_call | solution.py:309
  36.6 0.0 collective-permute-done.hidden_other_ref
  36.6 0.0 collective-permute-done.1.other_ref
  36.6 1.5 %shard_map.80 = f32[3584,128]{1,0:T(8,128)} custom-call(bf16[16,3584]{1,0:T(8,128)(2,1)S(1)} %slice.8.hidden_ref, bf16[16,3584]{1,0:T(8,128)(2,1)S(1)} %collective-permute-done.hidden_other_ref, bf16[16,128]{1,0:T(8,128)(2,1)S(1)} %shard_map.79.grad_ref, bf16[16,128]{1,0:T(8,128)(2,1)S(1)} %collective-permute-done.1.other_ref), custom_call_target="tpu_custom_call" | custom-call | tf_op jit(solution)/shard_map/pallas_call | solution.py:316
  (3 shorter events, 0.0 us)
Async XLA Ops:
  2.1 16.3 %all-to-all-start = ((bf16[8,2,8320]{2,1,0:T(2,128)(2,1)}), bf16[8,2,8320]{2,1,0:T(2,128)(2,1)S(1)}, u32[]{:S(2)}, u32[]{:S(2)}) async-start(bf16[8,2,8320]{2,1,0:T(2,128)(2,1)} %shard_map.76), calls=%async_computation | async-start | bytes 532480 | tf_op jit(solution)/shard_map/all_to_all | solution.py:30
  20.7 14.3 %all-to-all-start.1 = ((bf16[8,8,2816]{2,1,0:T(8,128)(2,1)}), bf16[8,8,2816]{2,1,0:T(8,128)(2,1)S(1)}, u32[]{:S(2)}, u32[]{:S(2)}) async-start(bf16[8,8,2816]{2,1,0:T(8,128)(2,1)} %get-tuple-element.9), calls=%async_computation.1 | async-start | bytes 720896 | tf_op jit(solution)/shard_map/all_to_all | solution.py:30
  24.3 12.3 %collective-permute-start = (bf16[16,3584]{1,0:T(8,128)(2,1)S(1)}, bf16[16,3584]{1,0:T(8,128)(2,1)S(1)}, u32[]{:S(2)}, u32[]{:S(2)}) collective-permute-start(bf16[16,3584]{1,0:T(8,128)(2,1)S(1)} %slice.8.hidden_ref), channel_id=1, source_target_pairs={{0,1},{1,0},{2,3},{3,2},{4,5},{5,4},{6,7},{7,6},{8,9},{9,8},{10,11... | collective-permute-start | bytes 344072 | tf_op jit(solution)/shard_map/ppermute | solution.py:289
  35.3 1.4 %collective-permute-start.1 = (bf16[16,128]{1,0:T(8,128)(2,1)S(1)}, bf16[16,128]{1,0:T(8,128)(2,1)S(1)}, u32[]{:S(2)}, u32[]{:S(2)}) collective-permute-start(bf16[16,128]{1,0:T(8,128)(2,1)S(1)} %shard_map.79.grad_ref), channel_id=1, source_target_pairs={{0,1},{1,0},{2,3},{3,2},{4,5},{5,4},{6,7},{7,6},{8,9},{9,8},{10,11... | collective-permute-start | bytes 12296 | tf_op jit(solution)/shard_map/ppermute | solution.py:308

commit v15 on v14

--- a/solution.py
+++ b/solution.py
@@ -11,6 +11,7 @@
 
 
 UNROLL = 16
+LANES = 128
 PIECES = 7
 SMEM = pl.BlockSpec(memory_space=pltpu.SMEM)
 VMEM = pl.BlockSpec(memory_space=pltpu.VMEM)
@@ -92,20 +93,12 @@
         copies.append(pltpu.make_async_copy(out_ref.at[:, :, lanes], out_hbm.at[:, :, lanes], sems.at[piece]))
         copies[-1].start()
 
-    def logits(start, size):
-        half = size // 2
-        sides = [slice(start, start + half), slice(start + half, start + size)]
-        left = jnp.concatenate([rows_ref[:, side] for side in sides], axis=0)
-        right = jnp.concatenate([heads_ref[side, :] for side in sides], axis=1)
-        both = dot(left, right, ((1,), (0,)))
-        return both[:tokens, :columns] + both[tokens:, columns:]
-
-    student = logits(teacher_width, width)
-    teacher = logits(0, teacher_width)
+    student = dot(rows_ref[:, teacher_width : teacher_width + width], heads_ref[teacher_width:, :], ((1,), (0,)))
+    teacher = dot(rows_ref[:, :teacher_width], heads_ref[:teacher_width, :], ((1,), (0,)))
     code = rows_ref[:, teacher_width + width :].astype(F32)
     lane = iota(code.shape, 1)
     label = jnp.sum(jnp.where(lane == 0, code * 128.0, jnp.where(lane == 1, code, 0.0)), axis=1, keepdims=True)
-    target = (label.astype(jnp.int32) == iota((tokens, columns), 1) + first_ref[...]).astype(F32)
+    target = (label.astype(jnp.int32) - first_ref[0] == iota((tokens, columns), 1)).astype(F32)
     teacher_ref[...] = teacher
     student_ref[...] = student
     target_ref[...] = target
@@ -158,7 +151,7 @@
     for shard in range(shards):
         block = jnp.where(lane < 32, by_row[8 * shard : 8 * shard + 8], shared)
         out_ref[shard, :, 3 * quarter :] = block.astype(BF16)
-    send_out(3, 3 * quarter, 128)
+    send_out(0, 3 * quarter, 128)
 
     members = jnp.concatenate([exp_s, exp_t, kappa * combined * total(target) - target], axis=0)
     member_high = members.astype(BF16)
@@ -170,10 +163,6 @@
     left = dot(pick, jnp.concatenate([member_high, member_low], axis=1), ((1,), (0,))).astype(BF16)
     left = jnp.concatenate([left[:, :columns], left[:, columns:]], axis=0)
 
-    def partials(start):
-        both = dot(left, heads_ref[teacher_width + start : teacher_width + start + quarter, :], ((1,), (1,)))
-        return both[:wide] + both[wide:]
-
     place = iota((wide, 1), 0) % 8
     has_label = stat_by_row(7) > 0.5
     scale_s = jnp.where(has_label, 0.0, 2.0 / stat_by_row(4))
@@ -182,21 +171,31 @@
     in_third = ((place == 4) | (place == 5)).astype(F32)
     scale_s = jnp.where(place >= 6, scale_s, 0.0)
     scale_t = jnp.where(place >= 6, scale_t, 0.0)
-    last = partials(3 * quarter)
-    correction = jnp.zeros((wide, quarter), F32)
-    for j in range(3):
-        exact = partials(j * quarter) + jnp.where(place >= 6, pltpu.roll(last, 6 - 2 * j, 0), 0.0)
-        sent = exact.astype(BF16).astype(F32)
-        residue = exact - sent
-        if j < 2:
-            correction += residue * (scale_s, scale_t)[j]
-        else:
-            sent += correction
-        scaled = residue * scale
-        sent += in_third * (pltpu.roll(scaled, 4, 0) + pltpu.roll(scaled, 2, 0))
-        for shard in range(shards):
-            out_ref[shard, :, j * quarter : (j + 1) * quarter] = sent[8 * shard : 8 * shard + 8].astype(BF16)
-        send_out(j, j * quarter, quarter)
+    chunks = quarter // LANES
+    first_unsent = 0
+    for chunk in range(chunks):
+        starts = [teacher_width + j * quarter + chunk * LANES for j in range(4)]
+        right = jnp.concatenate([heads_ref[start : start + LANES, :] for start in starts], axis=0)
+        both = dot(left, right, ((1,), (1,)))
+        exact = [both[:wide, j * LANES : (j + 1) * LANES] + both[wide:, j * LANES : (j + 1) * LANES] for j in range(4)]
+        correction = jnp.zeros((wide, LANES), F32)
+        for j in range(3):
+            whole = jnp.where(place >= 6, pltpu.roll(exact[3], 6 - 2 * j, 0), exact[j])
+            sent = whole.astype(BF16).astype(F32)
+            residue = whole - sent
+            if j < 2:
+                correction += residue * (scale_s, scale_t)[j]
+            else:
+                sent += correction
+            scaled = residue * scale
+            sent += in_third * (pltpu.roll(scaled, 4, 0) + pltpu.roll(scaled, 2, 0))
+            lanes = slice((3 * chunk + j) * LANES, (3 * chunk + j + 1) * LANES)
+            for shard in range(shards):
+                out_ref[shard, :, lanes] = sent[8 * shard : 8 * shard + 8].astype(BF16)
+        if chunk % 3 == 2 or chunk == chunks - 1:
+            end = 3 * (chunk + 1) * LANES
+            send_out(len(copies), first_unsent, end - first_unsent)
+            first_unsent = end
     for copy in copies:
         copy.wait()
 
@@ -254,9 +253,11 @@
         weight = jnp.where(
             place < 2, weight_s, jnp.where(place < 4, weight_t, jnp.where(place < 6, weight_l, weight_last))
         )
-        piece = jnp.zeros((8, quarter), F32)
-        for shard in range(shards):
-            piece += weight[shard] * arrived_ref[shard, :, j * quarter : (j + 1) * quarter].astype(F32)
+        piece = []
+        for chunk in range(quarter // LANES):
+            lanes = slice((3 * chunk + j) * LANES, (3 * chunk + j + 1) * LANES)
+            piece.append(sum(weight[shard] * arrived_ref[shard, :, lanes].astype(F32) for shard in range(shards)))
+        piece = jnp.concatenate(piece, axis=1)
         last += piece
         out_ref[:, j * quarter : (j + 1) * quarter] = piece[0:2] + piece[2:4] + piece[4:6]
     out_ref[:, 3 * quarter :] = last[6:8]
@@ -292,11 +293,11 @@
     payload, teacher_logits, student_logits, target = pl.pallas_call(
         raw_partial_kernel,
         out_shape=(jax.ShapeDtypeStruct((shards, 8, 3 * quarter + 128), BF16), square, square, square),
-        in_specs=[VMEM, VMEM, VMEM],
+        in_specs=[SMEM, VMEM, VMEM],
         out_specs=(ANY, VMEM, VMEM, VMEM),
-        scratch_shapes=[pltpu.VMEM((shards, 8, 3 * quarter + 128), BF16), pltpu.SemaphoreType.DMA((4,))],
+        scratch_shapes=[pltpu.VMEM((shards, 8, 3 * quarter + 128), BF16), pltpu.SemaphoreType.DMA((2 + quarter // LANES // 3,))],
         compiler_params=SMALL,
-    )(jnp.full((1, columns_here), here * columns_here, jnp.int32), rows, jnp.concatenate([teacher_head, student_head], axis=0))
+    )((here * columns_here)[None], rows, jnp.concatenate([teacher_head, student_head], axis=0))
     arrived = swap(payload)
     grad_rows = pl.pallas_call(
         logit_grad_kernel,

time: 38.6 us -> 38.4 us (level)
  no operation moved by 1% of the time
where the time goes in v15:
time: 38.4 us; the launch traced here: 38 us
  waiting for transfers between devices  17.9 us (47%)
  starting transfers between devices  11 us (29%)
  Pallas kernels  6.62 us (17%)
  other arithmetic  1.69 us (4%)
  between operations  0.7 us (2%)
    all_to_all x2, waiting for transfers between devices, swap(): lax.all_to_all(blocks, 'vocab', split_axis=0, concat_axis=0, tiled=True)  17.9 us
    all_to_all x2, starting transfers between devices, swap(): lax.all_to_all(blocks, 'vocab', split_axis=0, concat_axis=0, tiled=True)  10.9 us
    pallas_call x1, Pallas kernels, two_exchanges(): pl.pallas_call(raw_partial_kernel, out_shape=(jax.ShapeDtypeStruct((shard...  2.04 us
    concatenate x1, other arithmetic, two_exchanges(): jnp.concatenate([teacher_head, student_head], axis=0)  1.69 us
    pallas_call x1, Pallas kernels, two_exchanges(): pl.pallas_call(head_grad_kernel, out_shape=jax.ShapeDtypeStruct((width, c...  1.54 us
    pallas_call x1, Pallas kernels, gather_tokens(): pl.pallas_call(payload_kernel, out_shape=jax.ShapeDtypeStruct((shards, ow...  1.48 us
    pallas_call x1, Pallas kernels, two_exchanges(): pl.pallas_call(owner_kernel, out_shape=(jax.ShapeDtypeStruct((own, width)...  1.26 us
  transfers between devices with their start and end apart: 4, of which 2 were waited for; matrix products, arithmetic and copies ran while one was open for 4% of the time, Pallas kernels for 4%

profile of v15, /device:TPU:0, one launch (start us, length us, event | category | flops | bytes accessed | tf_op | source)
XLA Modules:
  0.0 38.0 jit_solution(12963816599222928717)
XLA Ops:
  0.6 1.5 %shard_map.76 = bf16[8,2,8320]{2,1,0:T(2,128)(2,1)} custom-call(s32[2]{0:T(128)} %labels_ref.1, bf16[2,4608]{1,0:T(2,128)(2,1)} %teacher_ref.1, bf16[2,3584]{1,0:T(2,128)(2,1)} %student_ref.1), custom_call_target="tpu_custom_call" | custom-call | tf_op jit(solution)/shard_map/pallas_call | solution.py:63
  2.1 7.3 %all-to-all-start = ((bf16[8,2,8320]{2,1,0:T(2,128)(2,1)}), bf16[8,2,8320]{2,1,0:T(2,128)(2,1)S(1)}, u32[]{:S(2)}, u32[]{:S(2)}) async-start(bf16[8,2,8320]{2,1,0:T(2,128)(2,1)} %shard_map.76), calls=%async_computation | async-start | bytes 532480 | tf_op jit(solution)/shard_map/all_to_all | solution.py:31
  9.4 1.7 %pad_maximum_fusion.heads_ref = bf16[8192,128]{1,0:T(8,128)(2,1)S(1)} fusion(bf16[3584,128]{1,0:T(8,128)(2,1)} %param.8, bf16[4608,128]{1,0:T(8,128)(2,1)} %param.7), kind=kLoop, calls=%fused_computation | loop fusion | flops 4194304 | bytes 4194304 | tf_op jit(solution)/shard_map/concatenate | solution.py:300
  11.1 7.3 %all-to-all-done = bf16[8,2,8320]{2,1,0:T(2,128)(2,1)S(1)} async-done(((bf16[8,2,8320]{2,1,0:T(2,128)(2,1)}), bf16[8,2,8320]{2,1,0:T(2,128)(2,1)S(1)}, u32[]{:S(2)}, u32[]{:S(2)}) %all-to-all-start) | async-done | bytes 266272 | tf_op jit(solution)/shard_map/all_to_all | solution.py:31
  18.4 0.1 reshape.9.rows_ref
  18.5 2.0 %shard_map.77 = (bf16[8,8,2816]{2,1,0:T(8,128)(2,1)}, f32[16,128]{1,0:T(8,128)S(1)}, f32[16,128]{1,0:T(8,128)S(1)}, f32[16,128]{1,0:T(8,128)S(1)}) custom-call(s32[1]{0:T(128)} %bitcast.first_ref, bf16[16,8320]{1,0:T(8,128)(2,1)S(1)} %reshape.9.rows_ref, bf16[8192,128]{1,0:T(8,128)(2,1)S(1)} %pad_maximum_fusion.heads_ref), custom_call_target="tpu_custom_call" | custom-call | tf_op jit(solution)/shard_map/pallas_call | solution.py:293
  20.5 3.6 %all-to-all-start.1 = ((bf16[8,8,2816]{2,1,0:T(8,128)(2,1)}), bf16[8,8,2816]{2,1,0:T(8,128)(2,1)S(1)}, u32[]{:S(2)}, u32[]{:S(2)}) async-start(bf16[8,8,2816]{2,1,0:T(8,128)(2,1)} %get-tuple-element.9), calls=%async_computation.1 | async-start | bytes 720896 | tf_op jit(solution)/shard_map/all_to_all | solution.py:31
  24.1 0.1 collective-permute-start
  24.2 10.6 %all-to-all-done.1.arrived_ref = bf16[8,8,2816]{2,1,0:T(8,128)(2,1)S(1)} async-done(((bf16[8,8,2816]{2,1,0:T(8,128)(2,1)}), bf16[8,8,2816]{2,1,0:T(8,128)(2,1)S(1)}, u32[]{:S(2)}, u32[]{:S(2)}) %all-to-all-start.1) | async-done | bytes 360480 | tf_op jit(solution)/shard_map/all_to_all | solution.py:31
  34.8 0.3 shard_map.79.grad_ref
  35.1 0.1 collective-permute-start.1
  35.2 1.3 %shard_map.78 = (f32[2,3584]{1,0:T(2,128)}, f32[2]{0:T(128)}) custom-call(bf16[8,8,2816]{2,1,0:T(8,128)(2,1)S(1)} %all-to-all-done.1.arrived_ref), custom_call_target="tpu_custom_call" | custom-call | tf_op jit(solution)/shard_map/pallas_call | solution.py:310
  36.4 0.0 collective-permute-done.hidden_other_ref
  36.5 0.0 collective-permute-done.1.other_ref
  36.5 1.5 %shard_map.80 = f32[3584,128]{1,0:T(8,128)} custom-call(bf16[16,3584]{1,0:T(8,128)(2,1)S(1)} %slice.8.hidden_ref, bf16[16,3584]{1,0:T(8,128)(2,1)S(1)} %collective-permute-done.hidden_other_ref, bf16[16,128]{1,0:T(8,128)(2,1)S(1)} %shard_map.79.grad_ref, bf16[16,128]{1,0:T(8,128)(2,1)S(1)} %collective-permute-done.1.other_ref), custom_call_target="tpu_custom_call" | custom-call | tf_op jit(solution)/shard_map/pallas_call | solution.py:317
  (2 shorter events, 0.0 us)
Async XLA Ops:
  2.1 16.3 %all-to-all-start = ((bf16[8,2,8320]{2,1,0:T(2,128)(2,1)}), bf16[8,2,8320]{2,1,0:T(2,128)(2,1)S(1)}, u32[]{:S(2)}, u32[]{:S(2)}) async-start(bf16[8,2,8320]{2,1,0:T(2,128)(2,1)} %shard_map.76), calls=%async_computation | async-start | bytes 532480 | tf_op jit(solution)/shard_map/all_to_all | solution.py:31
  20.5 14.3 %all-to-all-start.1 = ((bf16[8,8,2816]{2,1,0:T(8,128)(2,1)}), bf16[8,8,2816]{2,1,0:T(8,128)(2,1)S(1)}, u32[]{:S(2)}, u32[]{:S(2)}) async-start(bf16[8,8,2816]{2,1,0:T(8,128)(2,1)} %get-tuple-element.9), calls=%async_computation.1 | async-start | bytes 720896 | tf_op jit(solution)/shard_map/all_to_all | solution.py:31
  24.1 12.3 %collective-permute-start = (bf16[16,3584]{1,0:T(8,128)(2,1)S(1)}, bf16[16,3584]{1,0:T(8,128)(2,1)S(1)}, u32[]{:S(2)}, u32[]{:S(2)}) collective-permute-start(bf16[16,3584]{1,0:T(8,128)(2,1)S(1)} %slice.8.hidden_ref), channel_id=1, source_target_pairs={{0,1},{1,0},{2,3},{3,2},{4,5},{5,4},{6,7},{7,6},{8,9},{9,8},{10,11... | collective-permute-start | bytes 344072 | tf_op jit(solution)/shard_map/ppermute | solution.py:290
  35.1 1.4 %collective-permute-start.1 = (bf16[16,128]{1,0:T(8,128)(2,1)S(1)}, bf16[16,128]{1,0:T(8,128)(2,1)S(1)}, u32[]{:S(2)}, u32[]{:S(2)}) collective-permute-start(bf16[16,128]{1,0:T(8,128)(2,1)S(1)} %shard_map.79.grad_ref), channel_id=1, source_target_pairs={{0,1},{1,0},{2,3},{3,2},{4,5},{5,4},{6,7},{7,6},{8,9},{9,8},{10,11... | collective-permute-start | bytes 12296 | tf_op jit(solution)/shard_map/ppermute | solution.py:309

commit v16 on v15

--- a/solution.py
+++ b/solution.py
@@ -98,7 +98,7 @@
     code = rows_ref[:, teacher_width + width :].astype(F32)
     lane = iota(code.shape, 1)
     label = jnp.sum(jnp.where(lane == 0, code * 128.0, jnp.where(lane == 1, code, 0.0)), axis=1, keepdims=True)
-    target = (label.astype(jnp.int32) - first_ref[0] == iota((tokens, columns), 1)).astype(F32)
+    target = (label.astype(jnp.int32) == iota((tokens, columns), 1) + first_ref[...]).astype(F32)
     teacher_ref[...] = teacher
     student_ref[...] = student
     target_ref[...] = target
@@ -111,18 +111,21 @@
     exp_t = jnp.exp(teacher - top_t)
     exp_s = jnp.exp(student - top_s)
     mass_t, mass_s = total(exp_t), total(exp_s)
-    combined = exp_s * (2.0 / mass_s) - exp_t / mass_t
-    confidence = total(target * (exp_s * (2.0 / mass_s) + exp_t / mass_t))
-    kappa = (confidence > 0.75).astype(F32)
+    guess = jnp.abs(exp_s * (2.0 / mass_s) - exp_t / mass_t)
+    lane = iota((tokens, columns), 1)
+    largest = jnp.max(guess, axis=1, keepdims=True)
+    where_largest = jnp.min(jnp.where(guess == largest, lane, columns), axis=1, keepdims=True)
+    has_label = total(target)
+    chosen = jnp.where(has_label > 0.5, target, (lane == where_largest).astype(F32))
     stats = [
         top_t,
         mass_t,
         total(exp_t * (teacher - student)),
         top_s,
         mass_s,
-        total(target * student),
-        total(target * teacher),
-        2.0 * kappa + total(target),
+        total(chosen * student),
+        total(chosen * teacher),
+        has_label,
     ]
     lane = iota((tokens, 128), 1)
     table = jnp.zeros((tokens, 128), F32)
@@ -139,10 +142,6 @@
     of_token = (column == (row // 8) * 2 + row % 2).astype(F32).astype(BF16)
     by_row = dot(of_token, parts, ((1,), (0,)))
 
-    def stat_by_row(k):
-        picked = by_row[:, k : k + 1] + by_row[:, 8 + k : 9 + k] + by_row[:, 16 + k : 17 + k]
-        return picked
-
     lane = iota((8, 128), 1)
     shared = jnp.zeros((8, 128), F32)
     wide_parts = parts.astype(F32)
@@ -153,7 +152,7 @@
         out_ref[shard, :, 3 * quarter :] = block.astype(BF16)
     send_out(0, 3 * quarter, 128)
 
-    members = jnp.concatenate([exp_s, exp_t, kappa * combined * total(target) - target], axis=0)
+    members = jnp.concatenate([exp_s * (1.0 - chosen), exp_t * (1.0 - chosen), chosen], axis=0)
     member_high = members.astype(BF16)
     member_low = (members - member_high.astype(F32)).astype(BF16)
     row, column = iota((wide, 3 * tokens), 0), iota((wide, 3 * tokens), 1)
@@ -164,13 +163,6 @@
     left = jnp.concatenate([left[:, :columns], left[:, columns:]], axis=0)
 
     place = iota((wide, 1), 0) % 8
-    has_label = stat_by_row(7) > 0.5
-    scale_s = jnp.where(has_label, 0.0, 2.0 / stat_by_row(4))
-    scale_t = jnp.where(has_label, 0.0, -1.0 / stat_by_row(1))
-    scale = jnp.where(place < 2, scale_s, jnp.where(place < 4, scale_t, 0.0))
-    in_third = ((place == 4) | (place == 5)).astype(F32)
-    scale_s = jnp.where(place >= 6, scale_s, 0.0)
-    scale_t = jnp.where(place >= 6, scale_t, 0.0)
     chunks = quarter // LANES
     first_unsent = 0
     for chunk in range(chunks):
@@ -178,17 +170,8 @@
         right = jnp.concatenate([heads_ref[start : start + LANES, :] for start in starts], axis=0)
         both = dot(left, right, ((1,), (1,)))
         exact = [both[:wide, j * LANES : (j + 1) * LANES] + both[wide:, j * LANES : (j + 1) * LANES] for j in range(4)]
-        correction = jnp.zeros((wide, LANES), F32)
         for j in range(3):
-            whole = jnp.where(place >= 6, pltpu.roll(exact[3], 6 - 2 * j, 0), exact[j])
-            sent = whole.astype(BF16).astype(F32)
-            residue = whole - sent
-            if j < 2:
-                correction += residue * (scale_s, scale_t)[j]
-            else:
-                sent += correction
-            scaled = residue * scale
-            sent += in_third * (pltpu.roll(scaled, 4, 0) + pltpu.roll(scaled, 2, 0))
+            sent = jnp.where(place >= 6, pltpu.roll(exact[3], 6 - 2 * j, 0), exact[j])
             lanes = slice((3 * chunk + j) * LANES, (3 * chunk + j + 1) * LANES)
             for shard in range(shards):
                 out_ref[shard, :, lanes] = sent[8 * shard : 8 * shard + 8].astype(BF16)
@@ -232,21 +215,16 @@
     quarter = (lanes - 128) // 3
     stats, top_t, factor_t, mass_t, top_s, factor_s, mass_s = fold(sum_parts(arrived_ref[:, :, 3 * quarter :]), 0)
     cross = jnp.sum(stats[2] * factor_t, axis=0)
-    picked = jnp.sum(stats[5], axis=0)
-    picked_t = jnp.sum(stats[6], axis=0)
+    picked = jnp.sum(stats[7] * stats[5], axis=0)
     loss = cross / mass_t - top_t - jnp.log(mass_t) + 2.0 * (top_s + jnp.log(mass_s)) - picked
     token = lax.broadcasted_iota(jnp.int32, (8, 1), 0)
     for t in range(out_ref.shape[0]):
         loss_ref[t] = jnp.sum(jnp.where(token == t, loss, 0.0))
-    label_grad = 2.0 * (jnp.exp(picked - top_s) / mass_s) - jnp.exp(picked_t - top_t) / mass_t - 1.0
-    rounding = label_grad.astype(BF16).astype(F32) - label_grad
-    weight_s = factor_s / mass_s
-    weight_t = factor_t / mass_t
-    share = 0.8 * weight_s * stats[4] + 0.2 * weight_t * stats[1]
-    kappa = jnp.where(stats[7] > 2.0, 1.0, 0.0)
-    weight_l = jnp.where(stats[7] > 0.5, 1.0 - (1.0 - kappa) * rounding, share)
-    weight_s = 2.0 * (weight_s - kappa / stats[4])
-    weight_t = kappa / stats[1] - weight_t
+    chosen_s = jnp.exp(stats[5] - top_s) / mass_s
+    chosen_t = jnp.exp(stats[6] - top_t) / mass_t
+    weight_l = (2.0 * chosen_s - chosen_t - stats[7]).astype(BF16).astype(F32)
+    weight_s = 2.0 * (factor_s / mass_s)
+    weight_t = -(factor_t / mass_t)
     place = lax.broadcasted_iota(jnp.int32, (shards, 8, 1), 1)
     last = jnp.zeros((8, quarter), F32)
     for j, weight_last in enumerate((weight_s, weight_t, weight_l)):
@@ -289,15 +267,17 @@
     other = [(0, 1), (1, 0)]
     student_other = lax.ppermute(student_rows, "rows", other)
 
+    first_column = jnp.full((1, columns_here), here * columns_here, jnp.int32)
+    heads = jnp.concatenate([teacher_head, student_head], axis=0)
     square = jax.ShapeDtypeStruct((tokens, columns_here), F32)
     payload, teacher_logits, student_logits, target = pl.pallas_call(
         raw_partial_kernel,
         out_shape=(jax.ShapeDtypeStruct((shards, 8, 3 * quarter + 128), BF16), square, square, square),
-        in_specs=[SMEM, VMEM, VMEM],
+        in_specs=[VMEM, VMEM, VMEM],
         out_specs=(ANY, VMEM, VMEM, VMEM),
         scratch_shapes=[pltpu.VMEM((shards, 8, 3 * quarter + 128), BF16), pltpu.SemaphoreType.DMA((2 + quarter // LANES // 3,))],
         compiler_params=SMALL,
-    )((here * columns_here)[None], rows, jnp.concatenate([teacher_head, student_head], axis=0))
+    )(first_column, rows, heads)
     arrived = swap(payload)
     grad_rows = pl.pallas_call(
         logit_grad_kernel,

time: 38.4 us -> 38.4 us (level)
  no operation moved by 1% of the time
where the time goes in v16:
time: 38.4 us; the launch traced here: 37.9 us
  waiting for transfers between devices  17.9 us (47%)
  starting transfers between devices  11 us (29%)
  Pallas kernels  6.55 us (17%)
  other arithmetic  1.69 us (4%)
  between operations  0.71 us (2%)
    all_to_all x2, waiting for transfers between devices, swap(): lax.all_to_all(blocks, 'vocab', split_axis=0, concat_axis=0, tiled=True)  17.9 us
    all_to_all x2, starting transfers between devices, swap(): lax.all_to_all(blocks, 'vocab', split_axis=0, concat_axis=0, tiled=True)  10.9 us
    pallas_call x1, Pallas kernels, two_exchanges(): pl.pallas_call(raw_partial_kernel, out_shape=(jax.ShapeDtypeStruct((shard...  1.98 us
    concatenate x1, other arithmetic, two_exchanges(): heads = jnp.concatenate([teacher_head, student_head], axis=0)  1.69 us
    pallas_call x1, Pallas kernels, two_exchanges(): pl.pallas_call(head_grad_kernel, out_shape=jax.ShapeDtypeStruct((width, c...  1.54 us
    pallas_call x1, Pallas kernels, gather_tokens(): pl.pallas_call(payload_kernel, out_shape=jax.ShapeDtypeStruct((shards, ow...  1.48 us
    pallas_call x1, Pallas kernels, two_exchanges(): pl.pallas_call(owner_kernel, out_shape=(jax.ShapeDtypeStruct((own, width)...  1.24 us
  transfers between devices with their start and end apart: 4, of which 2 were waited for; matrix products, arithmetic and copies ran while one was open for 4% of the time, Pallas kernels for 4%

profile of v16, /device:TPU:0, one launch (start us, length us, event | category | flops | bytes accessed | tf_op | source)
XLA Modules:
  0.0 37.9 jit_solution(7779522231279447429)
XLA Ops:
  0.6 1.5 %shard_map.76 = bf16[8,2,8320]{2,1,0:T(2,128)(2,1)} custom-call(s32[2]{0:T(128)} %labels_ref.1, bf16[2,4608]{1,0:T(2,128)(2,1)} %teacher_ref.1, bf16[2,3584]{1,0:T(2,128)(2,1)} %student_ref.1), custom_call_target="tpu_custom_call" | custom-call | tf_op jit(solution)/shard_map/pallas_call | solution.py:63
  2.1 7.3 %all-to-all-start = ((bf16[8,2,8320]{2,1,0:T(2,128)(2,1)}), bf16[8,2,8320]{2,1,0:T(2,128)(2,1)S(1)}, u32[]{:S(2)}, u32[]{:S(2)}) async-start(bf16[8,2,8320]{2,1,0:T(2,128)(2,1)} %shard_map.76), calls=%async_computation | async-start | bytes 532480 | tf_op jit(solution)/shard_map/all_to_all | solution.py:31
  9.4 1.7 %pad_maximum_fusion.heads_ref = bf16[8192,128]{1,0:T(8,128)(2,1)S(1)} fusion(bf16[3584,128]{1,0:T(8,128)(2,1)} %param.8, bf16[4608,128]{1,0:T(8,128)(2,1)} %param.7), kind=kLoop, calls=%fused_computation | loop fusion | flops 4194304 | bytes 4194304 | tf_op jit(solution)/shard_map/concatenate | solution.py:271
  11.1 7.3 %all-to-all-done = bf16[8,2,8320]{2,1,0:T(2,128)(2,1)S(1)} async-done(((bf16[8,2,8320]{2,1,0:T(2,128)(2,1)}), bf16[8,2,8320]{2,1,0:T(2,128)(2,1)S(1)}, u32[]{:S(2)}, u32[]{:S(2)}) %all-to-all-start) | async-done | bytes 266272 | tf_op jit(solution)/shard_map/all_to_all | solution.py:31
  18.4 0.1 reshape.9.rows_ref
  18.5 2.0 %shard_map.77 = (bf16[8,8,2816]{2,1,0:T(8,128)(2,1)}, f32[16,128]{1,0:T(8,128)S(1)}, f32[16,128]{1,0:T(8,128)S(1)}, f32[16,128]{1,0:T(8,128)S(1)}) custom-call(s32[1,128]{1,0:T(1,128)S(1)} %broadcast_in_dim.3.first_ref, bf16[16,8320]{1,0:T(8,128)(2,1)S(1)} %reshape.9.rows_ref, bf16[8192,128]{1,0:T(8,128)(2,1)S(1)} %pad_maximum_fusion.heads_ref), custom_call_target="tpu_custom_call" | custom-call | tf_op jit(solution)/shard_map/pallas_call | solution.py:273
  20.5 3.6 %all-to-all-start.1 = ((bf16[8,8,2816]{2,1,0:T(8,128)(2,1)}), bf16[8,8,2816]{2,1,0:T(8,128)(2,1)S(1)}, u32[]{:S(2)}, u32[]{:S(2)}) async-start(bf16[8,8,2816]{2,1,0:T(8,128)(2,1)} %get-tuple-element.9), calls=%async_computation.1 | async-start | bytes 720896 | tf_op jit(solution)/shard_map/all_to_all | solution.py:31
  24.1 0.1 collective-permute-start
  24.2 10.6 %all-to-all-done.1.arrived_ref = bf16[8,8,2816]{2,1,0:T(8,128)(2,1)S(1)} async-done(((bf16[8,8,2816]{2,1,0:T(8,128)(2,1)}), bf16[8,8,2816]{2,1,0:T(8,128)(2,1)S(1)}, u32[]{:S(2)}, u32[]{:S(2)}) %all-to-all-start.1) | async-done | bytes 360480 | tf_op jit(solution)/shard_map/all_to_all | solution.py:31
  34.7 0.3 shard_map.79.grad_ref
  35.1 0.1 collective-permute-start.1
  35.1 1.2 %shard_map.78 = (f32[2,3584]{1,0:T(2,128)}, f32[2]{0:T(128)}) custom-call(bf16[8,8,2816]{2,1,0:T(8,128)(2,1)S(1)} %all-to-all-done.1.arrived_ref), custom_call_target="tpu_custom_call" | custom-call | tf_op jit(solution)/shard_map/pallas_call | solution.py:290
  36.4 0.0 collective-permute-done.hidden_other_ref
  36.4 0.0 collective-permute-done.1.other_ref
  36.4 1.5 %shard_map.80 = f32[3584,128]{1,0:T(8,128)} custom-call(bf16[16,3584]{1,0:T(8,128)(2,1)S(1)} %slice.8.hidden_ref, bf16[16,3584]{1,0:T(8,128)(2,1)S(1)} %collective-permute-done.hidden_other_ref, bf16[16,128]{1,0:T(8,128)(2,1)S(1)} %shard_map.79.grad_ref, bf16[16,128]{1,0:T(8,128)(2,1)S(1)} %collective-permute-done.1.other_ref), custom_call_target="tpu_custom_call" | custom-call | tf_op jit(solution)/shard_map/pallas_call | solution.py:297
  (3 shorter events, 0.0 us)
Async XLA Ops:
  2.1 16.3 %all-to-all-start = ((bf16[8,2,8320]{2,1,0:T(2,128)(2,1)}), bf16[8,2,8320]{2,1,0:T(2,128)(2,1)S(1)}, u32[]{:S(2)}, u32[]{:S(2)}) async-start(bf16[8,2,8320]{2,1,0:T(2,128)(2,1)} %shard_map.76), calls=%async_computation | async-start | bytes 532480 | tf_op jit(solution)/shard_map/all_to_all | solution.py:31
  20.5 14.3 %all-to-all-start.1 = ((bf16[8,8,2816]{2,1,0:T(8,128)(2,1)}), bf16[8,8,2816]{2,1,0:T(8,128)(2,1)S(1)}, u32[]{:S(2)}, u32[]{:S(2)}) async-start(bf16[8,8,2816]{2,1,0:T(8,128)(2,1)} %get-tuple-element.9), calls=%async_computation.1 | async-start | bytes 720896 | tf_op jit(solution)/shard_map/all_to_all | solution.py:31
  24.1 12.3 %collective-permute-start = (bf16[16,3584]{1,0:T(8,128)(2,1)S(1)}, bf16[16,3584]{1,0:T(8,128)(2,1)S(1)}, u32[]{:S(2)}, u32[]{:S(2)}) collective-permute-start(bf16[16,3584]{1,0:T(8,128)(2,1)S(1)} %slice.8.hidden_ref), channel_id=1, source_target_pairs={{0,1},{1,0},{2,3},{3,2},{4,5},{5,4},{6,7},{7,6},{8,9},{9,8},{10,11... | collective-permute-start | bytes 344072 | tf_op jit(solution)/shard_map/ppermute | solution.py:268
  35.1 1.3 %collective-permute-start.1 = (bf16[16,128]{1,0:T(8,128)(2,1)S(1)}, bf16[16,128]{1,0:T(8,128)(2,1)S(1)}, u32[]{:S(2)}, u32[]{:S(2)}) collective-permute-start(bf16[16,128]{1,0:T(8,128)(2,1)S(1)} %shard_map.79.grad_ref), channel_id=1, source_target_pairs={{0,1},{1,0},{2,3},{3,2},{4,5},{5,4},{6,7},{7,6},{8,9},{9,8},{10,11... | collective-permute-start | bytes 12296 | tf_op jit(solution)/shard_map/ppermute | solution.py:289

commit v17 on v16

--- a/solution.py
+++ b/solution.py
@@ -11,7 +11,7 @@
 
 
 UNROLL = 16
-LANES = 128
+LANES = 512
 PIECES = 7
 SMEM = pl.BlockSpec(memory_space=pltpu.SMEM)
 VMEM = pl.BlockSpec(memory_space=pltpu.VMEM)
@@ -76,8 +76,7 @@
     shards = out_ref.shape[0]
     wide = 8 * shards
     columns = heads_ref.shape[1]
-    quarter = (out_ref.shape[2] - 128) // 3
-    width = 4 * quarter
+    width = out_ref.shape[2] - 128
     teacher_width = heads_ref.shape[0] - width
 
     def iota(shape, dim):
@@ -113,10 +112,15 @@
     mass_t, mass_s = total(exp_t), total(exp_s)
     guess = jnp.abs(exp_s * (2.0 / mass_s) - exp_t / mass_t)
     lane = iota((tokens, columns), 1)
-    largest = jnp.max(guess, axis=1, keepdims=True)
-    where_largest = jnp.min(jnp.where(guess == largest, lane, columns), axis=1, keepdims=True)
+
+    def largest(values):
+        at_top = values == jnp.max(values, axis=1, keepdims=True)
+        return (lane == jnp.min(jnp.where(at_top, lane, columns), axis=1, keepdims=True)).astype(F32)
+
     has_label = total(target)
-    chosen = jnp.where(has_label > 0.5, target, (lane == where_largest).astype(F32))
+    chosen = jnp.where(has_label > 0.5, target, largest(guess))
+    second_chosen = largest(jnp.where(chosen > 0.5, -1.0, guess))
+    rest = 1.0 - chosen - second_chosen
     stats = [
         top_t,
         mass_t,
@@ -134,9 +138,15 @@
     first = table.astype(BF16).astype(F32)
     second = (table - first).astype(BF16).astype(F32)
     part = (lane % 32) // 8
-    parts = jnp.where(
-        part == 0, first, jnp.where(part == 1, second, jnp.where(part == 2, table - first - second, 0.0))
-    ).astype(BF16)
+    parts = jnp.where(part == 0, first, jnp.where(part == 1, second, table - first - second))
+    slot = lane % 32 - 24
+    for place, values in enumerate((student, teacher)):
+        value = total(second_chosen * values)
+        high = value.astype(BF16).astype(F32)
+        middle = (value - high).astype(BF16).astype(F32)
+        for k, piece in enumerate((high, middle, value - high - middle)):
+            parts = jnp.where(slot == 3 * place + k, piece, parts)
+    parts = jnp.where(slot >= 6, 0.0, parts).astype(BF16)
 
     row, column = iota((wide, tokens), 0), iota((wide, tokens), 1)
     of_token = (column == (row // 8) * 2 + row % 2).astype(F32).astype(BF16)
@@ -149,36 +159,25 @@
         shared = jnp.where(lane // 32 == group + 1, wide_parts[8 * group : 8 * group + 8], shared)
     for shard in range(shards):
         block = jnp.where(lane < 32, by_row[8 * shard : 8 * shard + 8], shared)
-        out_ref[shard, :, 3 * quarter :] = block.astype(BF16)
-    send_out(0, 3 * quarter, 128)
-
-    members = jnp.concatenate([exp_s * (1.0 - chosen), exp_t * (1.0 - chosen), chosen], axis=0)
+        out_ref[shard, :, width:] = block.astype(BF16)
+    send_out(0, width, 128)
+
+    members = jnp.concatenate([exp_s * rest, exp_t * rest, chosen, second_chosen], axis=0)
     member_high = members.astype(BF16)
     member_low = (members - member_high.astype(F32)).astype(BF16)
-    row, column = iota((wide, 3 * tokens), 0), iota((wide, 3 * tokens), 1)
-    place = row % 8
-    token = (row // 8) * 2 + row % 2
-    pick = ((place < 6) & (column == (place // 2) * tokens + token)).astype(F32).astype(BF16)
+    row, column = iota((wide, 4 * tokens), 0), iota((wide, 4 * tokens), 1)
+    of_member = column == ((row % 8) // 2) * tokens + (row // 8) * 2 + row % 2
+    pick = of_member.astype(F32).astype(BF16)
     left = dot(pick, jnp.concatenate([member_high, member_low], axis=1), ((1,), (0,))).astype(BF16)
     left = jnp.concatenate([left[:, :columns], left[:, columns:]], axis=0)
 
-    place = iota((wide, 1), 0) % 8
-    chunks = quarter // LANES
-    first_unsent = 0
-    for chunk in range(chunks):
-        starts = [teacher_width + j * quarter + chunk * LANES for j in range(4)]
-        right = jnp.concatenate([heads_ref[start : start + LANES, :] for start in starts], axis=0)
-        both = dot(left, right, ((1,), (1,)))
-        exact = [both[:wide, j * LANES : (j + 1) * LANES] + both[wide:, j * LANES : (j + 1) * LANES] for j in range(4)]
-        for j in range(3):
-            sent = jnp.where(place >= 6, pltpu.roll(exact[3], 6 - 2 * j, 0), exact[j])
-            lanes = slice((3 * chunk + j) * LANES, (3 * chunk + j + 1) * LANES)
-            for shard in range(shards):
-                out_ref[shard, :, lanes] = sent[8 * shard : 8 * shard + 8].astype(BF16)
-        if chunk % 3 == 2 or chunk == chunks - 1:
-            end = 3 * (chunk + 1) * LANES
-            send_out(len(copies), first_unsent, end - first_unsent)
-            first_unsent = end
+    for start in range(0, width, LANES):
+        head = heads_ref[teacher_width + start : teacher_width + start + LANES, :]
+        both = dot(left, head, ((1,), (1,)))
+        sent = both[:wide] + both[wide:]
+        for shard in range(shards):
+            out_ref[shard, :, start : start + LANES] = sent[8 * shard : 8 * shard + 8].astype(BF16)
+        send_out(1 + start // LANES, start, LANES)
     for copy in copies:
         copy.wait()
 
@@ -212,33 +211,33 @@
 
 def owner_kernel(arrived_ref, out_ref, loss_ref):
     shards, _, lanes = arrived_ref.shape
-    quarter = (lanes - 128) // 3
-    stats, top_t, factor_t, mass_t, top_s, factor_s, mass_s = fold(sum_parts(arrived_ref[:, :, 3 * quarter :]), 0)
+    width = lanes - 128
+    tail = arrived_ref[:, :, width:]
+    stats, top_t, factor_t, mass_t, top_s, factor_s, mass_s = fold(sum_parts(tail), 0)
+    extra = [tail[:, :, k : k + 1].astype(F32) for k in range(24, 30)]
     cross = jnp.sum(stats[2] * factor_t, axis=0)
     picked = jnp.sum(stats[7] * stats[5], axis=0)
     loss = cross / mass_t - top_t - jnp.log(mass_t) + 2.0 * (top_s + jnp.log(mass_s)) - picked
     token = lax.broadcasted_iota(jnp.int32, (8, 1), 0)
     for t in range(out_ref.shape[0]):
         loss_ref[t] = jnp.sum(jnp.where(token == t, loss, 0.0))
-    chosen_s = jnp.exp(stats[5] - top_s) / mass_s
-    chosen_t = jnp.exp(stats[6] - top_t) / mass_t
-    weight_l = (2.0 * chosen_s - chosen_t - stats[7]).astype(BF16).astype(F32)
-    weight_s = 2.0 * (factor_s / mass_s)
-    weight_t = -(factor_t / mass_t)
+    def entry(student, teacher, label):
+        prob_s = jnp.exp(student - top_s) / mass_s
+        prob_t = jnp.exp(teacher - top_t) / mass_t
+        return (2.0 * prob_s - prob_t - label).astype(BF16).astype(F32)
+
+    chosen = entry(stats[5], stats[6], stats[7])
+    second_chosen = entry(extra[0] + extra[1] + extra[2], extra[3] + extra[4] + extra[5], 0.0)
     place = lax.broadcasted_iota(jnp.int32, (shards, 8, 1), 1)
-    last = jnp.zeros((8, quarter), F32)
-    for j, weight_last in enumerate((weight_s, weight_t, weight_l)):
-        weight = jnp.where(
-            place < 2, weight_s, jnp.where(place < 4, weight_t, jnp.where(place < 6, weight_l, weight_last))
-        )
-        piece = []
-        for chunk in range(quarter // LANES):
-            lanes = slice((3 * chunk + j) * LANES, (3 * chunk + j + 1) * LANES)
-            piece.append(sum(weight[shard] * arrived_ref[shard, :, lanes].astype(F32) for shard in range(shards)))
-        piece = jnp.concatenate(piece, axis=1)
-        last += piece
-        out_ref[:, j * quarter : (j + 1) * quarter] = piece[0:2] + piece[2:4] + piece[4:6]
-    out_ref[:, 3 * quarter :] = last[6:8]
+    weight = jnp.where(
+        place < 2,
+        2.0 * (factor_s / mass_s),
+        jnp.where(place < 4, -(factor_t / mass_t), jnp.where(place < 6, chosen, second_chosen)),
+    )
+    for start in range(0, width, LANES):
+        lanes = slice(start, start + LANES)
+        piece = sum(weight[shard] * arrived_ref[shard, :, lanes].astype(F32) for shard in range(shards))
+        out_ref[:, lanes] = piece[0:2] + piece[2:4] + piece[4:6] + piece[6:8]
 
 
 def head_grad_kernel(hidden_ref, hidden_other_ref, grad_ref, other_ref, out_ref, total_ref, sems):
@@ -260,7 +259,6 @@
     teacher_width, width = teacher_hidden.shape[1], student_hidden.shape[1]
     columns_here = student_head.shape[1]
     tokens = shards * own
-    quarter = width // 4
     here = lax.axis_index("vocab").astype(jnp.int32)
     rows = gather_tokens(teacher_hidden, student_hidden, labels, shards).reshape(tokens, -1)
     student_rows = rows[:, teacher_width : teacher_width + width]
@@ -272,10 +270,10 @@
     square = jax.ShapeDtypeStruct((tokens, columns_here), F32)
     payload, teacher_logits, student_logits, target = pl.pallas_call(
         raw_partial_kernel,
-        out_shape=(jax.ShapeDtypeStruct((shards, 8, 3 * quarter + 128), BF16), square, square, square),
+        out_shape=(jax.ShapeDtypeStruct((shards, 8, width + 128), BF16), square, square, square),
         in_specs=[VMEM, VMEM, VMEM],
         out_specs=(ANY, VMEM, VMEM, VMEM),
-        scratch_shapes=[pltpu.VMEM((shards, 8, 3 * quarter + 128), BF16), pltpu.SemaphoreType.DMA((2 + quarter // LANES // 3,))],
+        scratch_shapes=[pltpu.VMEM((shards, 8, width + 128), BF16), pltpu.SemaphoreType.DMA((1 + width // LANES,))],
         compiler_params=SMALL,
     )(first_column, rows, heads)
     arrived = swap(payload)
@@ -285,7 +283,7 @@
         in_specs=[VMEM] * 4,
         out_specs=VMEM,
         compiler_params=SMALL,
-    )(arrived[:, :, 3 * quarter :], teacher_logits, student_logits, target)
+    )(arrived[:, :, width:], teacher_logits, student_logits, target)
     grad_other = lax.ppermute(grad_rows, "rows", other)
     hidden_grad, token_loss = pl.pallas_call(
         owner_kernel,

time: 38.4 us -> 41.2 us (1.073)
  waiting for transfers between devices: 17.9 us -> 20.3 us
    all_to_all x2, waiting for transfers between devices: 17.9 us -> 20.3 us  [swap(): lax.all_to_all(blocks, 'vocab', split_axis=0, concat_axis=0, tiled=True)]
where the time goes in v17:
time: 41.2 us; the launch traced here: 40.7 us
  waiting for transfers between devices  20.3 us (49%)
  starting transfers between devices  11 us (27%)
  Pallas kernels  6.89 us (17%)
  other arithmetic  1.69 us (4%)
  between operations  0.71 us (2%)
    all_to_all x2, waiting for transfers between devices, swap(): lax.all_to_all(blocks, 'vocab', split_axis=0, concat_axis=0, tiled=True)  20.3 us
    all_to_all x2, starting transfers between devices, swap(): lax.all_to_all(blocks, 'vocab', split_axis=0, concat_axis=0, tiled=True)  10.9 us
    pallas_call x1, Pallas kernels, two_exchanges(): pl.pallas_call(raw_partial_kernel, out_shape=(jax.ShapeDtypeStruct((shard...  2.24 us
    concatenate x1, other arithmetic, two_exchanges(): heads = jnp.concatenate([teacher_head, student_head], axis=0)  1.69 us
    pallas_call x1, Pallas kernels, two_exchanges(): pl.pallas_call(head_grad_kernel, out_shape=jax.ShapeDtypeStruct((width, c...  1.54 us
    pallas_call x1, Pallas kernels, gather_tokens(): pl.pallas_call(payload_kernel, out_shape=jax.ShapeDtypeStruct((shards, ow...  1.48 us
    pallas_call x1, Pallas kernels, two_exchanges(): pl.pallas_call(owner_kernel, out_shape=(jax.ShapeDtypeStruct((own, width)...  1.33 us
  transfers between devices with their start and end apart: 4, of which 2 were waited for; matrix products, arithmetic and copies ran while one was open for 4% of the time, Pallas kernels for 4%

profile of v17, /device:TPU:0, one launch (start us, length us, event | category | flops | bytes accessed | tf_op | source)
XLA Modules:
  0.0 40.7 jit_solution(12971954066497355088)
XLA Ops:
  0.6 1.5 %shard_map.76 = bf16[8,2,8320]{2,1,0:T(2,128)(2,1)} custom-call(s32[2]{0:T(128)} %labels_ref.1, bf16[2,4608]{1,0:T(2,128)(2,1)} %teacher_ref.1, bf16[2,3584]{1,0:T(2,128)(2,1)} %student_ref.1), custom_call_target="tpu_custom_call" | custom-call | tf_op jit(solution)/shard_map/pallas_call | solution.py:63
  2.1 7.3 %all-to-all-start = ((bf16[8,2,8320]{2,1,0:T(2,128)(2,1)}), bf16[8,2,8320]{2,1,0:T(2,128)(2,1)S(1)}, u32[]{:S(2)}, u32[]{:S(2)}) async-start(bf16[8,2,8320]{2,1,0:T(2,128)(2,1)} %shard_map.76), calls=%async_computation | async-start | bytes 532480 | tf_op jit(solution)/shard_map/all_to_all | solution.py:31
  9.4 1.7 %pad_maximum_fusion.heads_ref = bf16[8192,128]{1,0:T(8,128)(2,1)S(1)} fusion(bf16[3584,128]{1,0:T(8,128)(2,1)} %param.8, bf16[4608,128]{1,0:T(8,128)(2,1)} %param.7), kind=kLoop, calls=%fused_computation | loop fusion | flops 4194304 | bytes 4194304 | tf_op jit(solution)/shard_map/concatenate | solution.py:269
  11.1 7.3 %all-to-all-done = bf16[8,2,8320]{2,1,0:T(2,128)(2,1)S(1)} async-done(((bf16[8,2,8320]{2,1,0:T(2,128)(2,1)}), bf16[8,2,8320]{2,1,0:T(2,128)(2,1)S(1)}, u32[]{:S(2)}, u32[]{:S(2)}) %all-to-all-start) | async-done | bytes 266272 | tf_op jit(solution)/shard_map/all_to_all | solution.py:31
  18.4 0.1 reshape.9.rows_ref
  18.5 2.2 %shard_map.77 = (bf16[8,8,3712]{2,1,0:T(8,128)(2,1)}, f32[16,128]{1,0:T(8,128)S(1)}, f32[16,128]{1,0:T(8,128)S(1)}, f32[16,128]{1,0:T(8,128)S(1)}) custom-call(s32[1,128]{1,0:T(1,128)S(1)} %broadcast_in_dim.3.first_ref, bf16[16,8320]{1,0:T(8,128)(2,1)S(1)} %reshape.9.rows_ref, bf16[8192,128]{1,0:T(8,128)(2,1)S(1)} %pad_maximum_fusion.heads_ref), custom_call_target="tpu_custom_call" | custom-call | tf_op jit(solution)/shard_map/pallas_call | solution.py:271
  20.7 3.6 %all-to-all-start.1 = ((bf16[8,8,3712]{2,1,0:T(8,128)(2,1)}), bf16[8,8,3712]{2,1,0:T(8,128)(2,1)S(1)}, u32[]{:S(2)}, u32[]{:S(2)}) async-start(bf16[8,8,3712]{2,1,0:T(8,128)(2,1)} %get-tuple-element.9), calls=%async_computation.1 | async-start | bytes 950272 | tf_op jit(solution)/shard_map/all_to_all | solution.py:31
  24.3 0.1 collective-permute-start
  24.4 13.0 %all-to-all-done.1.arrived_ref = bf16[8,8,3712]{2,1,0:T(8,128)(2,1)S(1)} async-done(((bf16[8,8,3712]{2,1,0:T(8,128)(2,1)}), bf16[8,8,3712]{2,1,0:T(8,128)(2,1)S(1)}, u32[]{:S(2)}, u32[]{:S(2)}) %all-to-all-start.1) | async-done | bytes 475168 | tf_op jit(solution)/shard_map/all_to_all | solution.py:31
  37.5 0.3 shard_map.79.grad_ref
  37.8 0.1 collective-permute-start.1
  37.8 1.3 %shard_map.78 = (f32[2,3584]{1,0:T(2,128)}, f32[2]{0:T(128)}) custom-call(bf16[8,8,3712]{2,1,0:T(8,128)(2,1)S(1)} %all-to-all-done.1.arrived_ref), custom_call_target="tpu_custom_call" | custom-call | tf_op jit(solution)/shard_map/pallas_call | solution.py:288
  39.2 0.0 collective-permute-done.hidden_other_ref
  39.2 0.0 collective-permute-done.1.other_ref
  39.2 1.5 %shard_map.80 = f32[3584,128]{1,0:T(8,128)} custom-call(bf16[16,3584]{1,0:T(8,128)(2,1)S(1)} %slice.8.hidden_ref, bf16[16,3584]{1,0:T(8,128)(2,1)S(1)} %collective-permute-done.hidden_other_ref, bf16[16,128]{1,0:T(8,128)(2,1)S(1)} %shard_map.79.grad_ref, bf16[16,128]{1,0:T(8,128)(2,1)S(1)} %collective-permute-done.1.other_ref), custom_call_target="tpu_custom_call" | custom-call | tf_op jit(solution)/shard_map/pallas_call | solution.py:295
  (3 shorter events, 0.0 us)
Async XLA Ops:
  2.1 16.3 %all-to-all-start = ((bf16[8,2,8320]{2,1,0:T(2,128)(2,1)}), bf16[8,2,8320]{2,1,0:T(2,128)(2,1)S(1)}, u32[]{:S(2)}, u32[]{:S(2)}) async-start(bf16[8,2,8320]{2,1,0:T(2,128)(2,1)} %shard_map.76), calls=%async_computation | async-start | bytes 532480 | tf_op jit(solution)/shard_map/all_to_all | solution.py:31
  20.7 16.7 %all-to-all-start.1 = ((bf16[8,8,3712]{2,1,0:T(8,128)(2,1)}), bf16[8,8,3712]{2,1,0:T(8,128)(2,1)S(1)}, u32[]{:S(2)}, u32[]{:S(2)}) async-start(bf16[8,8,3712]{2,1,0:T(8,128)(2,1)} %get-tuple-element.9), calls=%async_computation.1 | async-start | bytes 950272 | tf_op jit(solution)/shard_map/all_to_all | solution.py:31
  24.3 14.8 %collective-permute-start = (bf16[16,3584]{1,0:T(8,128)(2,1)S(1)}, bf16[16,3584]{1,0:T(8,128)(2,1)S(1)}, u32[]{:S(2)}, u32[]{:S(2)}) collective-permute-start(bf16[16,3584]{1,0:T(8,128)(2,1)S(1)} %slice.8.hidden_ref), channel_id=1, source_target_pairs={{0,1},{1,0},{2,3},{3,2},{4,5},{5,4},{6,7},{7,6},{8,9},{9,8},{10,11... | collective-permute-start | bytes 344072 | tf_op jit(solution)/shard_map/ppermute | solution.py:266
  37.8 1.4 %collective-permute-start.1 = (bf16[16,128]{1,0:T(8,128)(2,1)S(1)}, bf16[16,128]{1,0:T(8,128)(2,1)S(1)}, u32[]{:S(2)}, u32[]{:S(2)}) collective-permute-start(bf16[16,128]{1,0:T(8,128)(2,1)S(1)} %shard_map.79.grad_ref), channel_id=1, source_target_pairs={{0,1},{1,0},{2,3},{3,2},{4,5},{5,4},{6,7},{7,6},{8,9},{9,8},{10,11... | collective-permute-start | bytes 12296 | tf_op jit(solution)/shard_map/ppermute | solution.py:287

commit v18 on v16

--- a/solution.py
+++ b/solution.py
@@ -57,14 +57,30 @@
     return digits.astype(F32).astype(BF16)
 
 
+def payload_copy_kernel(labels_ref, teacher_ref, student_ref, out_hbm, block_ref, sems):
+    shards, own, _ = out_hbm.shape
+    teacher_width, student_width = teacher_ref.shape[1], student_ref.shape[1]
+    block_ref[:, :teacher_width] = teacher_ref[...]
+    block_ref[:, teacher_width : teacher_width + student_width] = student_ref[...]
+    block_ref[:, teacher_width + student_width :] = label_digits(labels_ref, own)
+    copies = [pltpu.make_async_copy(block_ref, out_hbm.at[shard], sems.at[shard]) for shard in range(shards)]
+    for copy in copies:
+        copy.start()
+    for copy in copies:
+        copy.wait()
+
+
 def gather_tokens(teacher_hidden, student_hidden, labels, shards):
     own, teacher_width = teacher_hidden.shape
     student_width = student_hidden.shape[1]
+    width = teacher_width + student_width + CODE
+    few = shards <= UNROLL
     payload = pl.pallas_call(
-        payload_kernel,
-        out_shape=jax.ShapeDtypeStruct((shards, own, teacher_width + student_width + CODE), BF16),
+        payload_copy_kernel if few else payload_kernel,
+        out_shape=jax.ShapeDtypeStruct((shards, own, width), BF16),
         in_specs=[SMEM, VMEM, VMEM],
-        out_specs=VMEM,
+        out_specs=ANY if few else VMEM,
+        scratch_shapes=[pltpu.VMEM((own, width), BF16), pltpu.SemaphoreType.DMA((shards,))] if few else [],
     )(labels, teacher_hidden, student_hidden)
     return swap(payload)
 

time: 38.4 us -> 38.4 us (level)
  no operation moved by 1% of the time
where the time goes in v18:
time: 38.4 us; the launch traced here: 38 us
  waiting for transfers between devices  17.9 us (47%)
  starting transfers between devices  11 us (29%)
  Pallas kernels  6.57 us (17%)
  other arithmetic  1.69 us (4%)
  between operations  0.71 us (2%)
    all_to_all x2, waiting for transfers between devices, swap(): lax.all_to_all(blocks, 'vocab', split_axis=0, concat_axis=0, tiled=True)  17.9 us
    all_to_all x2, starting transfers between devices, swap(): lax.all_to_all(blocks, 'vocab', split_axis=0, concat_axis=0, tiled=True)  10.9 us
    pallas_call x1, Pallas kernels, two_exchanges(): pl.pallas_call(raw_partial_kernel, out_shape=(jax.ShapeDtypeStruct((shard...  1.98 us
    concatenate x1, other arithmetic, two_exchanges(): heads = jnp.concatenate([teacher_head, student_head], axis=0)  1.69 us
    pallas_call x1, Pallas kernels, two_exchanges(): pl.pallas_call(head_grad_kernel, out_shape=jax.ShapeDtypeStruct((width, c...  1.53 us
    pallas_call x1, Pallas kernels, gather_tokens(): pl.pallas_call(payload_copy_kernel if few else payload_kernel, out_shape=...  1.5 us
    pallas_call x1, Pallas kernels, two_exchanges(): pl.pallas_call(owner_kernel, out_shape=(jax.ShapeDtypeStruct((own, width)...  1.24 us
  transfers between devices with their start and end apart: 4, of which 2 were waited for; matrix products, arithmetic and copies ran while one was open for 4% of the time, Pallas kernels for 4%

profile of v18, /device:TPU:0, one launch (start us, length us, event | category | flops | bytes accessed | tf_op | source)
XLA Modules:
  0.0 38.0 jit_solution(6236308087979449135)
XLA Ops:
  0.6 1.5 %shard_map.76 = bf16[8,2,8320]{2,1,0:T(2,128)(2,1)} custom-call(s32[2]{0:T(128)} %labels_ref.1, bf16[2,4608]{1,0:T(2,128)(2,1)} %teacher_ref.1, bf16[2,3584]{1,0:T(2,128)(2,1)} %student_ref.1), custom_call_target="tpu_custom_call" | custom-call | tf_op jit(solution)/shard_map/pallas_call | solution.py:78
  2.1 7.3 %all-to-all-start = ((bf16[8,2,8320]{2,1,0:T(2,128)(2,1)}), bf16[8,2,8320]{2,1,0:T(2,128)(2,1)S(1)}, u32[]{:S(2)}, u32[]{:S(2)}) async-start(bf16[8,2,8320]{2,1,0:T(2,128)(2,1)} %shard_map.76), calls=%async_computation | async-start | bytes 532480 | tf_op jit(solution)/shard_map/all_to_all | solution.py:31
  9.4 1.7 %pad_maximum_fusion.heads_ref = bf16[8192,128]{1,0:T(8,128)(2,1)S(1)} fusion(bf16[3584,128]{1,0:T(8,128)(2,1)} %param.8, bf16[4608,128]{1,0:T(8,128)(2,1)} %param.7), kind=kLoop, calls=%fused_computation | loop fusion | flops 4194304 | bytes 4194304 | tf_op jit(solution)/shard_map/concatenate | solution.py:287
  11.1 7.3 %all-to-all-done = bf16[8,2,8320]{2,1,0:T(2,128)(2,1)S(1)} async-done(((bf16[8,2,8320]{2,1,0:T(2,128)(2,1)}), bf16[8,2,8320]{2,1,0:T(2,128)(2,1)S(1)}, u32[]{:S(2)}, u32[]{:S(2)}) %all-to-all-start) | async-done | bytes 266272 | tf_op jit(solution)/shard_map/all_to_all | solution.py:31
  18.4 0.1 reshape.9.rows_ref
  18.5 2.0 %shard_map.77 = (bf16[8,8,2816]{2,1,0:T(8,128)(2,1)}, f32[16,128]{1,0:T(8,128)S(1)}, f32[16,128]{1,0:T(8,128)S(1)}, f32[16,128]{1,0:T(8,128)S(1)}) custom-call(s32[1,128]{1,0:T(1,128)S(1)} %broadcast_in_dim.3.first_ref, bf16[16,8320]{1,0:T(8,128)(2,1)S(1)} %reshape.9.rows_ref, bf16[8192,128]{1,0:T(8,128)(2,1)S(1)} %pad_maximum_fusion.heads_ref), custom_call_target="tpu_custom_call" | custom-call | tf_op jit(solution)/shard_map/pallas_call | solution.py:289
  20.5 3.6 %all-to-all-start.1 = ((bf16[8,8,2816]{2,1,0:T(8,128)(2,1)}), bf16[8,8,2816]{2,1,0:T(8,128)(2,1)S(1)}, u32[]{:S(2)}, u32[]{:S(2)}) async-start(bf16[8,8,2816]{2,1,0:T(8,128)(2,1)} %get-tuple-element.9), calls=%async_computation.1 | async-start | bytes 720896 | tf_op jit(solution)/shard_map/all_to_all | solution.py:31
  24.1 0.1 collective-permute-start
  24.2 10.6 %all-to-all-done.1.arrived_ref = bf16[8,8,2816]{2,1,0:T(8,128)(2,1)S(1)} async-done(((bf16[8,8,2816]{2,1,0:T(8,128)(2,1)}), bf16[8,8,2816]{2,1,0:T(8,128)(2,1)S(1)}, u32[]{:S(2)}, u32[]{:S(2)}) %all-to-all-start.1) | async-done | bytes 360480 | tf_op jit(solution)/shard_map/all_to_all | solution.py:31
  34.8 0.3 shard_map.79.grad_ref
  35.1 0.1 collective-permute-start.1
  35.2 1.2 %shard_map.78 = (f32[2,3584]{1,0:T(2,128)}, f32[2]{0:T(128)}) custom-call(bf16[8,8,2816]{2,1,0:T(8,128)(2,1)S(1)} %all-to-all-done.1.arrived_ref), custom_call_target="tpu_custom_call" | custom-call | tf_op jit(solution)/shard_map/pallas_call | solution.py:306
  36.4 0.0 collective-permute-done.hidden_other_ref
  36.4 0.0 collective-permute-done.1.other_ref
  36.4 1.5 %shard_map.80 = f32[3584,128]{1,0:T(8,128)} custom-call(bf16[16,3584]{1,0:T(8,128)(2,1)S(1)} %slice.8.hidden_ref, bf16[16,3584]{1,0:T(8,128)(2,1)S(1)} %collective-permute-done.hidden_other_ref, bf16[16,128]{1,0:T(8,128)(2,1)S(1)} %shard_map.79.grad_ref, bf16[16,128]{1,0:T(8,128)(2,1)S(1)} %collective-permute-done.1.other_ref), custom_call_target="tpu_custom_call" | custom-call | tf_op jit(solution)/shard_map/pallas_call | solution.py:313
  (3 shorter events, 0.0 us)
Async XLA Ops:
  2.1 16.3 %all-to-all-start = ((bf16[8,2,8320]{2,1,0:T(2,128)(2,1)}), bf16[8,2,8320]{2,1,0:T(2,128)(2,1)S(1)}, u32[]{:S(2)}, u32[]{:S(2)}) async-start(bf16[8,2,8320]{2,1,0:T(2,128)(2,1)} %shard_map.76), calls=%async_computation | async-start | bytes 532480 | tf_op jit(solution)/shard_map/all_to_all | solution.py:31
  20.5 14.3 %all-to-all-start.1 = ((bf16[8,8,2816]{2,1,0:T(8,128)(2,1)}), bf16[8,8,2816]{2,1,0:T(8,128)(2,1)S(1)}, u32[]{:S(2)}, u32[]{:S(2)}) async-start(bf16[8,8,2816]{2,1,0:T(8,128)(2,1)} %get-tuple-element.9), calls=%async_computation.1 | async-start | bytes 720896 | tf_op jit(solution)/shard_map/all_to_all | solution.py:31
  24.1 12.3 %collective-permute-start = (bf16[16,3584]{1,0:T(8,128)(2,1)S(1)}, bf16[16,3584]{1,0:T(8,128)(2,1)S(1)}, u32[]{:S(2)}, u32[]{:S(2)}) collective-permute-start(bf16[16,3584]{1,0:T(8,128)(2,1)S(1)} %slice.8.hidden_ref), channel_id=1, source_target_pairs={{0,1},{1,0},{2,3},{3,2},{4,5},{5,4},{6,7},{7,6},{8,9},{9,8},{10,11... | collective-permute-start | bytes 344072 | tf_op jit(solution)/shard_map/ppermute | solution.py:284
  35.1 1.3 %collective-permute-start.1 = (bf16[16,128]{1,0:T(8,128)(2,1)S(1)}, bf16[16,128]{1,0:T(8,128)(2,1)S(1)}, u32[]{:S(2)}, u32[]{:S(2)}) collective-permute-start(bf16[16,128]{1,0:T(8,128)(2,1)S(1)} %shard_map.79.grad_ref), channel_id=1, source_target_pairs={{0,1},{1,0},{2,3},{3,2},{4,5},{5,4},{6,7},{7,6},{8,9},{9,8},{10,11... | collective-permute-start | bytes 12296 | tf_op jit(solution)/shard_map/ppermute | solution.py:305

commit v19 on v16

--- a/solution.py
+++ b/solution.py
@@ -72,8 +72,8 @@
 def raw_partial_kernel(
     first_ref, rows_ref, heads_ref, out_hbm, teacher_ref, student_ref, target_ref, out_ref, sems
 ):
-    tokens = rows_ref.shape[0]
-    shards = out_ref.shape[0]
+    shards, own, _ = rows_ref.shape
+    tokens = shards * own
     wide = 8 * shards
     columns = heads_ref.shape[1]
     quarter = (out_ref.shape[2] - 128) // 3
@@ -93,9 +93,12 @@
         copies.append(pltpu.make_async_copy(out_ref.at[:, :, lanes], out_hbm.at[:, :, lanes], sems.at[piece]))
         copies[-1].start()
 
-    student = dot(rows_ref[:, teacher_width : teacher_width + width], heads_ref[teacher_width:, :], ((1,), (0,)))
-    teacher = dot(rows_ref[:, :teacher_width], heads_ref[:teacher_width, :], ((1,), (0,)))
-    code = rows_ref[:, teacher_width + width :].astype(F32)
+    def rows_of(start, end):
+        return jnp.concatenate([rows_ref[shard, :, start:end] for shard in range(shards)], axis=0)
+
+    student = dot(rows_of(teacher_width, teacher_width + width), heads_ref[teacher_width:, :], ((1,), (0,)))
+    teacher = dot(rows_of(0, teacher_width), heads_ref[:teacher_width, :], ((1,), (0,)))
+    code = rows_of(teacher_width + width, teacher_width + width + CODE).astype(F32)
     lane = iota(code.shape, 1)
     label = jnp.sum(jnp.where(lane == 0, code * 128.0, jnp.where(lane == 1, code, 0.0)), axis=1, keepdims=True)
     target = (label.astype(jnp.int32) == iota((tokens, columns), 1) + first_ref[...]).astype(F32)
@@ -262,8 +265,8 @@
     tokens = shards * own
     quarter = width // 4
     here = lax.axis_index("vocab").astype(jnp.int32)
-    rows = gather_tokens(teacher_hidden, student_hidden, labels, shards).reshape(tokens, -1)
-    student_rows = rows[:, teacher_width : teacher_width + width]
+    rows = gather_tokens(teacher_hidden, student_hidden, labels, shards)
+    student_rows = rows[:, :, teacher_width : teacher_width + width].reshape(tokens, width)
     other = [(0, 1), (1, 0)]
     student_other = lax.ppermute(student_rows, "rows", other)
 

time: 38.4 us -> 38.3 us (level)
  transfers between devices with their start and end apart: 4 -> 4, of which waited for: 2 -> 2; matrix products, arithmetic and copies ran while one was open for 4% -> 5% of each run, Pallas kernels for 4% -> 4%
where the time goes in v19:
time: 38.3 us; the launch traced here: 37.8 us
  waiting for transfers between devices  17.8 us (46%)
  starting transfers between devices  11 us (29%)
  Pallas kernels  6.55 us (17%)
  other arithmetic  1.69 us (4%)
  between operations  0.7 us (2%)
    all_to_all x2, waiting for transfers between devices, swap(): lax.all_to_all(blocks, 'vocab', split_axis=0, concat_axis=0, tiled=True)  17.8 us
    all_to_all x2, starting transfers between devices, swap(): lax.all_to_all(blocks, 'vocab', split_axis=0, concat_axis=0, tiled=True)  10.8 us
    pallas_call x1, Pallas kernels, two_exchanges(): pl.pallas_call(raw_partial_kernel, out_shape=(jax.ShapeDtypeStruct((shard...  1.99 us
    concatenate x1, other arithmetic, two_exchanges(): heads = jnp.concatenate([teacher_head, student_head], axis=0)  1.69 us
    pallas_call x1, Pallas kernels, two_exchanges(): pl.pallas_call(head_grad_kernel, out_shape=jax.ShapeDtypeStruct((width, c...  1.54 us
    pallas_call x1, Pallas kernels, gather_tokens(): pl.pallas_call(payload_kernel, out_shape=jax.ShapeDtypeStruct((shards, ow...  1.48 us
    pallas_call x1, Pallas kernels, two_exchanges(): pl.pallas_call(owner_kernel, out_shape=(jax.ShapeDtypeStruct((own, width)...  1.24 us
  transfers between devices with their start and end apart: 4, of which 2 were waited for; matrix products, arithmetic and copies ran while one was open for 5% of the time, Pallas kernels for 4%

profile of v19, /device:TPU:0, one launch (start us, length us, event | category | flops | bytes accessed | tf_op | source)
XLA Modules:
  0.0 37.8 jit_solution(18118661055533259895)
XLA Ops:
  0.6 1.5 %shard_map.76 = bf16[8,2,8320]{2,1,0:T(2,128)(2,1)} custom-call(s32[2]{0:T(128)} %labels_ref.1, bf16[2,4608]{1,0:T(2,128)(2,1)} %teacher_ref.1, bf16[2,3584]{1,0:T(2,128)(2,1)} %student_ref.1), custom_call_target="tpu_custom_call" | custom-call | tf_op jit(solution)/shard_map/pallas_call | solution.py:63
  2.1 7.3 %all-to-all-start = ((bf16[8,2,8320]{2,1,0:T(2,128)(2,1)}), bf16[8,2,8320]{2,1,0:T(2,128)(2,1)S(1)}, u32[]{:S(2)}, u32[]{:S(2)}) async-start(bf16[8,2,8320]{2,1,0:T(2,128)(2,1)} %shard_map.76), calls=%async_computation | async-start | bytes 532480 | tf_op jit(solution)/shard_map/all_to_all | solution.py:31
  9.4 1.7 %pad_maximum_fusion.heads_ref = bf16[8192,128]{1,0:T(8,128)(2,1)S(1)} fusion(bf16[3584,128]{1,0:T(8,128)(2,1)} %param.8, bf16[4608,128]{1,0:T(8,128)(2,1)} %param.7), kind=kLoop, calls=%fused_computation | loop fusion | flops 4194304 | bytes 4194304 | tf_op jit(solution)/shard_map/concatenate | solution.py:274
  11.1 7.3 %all-to-all-done.rows_ref = bf16[8,2,8320]{2,1,0:T(2,128)(2,1)S(1)} async-done(((bf16[8,2,8320]{2,1,0:T(2,128)(2,1)}), bf16[8,2,8320]{2,1,0:T(2,128)(2,1)S(1)}, u32[]{:S(2)}, u32[]{:S(2)}) %all-to-all-start) | async-done | bytes 266272 | tf_op jit(solution)/shard_map/all_to_all | solution.py:31
  18.4 2.0 %shard_map.77 = (bf16[8,8,2816]{2,1,0:T(8,128)(2,1)}, f32[16,128]{1,0:T(8,128)S(1)}, f32[16,128]{1,0:T(8,128)S(1)}, f32[16,128]{1,0:T(8,128)S(1)}) custom-call(s32[1,128]{1,0:T(1,128)S(1)} %broadcast_in_dim.3.first_ref, bf16[8,2,8320]{2,1,0:T(2,128)(2,1)S(1)} %all-to-all-done.rows_ref, bf16[8192,128]{1,0:T(8,128)(2,1)S(1)} %pad_maximum_fusion.heads_ref), custom_call_target="tpu_custom_call" | custom-call | tf_op jit(solution)/shard_map/pallas_call | solution.py:276
  20.4 3.6 %all-to-all-start.1 = ((bf16[8,8,2816]{2,1,0:T(8,128)(2,1)}), bf16[8,8,2816]{2,1,0:T(8,128)(2,1)S(1)}, u32[]{:S(2)}, u32[]{:S(2)}) async-start(bf16[8,8,2816]{2,1,0:T(8,128)(2,1)} %get-tuple-element.9), calls=%async_computation.1 | async-start | bytes 720896 | tf_op jit(solution)/shard_map/all_to_all | solution.py:31
  24.0 0.1 slice.8
  24.1 0.1 collective-permute-start
  24.2 10.4 %all-to-all-done.1.arrived_ref = bf16[8,8,2816]{2,1,0:T(8,128)(2,1)S(1)} async-done(((bf16[8,8,2816]{2,1,0:T(8,128)(2,1)}), bf16[8,8,2816]{2,1,0:T(8,128)(2,1)S(1)}, u32[]{:S(2)}, u32[]{:S(2)}) %all-to-all-start.1) | async-done | bytes 360480 | tf_op jit(solution)/shard_map/all_to_all | solution.py:31
  34.6 0.3 shard_map.79.grad_ref
  34.9 0.1 collective-permute-start.1
  35.0 1.2 %shard_map.78 = (f32[2,3584]{1,0:T(2,128)}, f32[2]{0:T(128)}) custom-call(bf16[8,8,2816]{2,1,0:T(8,128)(2,1)S(1)} %all-to-all-done.1.arrived_ref), custom_call_target="tpu_custom_call" | custom-call | tf_op jit(solution)/shard_map/pallas_call | solution.py:293
  36.3 0.0 collective-permute-done.hidden_other_ref
  36.3 0.0 collective-permute-done.1.other_ref
  36.3 1.5 %shard_map.80 = f32[3584,128]{1,0:T(8,128)} custom-call(bf16[16,3584]{1,0:T(8,128)(2,1)S(1)} %reshape.9.hidden_ref, bf16[16,3584]{1,0:T(8,128)(2,1)S(1)} %collective-permute-done.hidden_other_ref, bf16[16,128]{1,0:T(8,128)(2,1)S(1)} %shard_map.79.grad_ref, bf16[16,128]{1,0:T(8,128)(2,1)S(1)} %collective-permute-done.1.other_ref), custom_call_target="tpu_custom_call" | custom-call | tf_op jit(solution)/shard_map/pallas_call | solution.py:300
  (3 shorter events, 0.1 us)
Async XLA Ops:
  2.1 16.3 %all-to-all-start = ((bf16[8,2,8320]{2,1,0:T(2,128)(2,1)}), bf16[8,2,8320]{2,1,0:T(2,128)(2,1)S(1)}, u32[]{:S(2)}, u32[]{:S(2)}) async-start(bf16[8,2,8320]{2,1,0:T(2,128)(2,1)} %shard_map.76), calls=%async_computation | async-start | bytes 532480 | tf_op jit(solution)/shard_map/all_to_all | solution.py:31
  20.4 14.3 %all-to-all-start.1 = ((bf16[8,8,2816]{2,1,0:T(8,128)(2,1)}), bf16[8,8,2816]{2,1,0:T(8,128)(2,1)S(1)}, u32[]{:S(2)}, u32[]{:S(2)}) async-start(bf16[8,8,2816]{2,1,0:T(8,128)(2,1)} %get-tuple-element.9), calls=%async_computation.1 | async-start | bytes 720896 | tf_op jit(solution)/shard_map/all_to_all | solution.py:31
  24.1 12.2 %collective-permute-start = (bf16[16,3584]{1,0:T(8,128)(2,1)S(1)}, bf16[16,3584]{1,0:T(8,128)(2,1)S(1)}, u32[]{:S(2)}, u32[]{:S(2)}) collective-permute-start(bf16[16,3584]{1,0:T(8,128)(2,1)S(1)} %reshape.9.hidden_ref), channel_id=1, source_target_pairs={{0,1},{1,0},{2,3},{3,2},{4,5},{5,4},{6,7},{7,6},{8,9},{9,8},{10,11... | collective-permute-start | bytes 344072 | tf_op jit(solution)/shard_map/ppermute | solution.py:271
  34.9 1.3 %collective-permute-start.1 = (bf16[16,128]{1,0:T(8,128)(2,1)S(1)}, bf16[16,128]{1,0:T(8,128)(2,1)S(1)}, u32[]{:S(2)}, u32[]{:S(2)}) collective-permute-start(bf16[16,128]{1,0:T(8,128)(2,1)S(1)} %shard_map.79.grad_ref), channel_id=1, source_target_pairs={{0,1},{1,0},{2,3},{3,2},{4,5},{5,4},{6,7},{7,6},{8,9},{9,8},{10,11... | collective-permute-start | bytes 12296 | tf_op jit(solution)/shard_map/ppermute | solution.py:292

commit v20 on v16

--- a/solution.py
+++ b/solution.py
@@ -69,8 +69,15 @@
     return swap(payload)
 
 
+def plain_payload_kernel(teacher_ref, student_ref, out_ref):
+    teacher_width = teacher_ref.shape[1]
+    for shard in range(out_ref.shape[0]):
+        out_ref[shard, :, :teacher_width] = teacher_ref[...]
+        out_ref[shard, :, teacher_width:] = student_ref[...]
+
+
 def raw_partial_kernel(
-    first_ref, rows_ref, heads_ref, out_hbm, teacher_ref, student_ref, target_ref, out_ref, sems
+    first_ref, label_ref, rows_ref, heads_ref, out_hbm, teacher_ref, student_ref, target_ref, out_ref, sems
 ):
     tokens = rows_ref.shape[0]
     shards = out_ref.shape[0]
@@ -95,10 +102,7 @@
 
     student = dot(rows_ref[:, teacher_width : teacher_width + width], heads_ref[teacher_width:, :], ((1,), (0,)))
     teacher = dot(rows_ref[:, :teacher_width], heads_ref[:teacher_width, :], ((1,), (0,)))
-    code = rows_ref[:, teacher_width + width :].astype(F32)
-    lane = iota(code.shape, 1)
-    label = jnp.sum(jnp.where(lane == 0, code * 128.0, jnp.where(lane == 1, code, 0.0)), axis=1, keepdims=True)
-    target = (label.astype(jnp.int32) == iota((tokens, columns), 1) + first_ref[...]).astype(F32)
+    target = (label_ref[...] == iota((tokens, columns), 1) + first_ref[...]).astype(F32)
     teacher_ref[...] = teacher
     student_ref[...] = student
     target_ref[...] = target
@@ -262,7 +266,15 @@
     tokens = shards * own
     quarter = width // 4
     here = lax.axis_index("vocab").astype(jnp.int32)
-    rows = gather_tokens(teacher_hidden, student_hidden, labels, shards).reshape(tokens, -1)
+    payload = pl.pallas_call(
+        plain_payload_kernel,
+        out_shape=jax.ShapeDtypeStruct((shards, own, teacher_width + width), BF16),
+        in_specs=[VMEM, VMEM],
+        out_specs=VMEM,
+    )(teacher_hidden, student_hidden)
+    payload, labels = lax.optimization_barrier((payload, labels))
+    rows = swap(payload).reshape(tokens, -1)
+    label_rows = lax.all_gather(labels, "vocab", axis=0, tiled=True)[:, None]
     student_rows = rows[:, teacher_width : teacher_width + width]
     other = [(0, 1), (1, 0)]
     student_other = lax.ppermute(student_rows, "rows", other)
@@ -273,11 +285,11 @@
     payload, teacher_logits, student_logits, target = pl.pallas_call(
         raw_partial_kernel,
         out_shape=(jax.ShapeDtypeStruct((shards, 8, 3 * quarter + 128), BF16), square, square, square),
-        in_specs=[VMEM, VMEM, VMEM],
+        in_specs=[VMEM] * 4,
         out_specs=(ANY, VMEM, VMEM, VMEM),
         scratch_shapes=[pltpu.VMEM((shards, 8, 3 * quarter + 128), BF16), pltpu.SemaphoreType.DMA((2 + quarter // LANES // 3,))],
         compiler_params=SMALL,
-    )(first_column, rows, heads)
+    )(first_column, label_rows, rows, heads)
     arrived = swap(payload)
     grad_rows = pl.pallas_call(
         logit_grad_kernel,

time: 38.4 us -> 43.9 us (1.14)
  blocking collectives: 0 us -> 11.9 us
  waiting for transfers between devices: 17.9 us -> 8.78 us
  local copies, waits for them, and re-layouts: 0.11 us -> 2.3 us
  between operations: 0.71 us -> 1.37 us
    unnamed x0 -> x1, blocking collectives: none -> 11.9 us
    all_to_all x2, waiting for transfers between devices: 17.9 us -> 8.78 us  [swap(): lax.all_to_all(blocks, 'vocab', split_axis=0, concat_axis=0, tiled=True)]
    unnamed x0 -> x3, local copies, waits for them, and re-layouts: none -> 2.1 us
  transfers between devices with their start and end apart: 4 -> 4, of which waited for: 2 -> 1; matrix products, arithmetic and copies ran while one was open for 4% -> 9% of each run, Pallas kernels for 4% -> 4%
where the time goes in v20:
time: 43.9 us; the launch traced here: 43.4 us
  blocking collectives  11.9 us (27%)
  starting transfers between devices  10.8 us (25%)
  waiting for transfers between devices  8.78 us (20%)
  Pallas kernels  6.51 us (15%)
  local copies, waits for them, and re-layouts  2.3 us (5%)
  other arithmetic  1.69 us (4%)
  between operations  1.37 us (3%)
    unnamed x1, blocking collectives  11.9 us
    all_to_all x2, starting transfers between devices, swap(): lax.all_to_all(blocks, 'vocab', split_axis=0, concat_axis=0, tiled=True)  10.7 us
    all_to_all x2, waiting for transfers between devices, swap(): lax.all_to_all(blocks, 'vocab', split_axis=0, concat_axis=0, tiled=True)  8.78 us
    unnamed x3, local copies, waits for them, and re-layouts  2.1 us
    pallas_call x1, Pallas kernels, two_exchanges(): pl.pallas_call(raw_partial_kernel, out_shape=(jax.ShapeDtypeStruct((shard...  1.97 us
    concatenate x1, other arithmetic, two_exchanges(): heads = jnp.concatenate([teacher_head, student_head], axis=0)  1.69 us
    pallas_call x1, Pallas kernels, two_exchanges(): pl.pallas_call(head_grad_kernel, out_shape=jax.ShapeDtypeStruct((width, c...  1.54 us
    pallas_call x1, Pallas kernels, two_exchanges(): pl.pallas_call(plain_payload_kernel, out_shape=jax.ShapeDtypeStruct((shar...  1.45 us
  transfers between devices with their start and end apart: 4, of which 1 were waited for; matrix products, arithmetic and copies ran while one was open for 9% of the time, Pallas kernels for 4%

profile of v20, /device:TPU:0, one launch (start us, length us, event | category | flops | bytes accessed | tf_op | source)
XLA Modules:
  0.0 43.4 jit_solution(1490824485464867999)
XLA Ops:
  0.6 1.5 %shard_map.76 = bf16[8,2,8192]{2,1,0:T(2,128)(2,1)} custom-call(bf16[2,4608]{1,0:T(2,128)(2,1)} %teacher_ref.1, bf16[2,3584]{1,0:T(2,128)(2,1)} %student_ref.1), custom_call_target="tpu_custom_call" | custom-call | tf_op jit(solution)/shard_map/pallas_call | solution.py:269
  2.1 7.3 %all-to-all-start = ((bf16[8,2,8192]{2,1,0:T(2,128)(2,1)}), bf16[8,2,8192]{2,1,0:T(2,128)(2,1)S(1)}, u32[]{:S(2)}, u32[]{:S(2)}) async-start(bf16[8,2,8192]{2,1,0:T(2,128)(2,1)} %shard_map.76), calls=%async_computation | async-start | bytes 524288 | tf_op jit(solution)/shard_map/all_to_all | solution.py:31
  9.3 1.2 %dynamic-slice = u32[1]{0:T(128)} dynamic-slice(u32[32]{0:T(128)} %constant.13, u32[]{:T(128)S(6)} %add), dynamic_slice_sizes={1} | dynamic-slice | bytes 12
  11.2 0.9 %dynamic-update-slice = s32[16]{0:T(128)S(1)} dynamic-update-slice(s32[16]{0:T(128)S(1)} %broadcast, s32[2]{0:T(128)} %param.9, u32[]{:T(128)} %bitcast) | dynamic-update-slice | bytes 20
  12.1 1.7 %pad_maximum_fusion.heads_ref = bf16[8192,128]{1,0:T(8,128)(2,1)S(1)} fusion(bf16[3584,128]{1,0:T(8,128)(2,1)} %param.8, bf16[4608,128]{1,0:T(8,128)(2,1)} %param.7), kind=kLoop, calls=%fused_computation | loop fusion | flops 4194304 | bytes 4194304 | tf_op jit(solution)/shard_map/concatenate | solution.py:283
  13.8 11.9 %all-reduce = s32[16]{0:T(128)S(1)} all-reduce(s32[16]{0:T(128)S(1)} %dynamic-update-slice), channel_id=1, replica_groups=mesh['groups'=2,'vocab'=8,'rows'=2] {'vocab'}, use_global_device_ids=true, to_apply=%add | all-reduce | flops 16 | bytes 128
  25.7 0.1 copy.8.label_ref
  25.8 0.0 all-to-all-done
  25.8 0.1 reshape.9.rows_ref
  25.9 2.0 %shard_map.77 = (bf16[8,8,2816]{2,1,0:T(8,128)(2,1)}, f32[16,128]{1,0:T(8,128)S(1)}, f32[16,128]{1,0:T(8,128)S(1)}, f32[16,128]{1,0:T(8,128)S(1)}) custom-call(s32[1,128]{1,0:T(1,128)S(1)} %broadcast_in_dim.6.first_ref, s32[16,1]{1,0:T(8,128)S(1)} %copy.8.label_ref, bf16[16,8192]{1,0:T(8,128)(2,1)S(1)} %reshape.9.rows_ref, ...), custom_call_target="tpu_custom_call" | custom-call | tf_op jit(solution)/shard_map/pallas_call | solution.py:285
  27.9 3.5 %all-to-all-start.1 = ((bf16[8,8,2816]{2,1,0:T(8,128)(2,1)}), bf16[8,8,2816]{2,1,0:T(8,128)(2,1)S(1)}, u32[]{:S(2)}, u32[]{:S(2)}) async-start(bf16[8,8,2816]{2,1,0:T(8,128)(2,1)} %get-tuple-element.13), calls=%async_computation.1 | async-start | bytes 720896 | tf_op jit(solution)/shard_map/all_to_all | solution.py:31
  31.3 0.1 collective-permute-start
  31.4 8.8 %all-to-all-done.1.arrived_ref = bf16[8,8,2816]{2,1,0:T(8,128)(2,1)S(1)} async-done(((bf16[8,8,2816]{2,1,0:T(8,128)(2,1)}), bf16[8,8,2816]{2,1,0:T(8,128)(2,1)S(1)}, u32[]{:S(2)}, u32[]{:S(2)}) %all-to-all-start.1) | async-done | bytes 360480 | tf_op jit(solution)/shard_map/all_to_all | solution.py:31
  40.2 0.3 shard_map.79.grad_ref
  40.5 0.1 collective-permute-start.1
  40.6 1.2 %shard_map.78 = (f32[2,3584]{1,0:T(2,128)}, f32[2]{0:T(128)}) custom-call(bf16[8,8,2816]{2,1,0:T(8,128)(2,1)S(1)} %all-to-all-done.1.arrived_ref), custom_call_target="tpu_custom_call" | custom-call | tf_op jit(solution)/shard_map/pallas_call | solution.py:302
  41.8 0.0 collective-permute-done.hidden_other_ref
  41.8 0.0 collective-permute-done.1.other_ref
  41.9 1.5 %shard_map.80 = f32[3584,128]{1,0:T(8,128)} custom-call(bf16[16,3584]{1,0:T(8,128)(2,1)S(1)} %slice.8.hidden_ref, bf16[16,3584]{1,0:T(8,128)(2,1)S(1)} %collective-permute-done.hidden_other_ref, bf16[16,128]{1,0:T(8,128)(2,1)S(1)} %shard_map.79.grad_ref, bf16[16,128]{1,0:T(8,128)(2,1)S(1)} %collective-permute-done.1.other_ref), custom_call_target="tpu_custom_call" | custom-call | tf_op jit(solution)/shard_map/pallas_call | solution.py:309
  (4 shorter events, 0.0 us)
Async XLA Ops:
  2.1 23.7 %all-to-all-start = ((bf16[8,2,8192]{2,1,0:T(2,128)(2,1)}), bf16[8,2,8192]{2,1,0:T(2,128)(2,1)S(1)}, u32[]{:S(2)}, u32[]{:S(2)}) async-start(bf16[8,2,8192]{2,1,0:T(2,128)(2,1)} %shard_map.76), calls=%async_computation | async-start | bytes 524288 | tf_op jit(solution)/shard_map/all_to_all | solution.py:31
  27.9 12.3 %all-to-all-start.1 = ((bf16[8,8,2816]{2,1,0:T(8,128)(2,1)}), bf16[8,8,2816]{2,1,0:T(8,128)(2,1)S(1)}, u32[]{:S(2)}, u32[]{:S(2)}) async-start(bf16[8,8,2816]{2,1,0:T(8,128)(2,1)} %get-tuple-element.13), calls=%async_computation.1 | async-start | bytes 720896 | tf_op jit(solution)/shard_map/all_to_all | solution.py:31
  31.3 10.5 %collective-permute-start = (bf16[16,3584]{1,0:T(8,128)(2,1)S(1)}, bf16[16,3584]{1,0:T(8,128)(2,1)S(1)}, u32[]{:S(2)}, u32[]{:S(2)}) collective-permute-start(bf16[16,3584]{1,0:T(8,128)(2,1)S(1)} %slice.8.hidden_ref), channel_id=1, source_target_pairs={{0,1},{1,0},{2,3},{3,2},{4,5},{5,4},{6,7},{7,6},{8,9},{9,8},{10,11... | collective-permute-start | bytes 344072 | tf_op jit(solution)/shard_map/ppermute | solution.py:280
  40.5 1.3 %collective-permute-start.1 = (bf16[16,128]{1,0:T(8,128)(2,1)S(1)}, bf16[16,128]{1,0:T(8,128)(2,1)S(1)}, u32[]{:S(2)}, u32[]{:S(2)}) collective-permute-start(bf16[16,128]{1,0:T(8,128)(2,1)S(1)} %shard_map.79.grad_ref), channel_id=1, source_target_pairs={{0,1},{1,0},{2,3},{3,2},{4,5},{5,4},{6,7},{7,6},{8,9},{9,8},{10,11... | collective-permute-start | bytes 12296 | tf_op jit(solution)/shard_map/ppermute | solution.py:301

commit v21 on v16

--- a/solution.py
+++ b/solution.py
@@ -12,7 +12,7 @@
 
 UNROLL = 16
 LANES = 128
-PIECES = 7
+PIECES = 14
 SMEM = pl.BlockSpec(memory_space=pltpu.SMEM)
 VMEM = pl.BlockSpec(memory_space=pltpu.VMEM)
 ANY = pl.BlockSpec(memory_space=pl.ANY)

time: 38.4 us -> 38.4 us (level)
  no operation moved by 1% of the time
where the time goes in v21:
time: 38.4 us; the launch traced here: 38 us
  waiting for transfers between devices  17.9 us (47%)
  starting transfers between devices  11 us (29%)
  Pallas kernels  6.6 us (17%)
  other arithmetic  1.69 us (4%)
  between operations  0.71 us (2%)
    all_to_all x2, waiting for transfers between devices, swap(): lax.all_to_all(blocks, 'vocab', split_axis=0, concat_axis=0, tiled=True)  17.9 us
    all_to_all x2, starting transfers between devices, swap(): lax.all_to_all(blocks, 'vocab', split_axis=0, concat_axis=0, tiled=True)  10.9 us
    pallas_call x1, Pallas kernels, two_exchanges(): pl.pallas_call(raw_partial_kernel, out_shape=(jax.ShapeDtypeStruct((shard...  1.98 us
    concatenate x1, other arithmetic, two_exchanges(): heads = jnp.concatenate([teacher_head, student_head], axis=0)  1.69 us
    pallas_call x1, Pallas kernels, two_exchanges(): pl.pallas_call(head_grad_kernel, out_shape=jax.ShapeDtypeStruct((width, c...  1.59 us
    pallas_call x1, Pallas kernels, gather_tokens(): pl.pallas_call(payload_kernel, out_shape=jax.ShapeDtypeStruct((shards, ow...  1.48 us
    pallas_call x1, Pallas kernels, two_exchanges(): pl.pallas_call(owner_kernel, out_shape=(jax.ShapeDtypeStruct((own, width)...  1.24 us
  transfers between devices with their start and end apart: 4, of which 2 were waited for; matrix products, arithmetic and copies ran while one was open for 4% of the time, Pallas kernels for 4%

profile of v21, /device:TPU:0, one launch (start us, length us, event | category | flops | bytes accessed | tf_op | source)
XLA Modules:
  0.0 38.0 jit_solution(8912448140445675878)
XLA Ops:
  0.6 1.5 %shard_map.76 = bf16[8,2,8320]{2,1,0:T(2,128)(2,1)} custom-call(s32[2]{0:T(128)} %labels_ref.1, bf16[2,4608]{1,0:T(2,128)(2,1)} %teacher_ref.1, bf16[2,3584]{1,0:T(2,128)(2,1)} %student_ref.1), custom_call_target="tpu_custom_call" | custom-call | tf_op jit(solution)/shard_map/pallas_call | solution.py:63
  2.1 7.3 %all-to-all-start = ((bf16[8,2,8320]{2,1,0:T(2,128)(2,1)}), bf16[8,2,8320]{2,1,0:T(2,128)(2,1)S(1)}, u32[]{:S(2)}, u32[]{:S(2)}) async-start(bf16[8,2,8320]{2,1,0:T(2,128)(2,1)} %shard_map.76), calls=%async_computation | async-start | bytes 532480 | tf_op jit(solution)/shard_map/all_to_all | solution.py:31
  9.4 1.7 %pad_maximum_fusion.heads_ref = bf16[8192,128]{1,0:T(8,128)(2,1)S(1)} fusion(bf16[3584,128]{1,0:T(8,128)(2,1)} %param.8, bf16[4608,128]{1,0:T(8,128)(2,1)} %param.7), kind=kLoop, calls=%fused_computation | loop fusion | flops 4194304 | bytes 4194304 | tf_op jit(solution)/shard_map/concatenate | solution.py:271
  11.1 7.3 %all-to-all-done = bf16[8,2,8320]{2,1,0:T(2,128)(2,1)S(1)} async-done(((bf16[8,2,8320]{2,1,0:T(2,128)(2,1)}), bf16[8,2,8320]{2,1,0:T(2,128)(2,1)S(1)}, u32[]{:S(2)}, u32[]{:S(2)}) %all-to-all-start) | async-done | bytes 266272 | tf_op jit(solution)/shard_map/all_to_all | solution.py:31
  18.4 0.1 reshape.9.rows_ref
  18.5 2.0 %shard_map.77 = (bf16[8,8,2816]{2,1,0:T(8,128)(2,1)}, f32[16,128]{1,0:T(8,128)S(1)}, f32[16,128]{1,0:T(8,128)S(1)}, f32[16,128]{1,0:T(8,128)S(1)}) custom-call(s32[1,128]{1,0:T(1,128)S(1)} %broadcast_in_dim.3.first_ref, bf16[16,8320]{1,0:T(8,128)(2,1)S(1)} %reshape.9.rows_ref, bf16[8192,128]{1,0:T(8,128)(2,1)S(1)} %pad_maximum_fusion.heads_ref), custom_call_target="tpu_custom_call" | custom-call | tf_op jit(solution)/shard_map/pallas_call | solution.py:273
  20.5 3.6 %all-to-all-start.1 = ((bf16[8,8,2816]{2,1,0:T(8,128)(2,1)}), bf16[8,8,2816]{2,1,0:T(8,128)(2,1)S(1)}, u32[]{:S(2)}, u32[]{:S(2)}) async-start(bf16[8,8,2816]{2,1,0:T(8,128)(2,1)} %get-tuple-element.9), calls=%async_computation.1 | async-start | bytes 720896 | tf_op jit(solution)/shard_map/all_to_all | solution.py:31
  24.1 0.1 collective-permute-start
  24.2 10.6 %all-to-all-done.1.arrived_ref = bf16[8,8,2816]{2,1,0:T(8,128)(2,1)S(1)} async-done(((bf16[8,8,2816]{2,1,0:T(8,128)(2,1)}), bf16[8,8,2816]{2,1,0:T(8,128)(2,1)S(1)}, u32[]{:S(2)}, u32[]{:S(2)}) %all-to-all-start.1) | async-done | bytes 360480 | tf_op jit(solution)/shard_map/all_to_all | solution.py:31
  34.7 0.3 shard_map.79.grad_ref
  35.1 0.1 collective-permute-start.1
  35.1 1.2 %shard_map.78 = (f32[2,3584]{1,0:T(2,128)}, f32[2]{0:T(128)}) custom-call(bf16[8,8,2816]{2,1,0:T(8,128)(2,1)S(1)} %all-to-all-done.1.arrived_ref), custom_call_target="tpu_custom_call" | custom-call | tf_op jit(solution)/shard_map/pallas_call | solution.py:290
  36.4 0.0 collective-permute-done.hidden_other_ref
  36.4 0.0 collective-permute-done.1.other_ref
  36.4 1.6 %shard_map.80 = f32[3584,128]{1,0:T(8,128)} custom-call(bf16[16,3584]{1,0:T(8,128)(2,1)S(1)} %slice.8.hidden_ref, bf16[16,3584]{1,0:T(8,128)(2,1)S(1)} %collective-permute-done.hidden_other_ref, bf16[16,128]{1,0:T(8,128)(2,1)S(1)} %shard_map.79.grad_ref, bf16[16,128]{1,0:T(8,128)(2,1)S(1)} %collective-permute-done.1.other_ref), custom_call_target="tpu_custom_call" | custom-call | tf_op jit(solution)/shard_map/pallas_call | solution.py:297
  (3 shorter events, 0.0 us)
Async XLA Ops:
  2.1 16.3 %all-to-all-start = ((bf16[8,2,8320]{2,1,0:T(2,128)(2,1)}), bf16[8,2,8320]{2,1,0:T(2,128)(2,1)S(1)}, u32[]{:S(2)}, u32[]{:S(2)}) async-start(bf16[8,2,8320]{2,1,0:T(2,128)(2,1)} %shard_map.76), calls=%async_computation | async-start | bytes 532480 | tf_op jit(solution)/shard_map/all_to_all | solution.py:31
  20.5 14.3 %all-to-all-start.1 = ((bf16[8,8,2816]{2,1,0:T(8,128)(2,1)}), bf16[8,8,2816]{2,1,0:T(8,128)(2,1)S(1)}, u32[]{:S(2)}, u32[]{:S(2)}) async-start(bf16[8,8,2816]{2,1,0:T(8,128)(2,1)} %get-tuple-element.9), calls=%async_computation.1 | async-start | bytes 720896 | tf_op jit(solution)/shard_map/all_to_all | solution.py:31
  24.1 12.3 %collective-permute-start = (bf16[16,3584]{1,0:T(8,128)(2,1)S(1)}, bf16[16,3584]{1,0:T(8,128)(2,1)S(1)}, u32[]{:S(2)}, u32[]{:S(2)}) collective-permute-start(bf16[16,3584]{1,0:T(8,128)(2,1)S(1)} %slice.8.hidden_ref), channel_id=1, source_target_pairs={{0,1},{1,0},{2,3},{3,2},{4,5},{5,4},{6,7},{7,6},{8,9},{9,8},{10,11... | collective-permute-start | bytes 344072 | tf_op jit(solution)/shard_map/ppermute | solution.py:268
  35.1 1.3 %collective-permute-start.1 = (bf16[16,128]{1,0:T(8,128)(2,1)S(1)}, bf16[16,128]{1,0:T(8,128)(2,1)S(1)}, u32[]{:S(2)}, u32[]{:S(2)}) collective-permute-start(bf16[16,128]{1,0:T(8,128)(2,1)S(1)} %shard_map.79.grad_ref), channel_id=1, source_target_pairs={{0,1},{1,0},{2,3},{3,2},{4,5},{5,4},{6,7},{7,6},{8,9},{9,8},{10,11... | collective-permute-start | bytes 12296 | tf_op jit(solution)/shard_map/ppermute | solution.py:289
